TPU v7x, 256 devices: a whole 4x4x8 slice. The times are simulated.
256 devices in a mesh: row: 32 (over x, y, core), col: 8 (over z).
Axes of the slice: x: 4, y: 4, z: 8, core: 2. Of those that a mesh axis runs over, the one named last changes fastest.
Arguments:
- activations: bfloat16 [512, 16384], P('row', 'col'), may hold values from -6 to 6
- output_gradient: bfloat16 [512, 16384], P('row', 'col'), may hold values from -6 to 6
- frozen_gate_weight: bfloat16 [16384, 26624], P('col', 'row'), may hold values from -0.046875 to 0.046875
- frozen_up_weight: bfloat16 [16384, 26624], P('col', 'row'), may hold values from -0.046875 to 0.046875
- frozen_down_weight: bfloat16 [26624, 16384], P('row', 'col'), may hold values from -0.0390625 to 0.0390625
- gate_adapter_first: bfloat16 [16384, 64], P('col'), may hold values from -0.046875 to 0.046875
- gate_adapter_second: bfloat16 [64, 26624], P(None, 'row'), may hold values from -0.75 to 0.75
- up_adapter_first: bfloat16 [16384, 64], P('col'), may hold values from -0.046875 to 0.046875
- up_adapter_second: bfloat16 [64, 26624], P(None, 'row'), may hold values from -0.75 to 0.75
- down_adapter_first: bfloat16 [26624, 64], P('row'), may hold values from -0.0390625 to 0.0390625
- down_leave: bfloat16 [64, 16384], P(None, 'col'), may hold values from -0.75 to 0.75
Outputs:
- activation_gradient: bfloat16 [512, 16384], P('row', 'col')
- gate_adapter_first_gradient: float32 [16384, 64], P(('col', 'row'))
- gate_adapter_second_gradient: float32 [64, 26624], P(None, 'row')
- up_adapter_first_gradient: float32 [16384, 64], P(('col', 'row'))
- up_adapter_second_gradient: float32 [64, 26624], P(None, 'row')
- down_adapter_first_gradient: float32 [26624, 64], P('row')
- down_adapter_second_gradient: float32 [64, 16384], P(None, ('col', 'row'))
All inputs are finite; a program needn't handle non-finite values.
Results may differ from a plain program's by a relative error of at most 0.028.
Values may be sent and summed in bfloat16 or wider, within the bound.
No kernel may reach another device: no remote copies, remote signals or barrier semaphores. Data moves between devices by JAX's collectives and lax.ppermute only.
A program may use at most 128 MiB of HBM per device.

v0:
```python
import math

import jax
import jax.numpy as jnp
from jax import lax
from jax.sharding import PartitionSpec as P

adapter_scale = 0.5


def matrix_multiply(left, right):
    return jnp.dot(left, right, preferred_element_type=jnp.float32)


def multiply_right_transposed(left, right):
    return lax.dot_general(
        left, right, (((1,), (1,)), ((), ())), preferred_element_type=jnp.float32
    )


def multiply_left_transposed(left, right):
    return lax.dot_general(
        left, right, (((0,), (0,)), ((), ())), preferred_element_type=jnp.float32
    )


def pointwise(gate_activation, up_activation, backward_result):
    sigmoid_gate = jax.nn.sigmoid(gate_activation)
    silu_gate = gate_activation * sigmoid_gate
    hidden_state = (silu_gate * up_activation).astype(jnp.bfloat16)
    up_gradient_term = (backward_result * silu_gate).astype(jnp.bfloat16)
    gate_gradient_term = (
        backward_result
        * up_activation
        * sigmoid_gate
        * (1.0 + gate_activation * (1.0 - sigmoid_gate))
    ).astype(jnp.bfloat16)
    return (hidden_state, gate_gradient_term, up_gradient_term)


def shifted(size, step):
    return [(i, (i + step) % size) for i in range(size)]


def two_way_rings(axis, operands, up_steps, arrive):
    size = lax.axis_size(axis)
    state = list(operands)
    for step in range(1, size // 2 + 1):
        for stream, steps in enumerate(up_steps):
            up, down = state[stream]
            if step <= steps:
                up = lax.ppermute(up, axis, shifted(size, 1))
            if step <= size - 1 - steps:
                down = lax.ppermute(down, axis, shifted(size, -1))
            state[stream] = arrive(stream, step, up, down)
    return state


def ring_sums(block_ofs, axis, up_steps, operands):
    size = lax.axis_size(axis)
    here = lax.axis_index(axis)

    def block(stream, offset):
        return block_ofs[stream](lax.rem(here + offset + size, size))

    def arrive(stream, step, up, down):
        ups = up_steps[stream]
        downs = size - 1 - ups
        if step < ups:
            up = (up.astype(jnp.float32) + block(stream, ups - step)).astype(jnp.bfloat16)
        if step < downs:
            down = (down.astype(jnp.float32) + block(stream, step - downs)).astype(jnp.bfloat16)
        return up, down

    return [
        up.astype(jnp.float32) + down.astype(jnp.float32) + block(stream, 0)
        for stream, (up, down) in enumerate(two_way_rings(axis, operands, up_steps, arrive))
    ]


def gather_tokens(activations, output_gradient):
    tokens, width = activations.shape
    row_count = lax.axis_size("row")
    side = math.isqrt(row_count // 2)
    here = lax.axis_index("row")
    core = lax.rem(here, 2)
    x = here // (2 * side)
    y = lax.rem(here // 2, side)
    first_at = jnp.where(core == 0, x, y)
    second_at = jnp.where(core == 0, y, x)

    def moves(first, second):
        pairs = []
        for source in range(row_count):
            sx, sy, sc = source // (2 * side), source // 2 % side, source % 2
            step_x, step_y = (first, second) if sc == 0 else (second, first)
            pairs.append(
                (source, (((sx + step_x) % side) * side + (sy + step_y) % side) * 2 + sc)
            )
        return pairs

    swap = [(source, source ^ 1) for source in range(row_count)]

    def to_other_core(value):
        return lax.ppermute(value, "row", swap)

    mine = jnp.where(core == 0, activations, output_gradient)
    given = to_other_core(jnp.where(core == 0, output_gradient, activations))
    pair = jnp.concatenate(
        [jnp.where(core == 0, mine, given), jnp.where(core == 0, given, mine)], axis=0
    )
    slab = jnp.zeros((side,) + pair.shape, pair.dtype)
    slab = lax.dynamic_update_index_in_dim(slab, pair, first_at, 0)
    for step in (1, -1, 2):
        got = lax.ppermute(pair, "row", moves(step, 0))
        slab = lax.dynamic_update_index_in_dim(
            slab, got, lax.rem(first_at - step + side, side), 0
        )
    slab = slab.reshape(side * 2 * tokens, width)
    half = slab.shape[0] // 2

    before = lax.ppermute(slab, "row", moves(0, 1))
    after = lax.ppermute(slab, "row", moves(0, -1))
    far = jnp.concatenate(
        [
            lax.ppermute(before[:half], "row", moves(0, 1)),
            lax.ppermute(after[half:], "row", moves(0, -1)),
        ],
        axis=0,
    )
    gathered = jnp.zeros((2, side) + slab.shape, slab.dtype)
    for offset, part in ((0, slab), (-1, before), (1, after), (2, far)):
        for which, value, at in (
            (core, part, second_at),
            (1 - core, to_other_core(part), first_at),
        ):
            gathered = lax.dynamic_update_slice(
                gathered, value[None, None], (which, lax.rem(at + offset + side, side), 0, 0)
            )
    shape = (side, side, 2 * tokens, width)
    return gathered[0].reshape(shape), gathered[1].reshape(shape)


def body(
    activations,
    output_gradient,
    frozen_gate_weight,
    frozen_up_weight,
    frozen_down_weight,
    gate_adapter_first,
    gate_adapter_second,
    up_adapter_first,
    up_adapter_second,
    down_adapter_first,
    down_leave,
):
    share_tokens, width = activations.shape
    rank, hidden_units = gate_adapter_second.shape
    row_count = lax.axis_size("row")
    col_count = lax.axis_size("col")
    tokens_all = share_tokens * row_count
    col_tokens = tokens_all // col_count
    chips = row_count // 2
    core = lax.rem(lax.axis_index("row"), 2)
    cut = (hidden_units - rank) // 2
    wide_size = hidden_units - cut
    swap = [(i, i ^ 1) for i in range(row_count)]
    same_core = [[2 * chip + c for chip in range(chips)] for c in range(2)]

    gathered_act, gathered_out = gather_tokens(activations, output_gradient)
    side = gathered_act.shape[0]
    pair_tokens = 2 * share_tokens
    pairs_per_col = col_tokens // pair_tokens
    blocks_per_line = side // pairs_per_col
    full_act = gathered_act.reshape(tokens_all, width)
    full_out = gathered_out.reshape(tokens_all, width)

    def blocks_of(first, size):
        def lines_block(partial, index):
            lines = partial.reshape(side, side, pair_tokens, -1)
            place = (lax.rem(index, blocks_per_line) * pairs_per_col, index // blocks_per_line)
            chosen = lax.dynamic_slice(
                lines, place + (0, first), (pairs_per_col, 1, pair_tokens, size)
            )
            return chosen.reshape(col_tokens, size)

        def block_of(index):
            return jnp.stack(
                [
                    lines_block(partials[0], index),
                    lines_block(partials[1], index),
                    lax.dynamic_slice(
                        partials[2], (index * col_tokens, first), (col_tokens, size)
                    ),
                ]
            )

        return block_of

    def first_operands(block_of, ups):
        here = lax.axis_index("col")
        return tuple(
            block_of(lax.rem(here + offset + col_count, col_count)).astype(jnp.bfloat16)
            for offset in (ups, ups + 1 - col_count)
        )

    def deltas_of(totals, low, columns):
        gate_activation = totals[0] + adapter_scale * matrix_multiply(
            low[0], gate_adapter_second[:, columns]
        )
        up_activation = totals[1] + adapter_scale * matrix_multiply(
            low[1], up_adapter_second[:, columns]
        )
        backward_result = totals[2] + adapter_scale * multiply_right_transposed(
            low[2], down_adapter_first[columns]
        )
        return pointwise(gate_activation, up_activation, backward_result)

    partials = lax.optimization_barrier(
        (
            multiply_right_transposed(
                full_act, jnp.concatenate([frozen_gate_weight, gate_adapter_first], axis=1).T
            ),
            multiply_right_transposed(
                full_act, jnp.concatenate([frozen_up_weight, up_adapter_first], axis=1).T
            ),
            multiply_right_transposed(
                full_out, jnp.concatenate([frozen_down_weight, down_leave], axis=0)
            ),
        )
    )
    later = slice(cut, hidden_units)
    earlier = slice(0, cut)
    up_steps = (col_count // 2, col_count - 1 - col_count // 2)
    block_ofs = (blocks_of(cut, wide_size + rank), blocks_of(0, cut))
    totals, second_totals = ring_sums(
        block_ofs,
        "col",
        up_steps,
        [first_operands(block_of, ups) for block_of, ups in zip(block_ofs, up_steps)],
    )
    low = totals[:, :, wide_size:].astype(jnp.bfloat16)
    later_deltas = deltas_of(totals[:, :, :wide_size], low, later)
    earlier_deltas = deltas_of(second_totals, low, earlier)

    own_factors = None
    for (hidden, gate_delta, up_delta), columns in (
        (later_deltas, later),
        (earlier_deltas, earlier),
    ):
        term = jnp.concatenate(
            [
                matrix_multiply(hidden, down_adapter_first[columns]),
                multiply_right_transposed(gate_delta, gate_adapter_second[:, columns]),
                multiply_right_transposed(up_delta, up_adapter_second[:, columns]),
            ],
            axis=1,
        )
        own_factors = term if own_factors is None else own_factors + term

    def to_all(value, axis):
        count = lax.axis_size(axis)
        return lax.all_to_all(
            jnp.broadcast_to(value[None], (count,) + value.shape), axis, 0, 0, tiled=True
        )

    packed = jnp.concatenate(
        [
            earlier_deltas[1],
            later_deltas[1],
            earlier_deltas[2],
            later_deltas[2],
            earlier_deltas[0],
            later_deltas[0],
            low[0],
            low[1],
            low[2],
        ],
        axis=1,
    )
    piece = lax.all_gather(packed, "col", axis=0, tiled=True)
    factor_parts = to_all(own_factors.astype(jnp.bfloat16), "row")
    own_factors = jnp.sum(factor_parts.astype(jnp.float32), axis=0).astype(jnp.bfloat16)
    factors = to_all(own_factors, "col").reshape(tokens_all, 3 * rank)
    gate_weight, up_weight = lax.optimization_barrier(
        (frozen_gate_weight, frozen_up_weight, packed)
    )[:2]
    input_weight = jnp.concatenate([gate_weight, up_weight], axis=1)
    piece, factors, input_weight = lax.optimization_barrier((piece, factors, input_weight))

    deltas = piece[:, : 2 * hidden_units].reshape(chips, 2, share_tokens, 2 * hidden_units)

    def input_part(which):
        chosen = lax.dynamic_index_in_dim(deltas, which, 1, keepdims=False)
        return multiply_right_transposed(
            chosen.reshape(chips * share_tokens, 2 * hidden_units), input_weight
        )

    other = lax.ppermute(input_part(1 - core).astype(jnp.bfloat16), "row", swap)
    share = (input_part(core) + other.astype(jnp.float32)).astype(jnp.bfloat16)
    shares = lax.all_to_all(share, "row", 0, 0, axis_index_groups=same_core, tiled=True)
    summed = jnp.sum(shares.reshape(chips, share_tokens, width).astype(jnp.float32), axis=0)

    first_token = lax.axis_index("row") * share_tokens
    row_factors = lax.dynamic_slice_in_dim(factors, first_token, share_tokens, 0)
    activation_gradient = (
        summed
        + adapter_scale
        * (
            multiply_right_transposed(row_factors[:, rank : 2 * rank], gate_adapter_first)
            + multiply_right_transposed(row_factors[:, 2 * rank :], up_adapter_first)
        )
    ).astype(jnp.bfloat16)

    features = width // row_count
    first_feature = lax.axis_index("row") * features
    activation_columns = lax.dynamic_slice_in_dim(full_act, first_feature, features, 1)
    activation_columns = activation_columns.reshape(side, side, pair_tokens, features)
    activation_columns = activation_columns.swapaxes(0, 1).reshape(tokens_all, features)
    output_columns = lax.dynamic_slice_in_dim(full_out, first_feature, features, 1)
    first_gradients = adapter_scale * multiply_left_transposed(
        activation_columns, factors[:, rank:]
    )
    gate_adapter_first_gradient = first_gradients[:, :rank]
    up_adapter_first_gradient = first_gradients[:, rank:]
    down_adapter_second_gradient = adapter_scale * multiply_left_transposed(
        factors[:, :rank], output_columns
    )

    piece_gate = piece[:, :hidden_units]
    piece_up = piece[:, hidden_units : 2 * hidden_units]
    piece_hidden = piece[:, 2 * hidden_units : 3 * hidden_units]
    lows = piece[:, 3 * hidden_units :]
    gate_low, up_low, down_low = [lows[:, i * rank : (i + 1) * rank] for i in range(3)]
    gate_adapter_second_gradient = adapter_scale * multiply_left_transposed(gate_low, piece_gate)
    up_adapter_second_gradient = adapter_scale * multiply_left_transposed(up_low, piece_up)
    down_adapter_first_gradient = adapter_scale * multiply_left_transposed(piece_hidden, down_low)
    return (
        activation_gradient,
        gate_adapter_first_gradient,
        gate_adapter_second_gradient,
        up_adapter_first_gradient,
        up_adapter_second_gradient,
        down_adapter_first_gradient,
        down_adapter_second_gradient,
    )


def solution(mesh):
    return jax.shard_map(
        body,
        mesh=mesh,
        in_specs=(
            P("row", "col"),
            P("row", "col"),
            P("col", "row"),
            P("col", "row"),
            P("row", "col"),
            P("col", None),
            P(None, "row"),
            P("col", None),
            P(None, "row"),
            P("row", None),
            P(None, "col"),
        ),
        out_specs=(
            P("row", "col"),
            P(("col", "row"), None),
            P(None, "row"),
            P(("col", "row"), None),
            P(None, "row"),
            P("row", None),
            P(None, ("col", "row")),
        ),
        check_vma=False,
    )
```

profile of v0, /device:TPU:1, one launch (start us, length us, event | category | flops | bytes accessed | tf_op | source)
XLA Modules:
  0.0 195.0 jit_solution(14104883954592811525)
XLA Ops:
  8.1 3.3 %collective-permute-start = (bf16[16,2048]{1,0:T(8,128)(2,1)S(1)}, bf16[16,2048]{1,0:T(8,128)(2,1)S(1)}, u32[]{:S(2)}, u32[]{:S(2)}) collective-permute-start(bf16[16,2048]{1,0:T(8,128)(2,1)S(1)} %broadcast_select_fusion.2), channel_id=1, source_target_pairs={{0,8},{8,0},{16,24},{24,16},{32,40},{40,32},{48,56},{56,48},{64,72... | collective-permute-start | bytes 196616 | tf_op jit(solution)/shard_map/ppermute | solution.py:105
  16.0 5.0 %collective-permute-done.1 = bf16[32,2048]{1,0:T(8,128)(2,1)S(1)} collective-permute-done((bf16[32,2048]{1,0:T(8,128)(2,1)S(1)}, bf16[32,2048]{1,0:T(8,128)(2,1)S(1)}, u32[]{:S(2)}, u32[]{:S(2)}) %collective-permute-start.1) | collective-permute-done | bytes 131104 | tf_op jit(solution)/shard_map/ppermute | solution.py:115
  26.0 3.8 %collective-permute-done.7 = bf16[128,2048]{1,0:T(8,128)(2,1)S(1)} collective-permute-done((bf16[128,2048]{1,0:T(8,128)(2,1)S(1)}, bf16[128,2048]{1,0:T(8,128)(2,1)S(1)}, u32[]{:S(2)}, u32[]{:S(2)}) %collective-permute-start.7) | collective-permute-done | bytes 524320 | tf_op jit(solution)/shard_map/ppermute | solution.py:123
  29.8 3.5 %collective-permute-start.10 = (bf16[64,2048]{1,0:T(8,128)(2,1)S(1)}, bf16[64,2048]{1,0:T(8,128)(2,1)S(1)}, u32[]{:S(2)}, u32[]{:S(2)}) collective-permute-start(bf16[64,2048]{1,0:T(8,128)(2,1)S(1)} %slice.154), channel_id=1, source_target_pairs={{0,48},{8,200},{16,0},{24,216},{32,16},{40,232},{48,32},{56,248},{... | collective-permute-start | bytes 786440 | tf_op jit(solution)/shard_map/ppermute | solution.py:127
  33.4 2.7 %collective-permute-start.8 = (bf16[128,2048]{1,0:T(8,128)(2,1)S(1)}, bf16[128,2048]{1,0:T(8,128)(2,1)S(1)}, u32[]{:S(2)}, u32[]{:S(2)}) collective-permute-start(bf16[128,2048]{1,0:T(8,128)(2,1)S(1)} %collective-permute-done.7), channel_id=1, source_target_pairs={{0,8},{8,0},{16,24},{24,16},{32,40},{40,32},{48,56},{56,48},{64,72... | collective-permute-start | bytes 1572872 | tf_op jit(solution)/shard_map/ppermute | solution.py:105
  36.3 3.5 %collective-permute-done.9 = bf16[64,2048]{1,0:T(8,128)(2,1)S(1)} collective-permute-done((bf16[64,2048]{1,0:T(8,128)(2,1)S(1)}, bf16[64,2048]{1,0:T(8,128)(2,1)S(1)}, u32[]{:S(2)}, u32[]{:S(2)}) %collective-permute-start.9) | collective-permute-done | bytes 262176 | tf_op jit(solution)/shard_map/ppermute | solution.py:126
  39.9 4.0 %collective-permute-start.11 = (bf16[128,2048]{1,0:T(8,128)(2,1)S(1)}, bf16[128,2048]{1,0:T(8,128)(2,1)S(1)}, u32[]{:S(2)}, u32[]{:S(2)}) collective-permute-start(bf16[128,2048]{1,0:T(8,128)(2,1)S(1)} %constant_dynamic-update-slice_fusion.1), channel_id=1, source_target_pairs={{0,8},{8,0},{16,24},{24,16},{32,40},{40,32},{48,56},{56,48},{64,72... | collective-permute-start | bytes 1572872 | tf_op jit(solution)/shard_map/ppermute | solution.py:105
  56.2 5.7 %collective-permute-start.15 = (bf16[3,64,384]{2,1,0:T(8,128)(2,1)S(1)}, bf16[3,64,384]{2,1,0:T(8,128)(2,1)S(1)}, u32[]{:S(2)}, u32[]{:S(2)}) collective-permute-start(bf16[3,64,384]{2,1,0:T(8,128)(2,1)S(1)} %pad_maximum_fusion.4), channel_id=1, source_target_pairs={{0,7},{1,0},{2,1},{3,2},{4,3},{5,4},{6,5},{7,6},{8,15},{9,8},{10,9... | collective-permute-start | bytes 442376 | tf_op jit(solution)/shard_map/ppermute | solution.py:54
  62.0 2.7 %collective-permute-start.23 = (bf16[3,64,512]{2,1,0:T(8,128)(2,1)S(1)}, bf16[3,64,512]{2,1,0:T(8,128)(2,1)S(1)}, u32[]{:S(2)}, u32[]{:S(2)}) collective-permute-start(bf16[3,64,512]{2,1,0:T(8,128)(2,1)S(1)} %pad_maximum_fusion.2), channel_id=1, source_target_pairs={{0,7},{1,0},{2,1},{3,2},{4,3},{5,4},{6,5},{7,6},{8,15},{9,8},{10,9... | collective-permute-start | bytes 589832 | tf_op jit(solution)/shard_map/ppermute | solution.py:54
  68.0 2.7 %collective-permute-start.16 = (bf16[3,64,384]{2,1,0:T(8,128)(2,1)S(1)}, bf16[3,64,384]{2,1,0:T(8,128)(2,1)S(1)}, u32[]{:S(2)}, u32[]{:S(2)}) collective-permute-start(bf16[3,64,384]{2,1,0:T(8,128)(2,1)S(1)} %fusion.25), channel_id=1, source_target_pairs={{0,7},{1,0},{2,1},{3,2},{4,3},{5,4},{6,5},{7,6},{8,15},{9,8},{10,9... | collective-permute-start | bytes 442376 | tf_op jit(solution)/shard_map/ppermute | solution.py:54
  72.1 2.7 %collective-permute-start.24 = (bf16[3,64,512]{2,1,0:T(8,128)(2,1)S(1)}, bf16[3,64,512]{2,1,0:T(8,128)(2,1)S(1)}, u32[]{:S(2)}, u32[]{:S(2)}) collective-permute-start(bf16[3,64,512]{2,1,0:T(8,128)(2,1)S(1)} %fusion.21), channel_id=1, source_target_pairs={{0,7},{1,0},{2,1},{3,2},{4,3},{5,4},{6,5},{7,6},{8,15},{9,8},{10,9... | collective-permute-start | bytes 589832 | tf_op jit(solution)/shard_map/ppermute | solution.py:54
  75.3 2.7 %collective-permute-start.17 = (bf16[3,64,384]{2,1,0:T(8,128)(2,1)S(1)}, bf16[3,64,384]{2,1,0:T(8,128)(2,1)S(1)}, u32[]{:S(2)}, u32[]{:S(2)}) collective-permute-start(bf16[3,64,384]{2,1,0:T(8,128)(2,1)S(1)} %fusion.26), channel_id=1, source_target_pairs={{0,7},{1,0},{2,1},{3,2},{4,3},{5,4},{6,5},{7,6},{8,15},{9,8},{10,9... | collective-permute-start | bytes 442376 | tf_op jit(solution)/shard_map/ppermute | solution.py:54
  78.4 2.7 %collective-permute-start.25 = (bf16[3,64,512]{2,1,0:T(8,128)(2,1)S(1)}, bf16[3,64,512]{2,1,0:T(8,128)(2,1)S(1)}, u32[]{:S(2)}, u32[]{:S(2)}) collective-permute-start(bf16[3,64,512]{2,1,0:T(8,128)(2,1)S(1)} %fusion.22), channel_id=1, source_target_pairs={{0,7},{1,0},{2,1},{3,2},{4,3},{5,4},{6,5},{7,6},{8,15},{9,8},{10,9... | collective-permute-start | bytes 589832 | tf_op jit(solution)/shard_map/ppermute | solution.py:54
  81.2 3.3 %collective-permute-start.18 = (bf16[3,64,384]{2,1,0:T(8,128)(2,1)S(1)}, bf16[3,64,384]{2,1,0:T(8,128)(2,1)S(1)}, u32[]{:S(2)}, u32[]{:S(2)}) collective-permute-start(bf16[3,64,384]{2,1,0:T(8,128)(2,1)S(1)} %fusion.27), channel_id=1, source_target_pairs={{0,7},{1,0},{2,1},{3,2},{4,3},{5,4},{6,5},{7,6},{8,15},{9,8},{10,9... | collective-permute-start | bytes 442376 | tf_op jit(solution)/shard_map/ppermute | solution.py:54
  87.6 4.8 %collective-permute-done.22 = bf16[3,64,512]{2,1,0:T(8,128)(2,1)S(1)} collective-permute-done((bf16[3,64,512]{2,1,0:T(8,128)(2,1)S(1)}, bf16[3,64,512]{2,1,0:T(8,128)(2,1)S(1)}, u32[]{:S(2)}, u32[]{:S(2)}) %collective-permute-start.22) | collective-permute-done | bytes 196640 | tf_op jit(solution)/shard_map/ppermute | solution.py:52
  97.0 9.0 %all-to-all-start = ((bf16[32,64,192]{2,1,0:T(8,128)(2,1)}), bf16[32,64,192]{2,1,0:T(8,128)(2,1)S(1)}, u32[]{:S(2)}, u32[]{:S(2)}) async-start(bf16[32,64,192]{2,1,0:T(8,128)(2,1)} %broadcast_in_dim.65), calls=%async_computation | async-start | bytes 2097152 | tf_op jit(solution)/shard_map/all_to_all | solution.py:263
  106.0 17.0 %all-to-all-done = bf16[32,64,192]{2,1,0:T(8,128)(2,1)S(1)} async-done(((bf16[32,64,192]{2,1,0:T(8,128)(2,1)}), bf16[32,64,192]{2,1,0:T(8,128)(2,1)S(1)}, u32[]{:S(2)}, u32[]{:S(2)}) %all-to-all-start) | async-done | bytes 786464 | tf_op jit(solution)/shard_map/all_to_all | solution.py:263
  123.9 3.4 %all-to-all-start.1 = ((bf16[8,64,192]{2,1,0:T(8,128)(2,1)}), bf16[8,64,192]{2,1,0:T(8,128)(2,1)S(1)}, u32[]{:S(2)}, u32[]{:S(2)}) async-start(bf16[8,64,192]{2,1,0:T(8,128)(2,1)} %broadcast_in_dim.66), calls=%async_computation.1 | async-start | bytes 524288 | tf_op jit(solution)/shard_map/all_to_all | solution.py:263
  127.3 7.1 %pad_maximum_fusion = bf16[2048,1664]{0,1:T(8,128)(2,1)} fusion(bf16[2048,832]{0,1:T(8,128)(2,1)} %param.14, bf16[2048,832]{0,1:T(8,128)(2,1)} %param.13), kind=kLoop, calls=%fused_computation | loop fusion | flops 13631488 | bytes 13631488 | tf_op jit(solution)/shard_map/concatenate | solution.py:288
  134.4 7.0 %all-to-all-done.1 = bf16[8,64,192]{2,1,0:T(8,128)(2,1)S(1)} async-done(((bf16[8,64,192]{2,1,0:T(8,128)(2,1)}), bf16[8,64,192]{2,1,0:T(8,128)(2,1)S(1)}, u32[]{:S(2)}, u32[]{:S(2)}) %all-to-all-start.1) | async-done | bytes 196640 | tf_op jit(solution)/shard_map/all_to_all | solution.py:263
  143.9 6.0 %convolution_convert_fusion = bf16[256,2048]{1,0:T(8,128)(2,1)} fusion(bf16[256,1664]{1,0:T(8,128)(2,1)S(1)} %bitcast.181, bf16[2048,1664]{0,1:T(8,128)(2,1)} %pad_maximum_fusion), kind=kOutput, calls=%fused_computation.13 | convolution fusion | flops 1745354752 | bytes 8716288 | tf_op jit(solution)/shard_map/dot_general | solution.py:16
  155.1 6.6 %add_convert_fusion = bf16[256,2048]{1,0:T(8,128)(2,1)} fusion(bf16[256,2048]{1,0:T(8,128)(2,1)} %copy-done.12, bf16[256,1664]{1,0:T(8,128)(2,1)} %bitcast.180, bf16[2048,1664]{0,1:T(8,128)(2,1)} %pad_maximum_fusion), kind=kOutput, calls=%fused_computation.19 | convolution fusion | flops 1746403328 | bytes 9764864 | tf_op jit(solution)/shard_map/dot_general | solution.py:16
  161.7 7.2 %all-to-all-start.2 = ((bf16[16,16,2048]{2,1,0:T(8,128)(2,1)}), bf16[16,16,2048]{2,1,0:T(8,128)(2,1)}, u32[]{:S(2)}, u32[]{:S(2)}) async-start(bf16[16,16,2048]{2,1,0:T(8,128)(2,1)} %bitcast.179), calls=%async_computation.2 | async-start | bytes 2097152 | tf_op jit(solution)/shard_map/all_to_all | solution.py:301
  172.9 13.0 %all-to-all-done.2 = bf16[16,16,2048]{2,1,0:T(8,128)(2,1)} async-done(((bf16[16,16,2048]{2,1,0:T(8,128)(2,1)}), bf16[16,16,2048]{2,1,0:T(8,128)(2,1)}, u32[]{:S(2)}, u32[]{:S(2)}) %all-to-all-start.2) | async-done | bytes 1048608 | tf_op jit(solution)/shard_map/all_to_all | solution.py:301
  (151 shorter events, 50.7 us)
Async XLA Ops:
  7.2 134.2 %all-gather.2.cloned.1.call-start = ((), (), s32[]{:S(2)}) async-start(), calls=%async_computation.3 | async-start | bytes 3096576 | tf_op jit(solution)/shard_map/all_gather | solution.py:281
  13.2 7.8 %collective-permute-start.2 = (bf16[32,2048]{1,0:T(8,128)(2,1)S(1)}, bf16[32,2048]{1,0:T(8,128)(2,1)S(1)}, u32[]{:S(2)}, u32[]{:S(2)}) collective-permute-start(bf16[32,2048]{1,0:T(8,128)(2,1)S(1)} %pad_maximum_fusion.5), channel_id=1, source_target_pairs={{0,192},{8,56},{16,208},{24,8},{32,224},{40,24},{48,240},{56,40},{... | collective-permute-start | bytes 393224 | tf_op jit(solution)/shard_map/ppermute | solution.py:115
  14.3 6.7 %collective-permute-start.1 = (bf16[32,2048]{1,0:T(8,128)(2,1)S(1)}, bf16[32,2048]{1,0:T(8,128)(2,1)S(1)}, u32[]{:S(2)}, u32[]{:S(2)}) collective-permute-start(bf16[32,2048]{1,0:T(8,128)(2,1)S(1)} %pad_maximum_fusion.5), channel_id=1, source_target_pairs={{0,64},{8,24},{16,80},{24,40},{32,96},{40,56},{48,112},{56,8},{64,... | collective-permute-start | bytes 393224 | tf_op jit(solution)/shard_map/ppermute | solution.py:115
  14.7 6.3 %collective-permute-start.3 = (bf16[32,2048]{1,0:T(8,128)(2,1)S(1)}, bf16[32,2048]{1,0:T(8,128)(2,1)S(1)}, u32[]{:S(2)}, u32[]{:S(2)}) collective-permute-start(bf16[32,2048]{1,0:T(8,128)(2,1)S(1)} %pad_maximum_fusion.5), channel_id=1, source_target_pairs={{0,128},{8,40},{16,144},{24,56},{32,160},{40,8},{48,176},{56,24},{... | collective-permute-start | bytes 393224 | tf_op jit(solution)/shard_map/ppermute | solution.py:115
  21.1 8.7 %collective-permute-start.7 = (bf16[128,2048]{1,0:T(8,128)(2,1)S(1)}, bf16[128,2048]{1,0:T(8,128)(2,1)S(1)}, u32[]{:S(2)}, u32[]{:S(2)}) collective-permute-start(bf16[128,2048]{1,0:T(8,128)(2,1)S(1)} %bitcast.163), channel_id=1, source_target_pairs={{0,48},{8,200},{16,0},{24,216},{32,16},{40,232},{48,32},{56,248},{... | collective-permute-start | bytes 1572872 | tf_op jit(solution)/shard_map/ppermute | solution.py:123
  23.6 9.6 %collective-permute-start.5 = (bf16[128,2048]{1,0:T(8,128)(2,1)S(1)}, bf16[128,2048]{1,0:T(8,128)(2,1)S(1)}, u32[]{:S(2)}, u32[]{:S(2)}) collective-permute-start(bf16[128,2048]{1,0:T(8,128)(2,1)S(1)} %bitcast.164), channel_id=1, source_target_pairs={{0,16},{8,72},{16,32},{24,88},{32,48},{40,104},{48,0},{56,120},{64... | collective-permute-start | bytes 1572872 | tf_op jit(solution)/shard_map/ppermute | solution.py:122
  23.6 12.6 %collective-permute-start.4 = (bf16[128,2048]{1,0:T(8,128)(2,1)S(1)}, bf16[128,2048]{1,0:T(8,128)(2,1)S(1)}, u32[]{:S(2)}, u32[]{:S(2)}) collective-permute-start(bf16[128,2048]{1,0:T(8,128)(2,1)S(1)} %bitcast.165), channel_id=1, source_target_pairs={{0,8},{8,0},{16,24},{24,16},{32,40},{40,32},{48,56},{56,48},{64,72... | collective-permute-start | bytes 1572872 | tf_op jit(solution)/shard_map/ppermute | solution.py:105
  29.8 10.1 %collective-permute-start.10 = (bf16[64,2048]{1,0:T(8,128)(2,1)S(1)}, bf16[64,2048]{1,0:T(8,128)(2,1)S(1)}, u32[]{:S(2)}, u32[]{:S(2)}) collective-permute-start(bf16[64,2048]{1,0:T(8,128)(2,1)S(1)} %slice.154), channel_id=1, source_target_pairs={{0,48},{8,200},{16,0},{24,216},{32,16},{40,232},{48,32},{56,248},{... | collective-permute-start | bytes 786440 | tf_op jit(solution)/shard_map/ppermute | solution.py:127
  33.3 6.5 %collective-permute-start.9 = (bf16[64,2048]{1,0:T(8,128)(2,1)S(1)}, bf16[64,2048]{1,0:T(8,128)(2,1)S(1)}, u32[]{:S(2)}, u32[]{:S(2)}) collective-permute-start(bf16[64,2048]{1,0:T(8,128)(2,1)S(1)} %slice.153), channel_id=1, source_target_pairs={{0,16},{8,72},{16,32},{24,88},{32,48},{40,104},{48,0},{56,120},{64... | collective-permute-start | bytes 786440 | tf_op jit(solution)/shard_map/ppermute | solution.py:126
  33.4 10.7 %collective-permute-start.8 = (bf16[128,2048]{1,0:T(8,128)(2,1)S(1)}, bf16[128,2048]{1,0:T(8,128)(2,1)S(1)}, u32[]{:S(2)}, u32[]{:S(2)}) collective-permute-start(bf16[128,2048]{1,0:T(8,128)(2,1)S(1)} %collective-permute-done.7), channel_id=1, source_target_pairs={{0,8},{8,0},{16,24},{24,16},{32,40},{40,32},{48,56},{56,48},{64,72... | collective-permute-start | bytes 1572872 | tf_op jit(solution)/shard_map/ppermute | solution.py:105
  36.1 7.8 %collective-permute-start.6 = (bf16[128,2048]{1,0:T(8,128)(2,1)S(1)}, bf16[128,2048]{1,0:T(8,128)(2,1)S(1)}, u32[]{:S(2)}, u32[]{:S(2)}) collective-permute-start(bf16[128,2048]{1,0:T(8,128)(2,1)S(1)} %collective-permute-done.5), channel_id=1, source_target_pairs={{0,8},{8,0},{16,24},{24,16},{32,40},{40,32},{48,56},{56,48},{64,72... | collective-permute-start | bytes 1572872 | tf_op jit(solution)/shard_map/ppermute | solution.py:105
  56.2 11.8 %collective-permute-start.15 = (bf16[3,64,384]{2,1,0:T(8,128)(2,1)S(1)}, bf16[3,64,384]{2,1,0:T(8,128)(2,1)S(1)}, u32[]{:S(2)}, u32[]{:S(2)}) collective-permute-start(bf16[3,64,384]{2,1,0:T(8,128)(2,1)S(1)} %pad_maximum_fusion.4), channel_id=1, source_target_pairs={{0,7},{1,0},{2,1},{3,2},{4,3},{5,4},{6,5},{7,6},{8,15},{9,8},{10,9... | collective-permute-start | bytes 442376 | tf_op jit(solution)/shard_map/ppermute | solution.py:54
  62.0 10.0 %collective-permute-start.23 = (bf16[3,64,512]{2,1,0:T(8,128)(2,1)S(1)}, bf16[3,64,512]{2,1,0:T(8,128)(2,1)S(1)}, u32[]{:S(2)}, u32[]{:S(2)}) collective-permute-start(bf16[3,64,512]{2,1,0:T(8,128)(2,1)S(1)} %pad_maximum_fusion.2), channel_id=1, source_target_pairs={{0,7},{1,0},{2,1},{3,2},{4,3},{5,4},{6,5},{7,6},{8,15},{9,8},{10,9... | collective-permute-start | bytes 589832 | tf_op jit(solution)/shard_map/ppermute | solution.py:54
  64.8 6.9 %collective-permute-start.19 = (bf16[3,64,512]{2,1,0:T(8,128)(2,1)S(1)}, bf16[3,64,512]{2,1,0:T(8,128)(2,1)S(1)}, u32[]{:S(2)}, u32[]{:S(2)}) collective-permute-start(bf16[3,64,512]{2,1,0:T(8,128)(2,1)S(1)} %pad_maximum_fusion.1), channel_id=1, source_target_pairs={{0,1},{1,2},{2,3},{3,4},{4,5},{5,6},{6,7},{7,0},{8,9},{9,10},{10,1... | collective-permute-start | bytes 589832 | tf_op jit(solution)/shard_map/ppermute | solution.py:52
  67.9 7.2 %collective-permute-start.13 = (bf16[3,64,384]{2,1,0:T(8,128)(2,1)S(1)}, bf16[3,64,384]{2,1,0:T(8,128)(2,1)S(1)}, u32[]{:S(2)}, u32[]{:S(2)}) collective-permute-start(bf16[3,64,384]{2,1,0:T(8,128)(2,1)S(1)} %fusion.23), channel_id=1, source_target_pairs={{0,1},{1,2},{2,3},{3,4},{4,5},{5,6},{6,7},{7,0},{8,9},{9,10},{10,1... | collective-permute-start | bytes 442376 | tf_op jit(solution)/shard_map/ppermute | solution.py:52
  68.0 7.2 %collective-permute-start.16 = (bf16[3,64,384]{2,1,0:T(8,128)(2,1)S(1)}, bf16[3,64,384]{2,1,0:T(8,128)(2,1)S(1)}, u32[]{:S(2)}, u32[]{:S(2)}) collective-permute-start(bf16[3,64,384]{2,1,0:T(8,128)(2,1)S(1)} %fusion.25), channel_id=1, source_target_pairs={{0,7},{1,0},{2,1},{3,2},{4,3},{5,4},{6,5},{7,6},{8,15},{9,8},{10,9... | collective-permute-start | bytes 442376 | tf_op jit(solution)/shard_map/ppermute | solution.py:54
  71.8 6.4 %collective-permute-start.20 = (bf16[3,64,512]{2,1,0:T(8,128)(2,1)S(1)}, bf16[3,64,512]{2,1,0:T(8,128)(2,1)S(1)}, u32[]{:S(2)}, u32[]{:S(2)}) collective-permute-start(bf16[3,64,512]{2,1,0:T(8,128)(2,1)S(1)} %fusion.18), channel_id=1, source_target_pairs={{0,1},{1,2},{2,3},{3,4},{4,5},{5,6},{6,7},{7,0},{8,9},{9,10},{10,1... | collective-permute-start | bytes 589832 | tf_op jit(solution)/shard_map/ppermute | solution.py:52
  75.2 11.5 %collective-permute-start.14 = (bf16[3,64,384]{2,1,0:T(8,128)(2,1)S(1)}, bf16[3,64,384]{2,1,0:T(8,128)(2,1)S(1)}, u32[]{:S(2)}, u32[]{:S(2)}) collective-permute-start(bf16[3,64,384]{2,1,0:T(8,128)(2,1)S(1)} %fusion.24), channel_id=1, source_target_pairs={{0,1},{1,2},{2,3},{3,4},{4,5},{5,6},{6,7},{7,0},{8,9},{9,10},{10,1... | collective-permute-start | bytes 442376 | tf_op jit(solution)/shard_map/ppermute | solution.py:52
  78.2 8.3 %collective-permute-start.21 = (bf16[3,64,512]{2,1,0:T(8,128)(2,1)S(1)}, bf16[3,64,512]{2,1,0:T(8,128)(2,1)S(1)}, u32[]{:S(2)}, u32[]{:S(2)}) collective-permute-start(bf16[3,64,512]{2,1,0:T(8,128)(2,1)S(1)} %fusion.19), channel_id=1, source_target_pairs={{0,1},{1,2},{2,3},{3,4},{4,5},{5,6},{6,7},{7,0},{8,9},{9,10},{10,1... | collective-permute-start | bytes 589832 | tf_op jit(solution)/shard_map/ppermute | solution.py:52
  78.4 9.1 %collective-permute-start.25 = (bf16[3,64,512]{2,1,0:T(8,128)(2,1)S(1)}, bf16[3,64,512]{2,1,0:T(8,128)(2,1)S(1)}, u32[]{:S(2)}, u32[]{:S(2)}) collective-permute-start(bf16[3,64,512]{2,1,0:T(8,128)(2,1)S(1)} %fusion.22), channel_id=1, source_target_pairs={{0,7},{1,0},{2,1},{3,2},{4,3},{5,4},{6,5},{7,6},{8,15},{9,8},{10,9... | collective-permute-start | bytes 589832 | tf_op jit(solution)/shard_map/ppermute | solution.py:54
  81.2 6.3 %collective-permute-start.18 = (bf16[3,64,384]{2,1,0:T(8,128)(2,1)S(1)}, bf16[3,64,384]{2,1,0:T(8,128)(2,1)S(1)}, u32[]{:S(2)}, u32[]{:S(2)}) collective-permute-start(bf16[3,64,384]{2,1,0:T(8,128)(2,1)S(1)} %fusion.27), channel_id=1, source_target_pairs={{0,7},{1,0},{2,1},{3,2},{4,3},{5,4},{6,5},{7,6},{8,15},{9,8},{10,9... | collective-permute-start | bytes 442376 | tf_op jit(solution)/shard_map/ppermute | solution.py:54
  97.0 26.0 %all-to-all-start = ((bf16[32,64,192]{2,1,0:T(8,128)(2,1)}), bf16[32,64,192]{2,1,0:T(8,128)(2,1)S(1)}, u32[]{:S(2)}, u32[]{:S(2)}) async-start(bf16[32,64,192]{2,1,0:T(8,128)(2,1)} %broadcast_in_dim.65), calls=%async_computation | async-start | bytes 2097152 | tf_op jit(solution)/shard_map/all_to_all | solution.py:263
  123.9 17.5 %all-to-all-start.1 = ((bf16[8,64,192]{2,1,0:T(8,128)(2,1)}), bf16[8,64,192]{2,1,0:T(8,128)(2,1)S(1)}, u32[]{:S(2)}, u32[]{:S(2)}) async-start(bf16[8,64,192]{2,1,0:T(8,128)(2,1)} %broadcast_in_dim.66), calls=%async_computation.1 | async-start | bytes 524288 | tf_op jit(solution)/shard_map/all_to_all | solution.py:263
  161.7 24.2 %all-to-all-start.2 = ((bf16[16,16,2048]{2,1,0:T(8,128)(2,1)}), bf16[16,16,2048]{2,1,0:T(8,128)(2,1)}, u32[]{:S(2)}, u32[]{:S(2)}) async-start(bf16[16,16,2048]{2,1,0:T(8,128)(2,1)} %bitcast.179), calls=%async_computation.2 | async-start | bytes 2097152 | tf_op jit(solution)/shard_map/all_to_all | solution.py:301
  (22 other events, 148.8 us)
Sparse Core Ops, SparseCore 0:
  94.9 44.6 all-gather.1
where the time goes:
time: 196 us; the launch traced here: 195 us
  starting transfers between devices  64.6 us (33%)
  waiting for transfers between devices  63.1 us (32%)
  matrix products  28.3 us (14%)
  between operations  14.8 us (8%)
  local copies, waits for them, and re-layouts  13.1 us (7%)
  other arithmetic  11.1 us (6%)
    all_to_all x2, waiting for transfers between devices, to_all(): lax.all_to_all(jnp.broadcast_to(value[None], (count,) + value.shape), axi...  24 us
    ppermute x7, starting transfers between devices, two_way_rings(): down = lax.ppermute(down, axis, shifted(size, -1))  22.6 us
    dot_general x13, matrix products, multiply_right_transposed(): lax.dot_general(left, right, (((1,), (1,)), ((), ())), preferred_element_...  21.7 us
    all_to_all x1, waiting for transfers between devices, body(): lax.all_to_all(share, 'row', 0, 0, axis_index_groups=same_core, tiled=True)  13 us
    all_to_all x2, starting transfers between devices, to_all(): lax.all_to_all(jnp.broadcast_to(value[None], (count,) + value.shape), axi...  12.4 us
    ppermute x5, starting transfers between devices, to_other_core(): return lax.ppermute(value, 'row', swap)  11.9 us
    ppermute x7, waiting for transfers between devices, two_way_rings(): up = lax.ppermute(up, axis, shifted(size, 1))  10.8 us
    all_to_all x1, starting transfers between devices, body(): lax.all_to_all(share, 'row', 0, 0, axis_index_groups=same_core, tiled=True)  7.17 us
  transfers between devices with their start and end apart: 31, of which 15 were waited for; matrix products, arithmetic and copies ran while one was open for 10% of the time, Pallas kernels for 0%

commit v1 on v0

--- a/solution.py
+++ b/solution.py
@@ -123,8 +123,8 @@
     after = lax.ppermute(slab, "row", moves(0, -1))
     far = jnp.concatenate(
         [
-            lax.ppermute(before[:half], "row", moves(0, 1)),
-            lax.ppermute(after[half:], "row", moves(0, -1)),
+            lax.ppermute(slab[:half], "row", moves(0, 2)),
+            lax.ppermute(slab[half:], "row", moves(0, -2)),
         ],
         axis=0,
     )
@@ -266,15 +266,9 @@
 
     packed = jnp.concatenate(
         [
-            earlier_deltas[1],
-            later_deltas[1],
-            earlier_deltas[2],
-            later_deltas[2],
-            earlier_deltas[0],
-            later_deltas[0],
-            low[0],
-            low[1],
-            low[2],
+            piece
+            for which, rank_part in ((1, low[0]), (2, low[1]), (0, low[2]))
+            for piece in (earlier_deltas[which], later_deltas[which], rank_part)
         ],
         axis=1,
     )
@@ -282,19 +276,24 @@
     factor_parts = to_all(own_factors.astype(jnp.bfloat16), "row")
     own_factors = jnp.sum(factor_parts.astype(jnp.float32), axis=0).astype(jnp.bfloat16)
     factors = to_all(own_factors, "col").reshape(tokens_all, 3 * rank)
-    gate_weight, up_weight = lax.optimization_barrier(
-        (frozen_gate_weight, frozen_up_weight, packed)
-    )[:2]
-    input_weight = jnp.concatenate([gate_weight, up_weight], axis=1)
-    piece, factors, input_weight = lax.optimization_barrier((piece, factors, input_weight))
-
-    deltas = piece[:, : 2 * hidden_units].reshape(chips, 2, share_tokens, 2 * hidden_units)
+    piece, factors = lax.optimization_barrier((piece, factors))
+    packed_width = hidden_units + rank
+    piece_gate, piece_up, piece_hidden = [
+        piece[:, i * packed_width : i * packed_width + hidden_units] for i in range(3)
+    ]
+    gate_low, up_low, down_low = [
+        piece[:, i * packed_width + hidden_units : (i + 1) * packed_width] for i in range(3)
+    ]
 
     def input_part(which):
-        chosen = lax.dynamic_index_in_dim(deltas, which, 1, keepdims=False)
-        return multiply_right_transposed(
-            chosen.reshape(chips * share_tokens, 2 * hidden_units), input_weight
-        )
+        def term(deltas, weight):
+            lines = deltas.reshape(chips, 2, share_tokens, hidden_units)
+            chosen = lax.dynamic_index_in_dim(lines, which, 1, keepdims=False)
+            return multiply_right_transposed(
+                chosen.reshape(chips * share_tokens, hidden_units), weight
+            )
+
+        return term(piece_gate, frozen_gate_weight) + term(piece_up, frozen_up_weight)
 
     other = lax.ppermute(input_part(1 - core).astype(jnp.bfloat16), "row", swap)
     share = (input_part(core) + other.astype(jnp.float32)).astype(jnp.bfloat16)
@@ -327,11 +326,6 @@
         factors[:, :rank], output_columns
     )
 
-    piece_gate = piece[:, :hidden_units]
-    piece_up = piece[:, hidden_units : 2 * hidden_units]
-    piece_hidden = piece[:, 2 * hidden_units : 3 * hidden_units]
-    lows = piece[:, 3 * hidden_units :]
-    gate_low, up_low, down_low = [lows[:, i * rank : (i + 1) * rank] for i in range(3)]
     gate_adapter_second_gradient = adapter_scale * multiply_left_transposed(gate_low, piece_gate)
     up_adapter_second_gradient = adapter_scale * multiply_left_transposed(up_low, piece_up)
     down_adapter_first_gradient = adapter_scale * multiply_left_transposed(piece_hidden, down_low)

time: 196 us -> 194 us (0.990)
  blocking collectives: 0 us -> 28.3 us
  starting transfers between devices: 64.6 us -> 49.1 us
  waiting for transfers between devices: 63.1 us -> 52.4 us
  other arithmetic: 11.1 us -> 5.28 us
  matrix products: 28.3 us -> 31.1 us
    all_to_all x0 -> x1, blocking collectives: none -> 28.3 us  [to_all(): lax.all_to_all(jnp.broadcast_to(value[None], (count,) + value.shape), axi...]
    all_to_all x2 -> x1, waiting for transfers between devices: 24 us -> 10.6 us  [to_all(): lax.all_to_all(jnp.broadcast_to(value[None], (count,) + value.shape), axi...]
    all_to_all x2 -> x1, starting transfers between devices: 12.4 us -> 4.05 us  [to_all(): lax.all_to_all(jnp.broadcast_to(value[None], (count,) + value.shape), axi...]
    concatenate x1 -> x0, other arithmetic: 7.09 us -> none  [body(): input_weight = jnp.concatenate([gate_weight, up_weight], axis=1)]
    ppermute x2, waiting for transfers between devices: 3.47 us -> 8.65 us  [the longest x1 8.45 us: gather_tokens(): lax.ppermute(slab[half:], 'row', moves(0, -2))]
    ppermute x1, waiting for transfers between devices: 3.76 us -> 0.01 us  [gather_tokens(): after = lax.ppermute(slab, 'row', moves(0, -1))]
    ppermute x5, starting transfers between devices: 11.9 us -> 8.88 us  [to_other_core(): return lax.ppermute(value, 'row', swap)]
    dot_general x6, matrix products: 1.17 us -> 4.19 us  [matrix_multiply(): return jnp.dot(left, right, preferred_element_type=jnp.float32)]
  transfers between devices with their start and end apart: 31 -> 30, of which waited for: 15 -> 14; matrix products, arithmetic and copies ran while one was open for 10% -> 11% of each run, Pallas kernels for 0% -> 0%
where the time goes in v1:
time: 194 us; the launch traced here: 193 us
  waiting for transfers between devices  52.4 us (27%)
  starting transfers between devices  49.1 us (25%)
  matrix products  31.1 us (16%)
  blocking collectives  28.3 us (15%)
  between operations  14.8 us (8%)
  local copies, waits for them, and re-layouts  12.5 us (6%)
  other arithmetic  5.28 us (3%)
    all_to_all x1, blocking collectives, to_all(): lax.all_to_all(jnp.broadcast_to(value[None], (count,) + value.shape), axi...  28.3 us
    ppermute x7, starting transfers between devices, two_way_rings(): down = lax.ppermute(down, axis, shifted(size, -1))  22.8 us
    dot_general x15, matrix products, multiply_right_transposed(): lax.dot_general(left, right, (((1,), (1,)), ((), ())), preferred_element_...  19.9 us
    all_to_all x1, waiting for transfers between devices, body(): lax.all_to_all(share, 'row', 0, 0, axis_index_groups=same_core, tiled=True)  13.9 us
    all_to_all x1, waiting for transfers between devices, to_all(): lax.all_to_all(jnp.broadcast_to(value[None], (count,) + value.shape), axi...  10.6 us
    ppermute x7, waiting for transfers between devices, two_way_rings(): up = lax.ppermute(up, axis, shifted(size, 1))  9.78 us
    ppermute x5, starting transfers between devices, to_other_core(): return lax.ppermute(value, 'row', swap)  8.88 us
    ppermute x1, waiting for transfers between devices, gather_tokens(): lax.ppermute(slab[half:], 'row', moves(0, -2))  8.45 us
  transfers between devices with their start and end apart: 30, of which 14 were waited for; matrix products, arithmetic and copies ran while one was open for 11% of the time, Pallas kernels for 0%

profile of v1, /device:TPU:1, one launch (start us, length us, event | category | flops | bytes accessed | tf_op | source)
XLA Modules:
  0.0 193.4 jit_solution(13975615769230982409)
XLA Ops:
  8.1 3.3 %collective-permute-start = (bf16[16,2048]{1,0:T(8,128)(2,1)S(1)}, bf16[16,2048]{1,0:T(8,128)(2,1)S(1)}, u32[]{:S(2)}, u32[]{:S(2)}) collective-permute-start(bf16[16,2048]{1,0:T(8,128)(2,1)S(1)} %broadcast_select_fusion.2), channel_id=1, source_target_pairs={{0,8},{8,0},{16,24},{24,16},{32,40},{40,32},{48,56},{56,48},{64,72... | collective-permute-start | bytes 196616 | tf_op jit(solution)/shard_map/ppermute | solution.py:105
  13.3 2.7 %collective-permute-start.2 = (bf16[32,2048]{1,0:T(8,128)(2,1)S(1)}, bf16[32,2048]{1,0:T(8,128)(2,1)S(1)}, u32[]{:S(2)}, u32[]{:S(2)}) collective-permute-start(bf16[32,2048]{1,0:T(8,128)(2,1)S(1)} %pad_maximum_fusion.4), channel_id=1, source_target_pairs={{0,192},{8,56},{16,208},{24,8},{32,224},{40,24},{48,240},{56,40},{... | collective-permute-start | bytes 393224 | tf_op jit(solution)/shard_map/ppermute | solution.py:115
  16.0 2.6 %collective-permute-done.1 = bf16[32,2048]{1,0:T(8,128)(2,1)S(1)} collective-permute-done((bf16[32,2048]{1,0:T(8,128)(2,1)S(1)}, bf16[32,2048]{1,0:T(8,128)(2,1)S(1)}, u32[]{:S(2)}, u32[]{:S(2)}) %collective-permute-start.1) | collective-permute-done | bytes 131104 | tf_op jit(solution)/shard_map/ppermute | solution.py:115
  22.6 2.4 %collective-permute-start.4 = (bf16[128,2048]{1,0:T(8,128)(2,1)S(1)}, bf16[128,2048]{1,0:T(8,128)(2,1)S(1)}, u32[]{:S(2)}, u32[]{:S(2)}) collective-permute-start(bf16[128,2048]{1,0:T(8,128)(2,1)S(1)} %bitcast.166), channel_id=1, source_target_pairs={{0,8},{8,0},{16,24},{24,16},{32,40},{40,32},{48,56},{56,48},{64,72... | collective-permute-start | bytes 1572872 | tf_op jit(solution)/shard_map/ppermute | solution.py:105
  24.9 2.7 %collective-permute-start.7 = (bf16[128,2048]{1,0:T(8,128)(2,1)S(1)}, bf16[128,2048]{1,0:T(8,128)(2,1)S(1)}, u32[]{:S(2)}, u32[]{:S(2)}) collective-permute-start(bf16[128,2048]{1,0:T(8,128)(2,1)S(1)} %bitcast.168), channel_id=1, source_target_pairs={{0,48},{8,200},{16,0},{24,216},{32,16},{40,232},{48,32},{56,248},{... | collective-permute-start | bytes 1572872 | tf_op jit(solution)/shard_map/ppermute | solution.py:123
  28.8 8.5 %collective-permute-done.10 = bf16[64,2048]{1,0:T(8,128)(2,1)S(1)} collective-permute-done((bf16[64,2048]{1,0:T(8,128)(2,1)S(1)}, bf16[64,2048]{1,0:T(8,128)(2,1)S(1)}, u32[]{:S(2)}, u32[]{:S(2)}) %collective-permute-start.10) | collective-permute-done | bytes 262176 | tf_op jit(solution)/shard_map/ppermute | solution.py:127
  37.2 2.7 %collective-permute-start.11 = (bf16[128,2048]{1,0:T(8,128)(2,1)S(1)}, bf16[128,2048]{1,0:T(8,128)(2,1)S(1)}, u32[]{:S(2)}, u32[]{:S(2)}) collective-permute-start(bf16[128,2048]{1,0:T(8,128)(2,1)S(1)} %constant_dynamic-update-slice_fusion.1), channel_id=1, source_target_pairs={{0,8},{8,0},{16,24},{24,16},{32,40},{40,32},{48,56},{56,48},{64,72... | collective-permute-start | bytes 1572872 | tf_op jit(solution)/shard_map/ppermute | solution.py:105
  46.3 2.4 %fusion = f32[512,896]{1,0:T(8,128)S(1)} fusion(bf16[512,2048]{1,0:T(8,128)(2,1)S(1)} %bitcast.175, bf16[2048,64]{0,1:T(8,128)(2,1)S(1)} %copy-done.11, bf16[2048,832]{0,1:T(8,128)(2,1)S(1)} %copy-done), kind=kOutput, calls=%fused_computation | convolution fusion | flops 1886388224 | bytes 7602176 | tf_op jit(solution)/shard_map/dot_general | solution.py:16
  48.7 2.4 %fusion.4 = f32[512,896]{1,0:T(8,128)S(1)} fusion(bf16[512,2048]{1,0:T(8,128)(2,1)S(1)} %bitcast.176, bf16[2048,64]{0,1:T(8,128)(2,1)S(1)} %copy-done.9, bf16[2048,832]{0,1:T(8,128)(2,1)S(1)} %copy-done.1), kind=kOutput, calls=%fused_computation.4 | convolution fusion | flops 1886388224 | bytes 7602176 | tf_op jit(solution)/shard_map/dot_general | solution.py:16
  51.1 2.4 %fusion.8 = f32[512,896]{1,0:T(8,128)S(1)} fusion(bf16[512,2048]{1,0:T(8,128)(2,1)S(1)} %bitcast.173, bf16[64,2048]{1,0:T(8,128)(2,1)S(1)} %copy-done.15, bf16[832,2048]{1,0:T(8,128)(2,1)S(1)} %copy-done.14), kind=kOutput, calls=%fused_computation.8 | convolution fusion | flops 1886388224 | bytes 7602176 | tf_op jit(solution)/shard_map/dot_general | solution.py:16
  54.2 4.0 %collective-permute-start.15 = (bf16[3,64,384]{2,1,0:T(8,128)(2,1)S(1)}, bf16[3,64,384]{2,1,0:T(8,128)(2,1)S(1)}, u32[]{:S(2)}, u32[]{:S(2)}) collective-permute-start(bf16[3,64,384]{2,1,0:T(8,128)(2,1)S(1)} %pad_maximum_fusion.3), channel_id=1, source_target_pairs={{0,7},{1,0},{2,1},{3,2},{4,3},{5,4},{6,5},{7,6},{8,15},{9,8},{10,9... | collective-permute-start | bytes 442376 | tf_op jit(solution)/shard_map/ppermute | solution.py:54
  58.3 2.7 %collective-permute-start.23 = (bf16[3,64,512]{2,1,0:T(8,128)(2,1)S(1)}, bf16[3,64,512]{2,1,0:T(8,128)(2,1)S(1)}, u32[]{:S(2)}, u32[]{:S(2)}) collective-permute-start(bf16[3,64,512]{2,1,0:T(8,128)(2,1)S(1)} %pad_maximum_fusion.1), channel_id=1, source_target_pairs={{0,7},{1,0},{2,1},{3,2},{4,3},{5,4},{6,5},{7,6},{8,15},{9,8},{10,9... | collective-permute-start | bytes 589832 | tf_op jit(solution)/shard_map/ppermute | solution.py:54
  61.3 3.2 %collective-permute-start.16 = (bf16[3,64,384]{2,1,0:T(8,128)(2,1)S(1)}, bf16[3,64,384]{2,1,0:T(8,128)(2,1)S(1)}, u32[]{:S(2)}, u32[]{:S(2)}) collective-permute-start(bf16[3,64,384]{2,1,0:T(8,128)(2,1)S(1)} %fusion.24), channel_id=1, source_target_pairs={{0,7},{1,0},{2,1},{3,2},{4,3},{5,4},{6,5},{7,6},{8,15},{9,8},{10,9... | collective-permute-start | bytes 442376 | tf_op jit(solution)/shard_map/ppermute | solution.py:54
  64.9 3.7 %collective-permute-start.24 = (bf16[3,64,512]{2,1,0:T(8,128)(2,1)S(1)}, bf16[3,64,512]{2,1,0:T(8,128)(2,1)S(1)}, u32[]{:S(2)}, u32[]{:S(2)}) collective-permute-start(bf16[3,64,512]{2,1,0:T(8,128)(2,1)S(1)} %fusion.20), channel_id=1, source_target_pairs={{0,7},{1,0},{2,1},{3,2},{4,3},{5,4},{6,5},{7,6},{8,15},{9,8},{10,9... | collective-permute-start | bytes 589832 | tf_op jit(solution)/shard_map/ppermute | solution.py:54
  68.8 3.0 %collective-permute-start.17 = (bf16[3,64,384]{2,1,0:T(8,128)(2,1)S(1)}, bf16[3,64,384]{2,1,0:T(8,128)(2,1)S(1)}, u32[]{:S(2)}, u32[]{:S(2)}) collective-permute-start(bf16[3,64,384]{2,1,0:T(8,128)(2,1)S(1)} %fusion.25), channel_id=1, source_target_pairs={{0,7},{1,0},{2,1},{3,2},{4,3},{5,4},{6,5},{7,6},{8,15},{9,8},{10,9... | collective-permute-start | bytes 442376 | tf_op jit(solution)/shard_map/ppermute | solution.py:54
  72.0 2.7 %collective-permute-start.25 = (bf16[3,64,512]{2,1,0:T(8,128)(2,1)S(1)}, bf16[3,64,512]{2,1,0:T(8,128)(2,1)S(1)}, u32[]{:S(2)}, u32[]{:S(2)}) collective-permute-start(bf16[3,64,512]{2,1,0:T(8,128)(2,1)S(1)} %fusion.21), channel_id=1, source_target_pairs={{0,7},{1,0},{2,1},{3,2},{4,3},{5,4},{6,5},{7,6},{8,15},{9,8},{10,9... | collective-permute-start | bytes 589832 | tf_op jit(solution)/shard_map/ppermute | solution.py:54
  75.5 3.5 %collective-permute-start.18 = (bf16[3,64,384]{2,1,0:T(8,128)(2,1)S(1)}, bf16[3,64,384]{2,1,0:T(8,128)(2,1)S(1)}, u32[]{:S(2)}, u32[]{:S(2)}) collective-permute-start(bf16[3,64,384]{2,1,0:T(8,128)(2,1)S(1)} %fusion.26), channel_id=1, source_target_pairs={{0,7},{1,0},{2,1},{3,2},{4,3},{5,4},{6,5},{7,6},{8,15},{9,8},{10,9... | collective-permute-start | bytes 442376 | tf_op jit(solution)/shard_map/ppermute | solution.py:54
  79.0 4.1 %collective-permute-done.21 = bf16[3,64,512]{2,1,0:T(8,128)(2,1)S(1)} collective-permute-done((bf16[3,64,512]{2,1,0:T(8,128)(2,1)S(1)}, bf16[3,64,512]{2,1,0:T(8,128)(2,1)S(1)}, u32[]{:S(2)}, u32[]{:S(2)}) %collective-permute-start.21) | collective-permute-done | bytes 196640 | tf_op jit(solution)/shard_map/ppermute | solution.py:52
  83.3 5.6 %collective-permute-done.22 = bf16[3,64,512]{2,1,0:T(8,128)(2,1)S(1)} collective-permute-done((bf16[3,64,512]{2,1,0:T(8,128)(2,1)S(1)}, bf16[3,64,512]{2,1,0:T(8,128)(2,1)S(1)}, u32[]{:S(2)}, u32[]{:S(2)}) %collective-permute-start.22) | collective-permute-done | bytes 196640 | tf_op jit(solution)/shard_map/ppermute | solution.py:52
  100.5 28.3 %all_to_all.19 = bf16[32,64,192]{2,1,0:T(8,128)(2,1)} all-to-all(bf16[32,64,192]{2,1,0:T(8,128)(2,1)S(1)} %broadcast_in_dim.65), channel_id=1, replica_groups=mesh['row'=32,'col'=8] {'row'}, dimensions={0} | all-to-all | bytes 1572864 | tf_op jit(solution)/shard_map/all_to_all | solution.py:263
  130.9 4.1 %all-to-all-start.1 = ((bf16[8,64,192]{2,1,0:T(8,128)(2,1)}), bf16[8,64,192]{2,1,0:T(8,128)(2,1)}, u32[]{:S(2)}, u32[]{:S(2)}) async-start(bf16[8,64,192]{2,1,0:T(8,128)(2,1)} %broadcast_in_dim.66), calls=%async_computation.1 | async-start | bytes 524288 | tf_op jit(solution)/shard_map/all_to_all | solution.py:263
  136.0 10.6 %all-to-all-done.1 = bf16[8,64,192]{2,1,0:T(8,128)(2,1)} async-done(((bf16[8,64,192]{2,1,0:T(8,128)(2,1)}), bf16[8,64,192]{2,1,0:T(8,128)(2,1)}, u32[]{:S(2)}, u32[]{:S(2)}) %all-to-all-start.1) | async-done | bytes 196640 | tf_op jit(solution)/shard_map/all_to_all | solution.py:263
  161.3 4.5 %all-to-all-start.2 = ((bf16[16,16,2048]{2,1,0:T(8,128)(2,1)}), bf16[16,16,2048]{2,1,0:T(8,128)(2,1)}, u32[]{:S(2)}, u32[]{:S(2)}) async-start(bf16[16,16,2048]{2,1,0:T(8,128)(2,1)} %bitcast.170), calls=%async_computation.2 | async-start | bytes 2097152 | tf_op jit(solution)/shard_map/all_to_all | solution.py:300
  169.8 13.9 %all-to-all-done.2 = bf16[16,16,2048]{2,1,0:T(8,128)(2,1)} async-done(((bf16[16,16,2048]{2,1,0:T(8,128)(2,1)}), bf16[16,16,2048]{2,1,0:T(8,128)(2,1)}, u32[]{:S(2)}, u32[]{:S(2)}) %all-to-all-start.2) | async-done | bytes 1048608 | tf_op jit(solution)/shard_map/all_to_all | solution.py:300
  (157 shorter events, 52.9 us)
Async XLA Ops:
  7.2 139.4 %all-gather.2.cloned.1.call-start = ((), (), s32[]{:S(2)}) async-start(), calls=%async_computation.3 | async-start | bytes 3096576 | tf_op jit(solution)/shard_map/all_gather | solution.py:275
  13.3 6.0 %collective-permute-start.2 = (bf16[32,2048]{1,0:T(8,128)(2,1)S(1)}, bf16[32,2048]{1,0:T(8,128)(2,1)S(1)}, u32[]{:S(2)}, u32[]{:S(2)}) collective-permute-start(bf16[32,2048]{1,0:T(8,128)(2,1)S(1)} %pad_maximum_fusion.4), channel_id=1, source_target_pairs={{0,192},{8,56},{16,208},{24,8},{32,224},{40,24},{48,240},{56,40},{... | collective-permute-start | bytes 393224 | tf_op jit(solution)/shard_map/ppermute | solution.py:115
  21.6 7.1 %collective-permute-start.9 = (bf16[64,2048]{1,0:T(8,128)(2,1)S(1)}, bf16[64,2048]{1,0:T(8,128)(2,1)S(1)}, u32[]{:S(2)}, u32[]{:S(2)}) collective-permute-start(bf16[64,2048]{1,0:T(8,128)(2,1)S(1)} %bitcast.217), channel_id=1, source_target_pairs={{0,32},{8,136},{16,48},{24,152},{32,0},{40,168},{48,16},{56,184},{... | collective-permute-start | bytes 786440 | tf_op jit(solution)/shard_map/ppermute | solution.py:126
  22.6 17.9 %collective-permute-start.4 = (bf16[128,2048]{1,0:T(8,128)(2,1)S(1)}, bf16[128,2048]{1,0:T(8,128)(2,1)S(1)}, u32[]{:S(2)}, u32[]{:S(2)}) collective-permute-start(bf16[128,2048]{1,0:T(8,128)(2,1)S(1)} %bitcast.166), channel_id=1, source_target_pairs={{0,8},{8,0},{16,24},{24,16},{32,40},{40,32},{48,56},{56,48},{64,72... | collective-permute-start | bytes 1572872 | tf_op jit(solution)/shard_map/ppermute | solution.py:105
  24.9 15.0 %collective-permute-start.5 = (bf16[128,2048]{1,0:T(8,128)(2,1)S(1)}, bf16[128,2048]{1,0:T(8,128)(2,1)S(1)}, u32[]{:S(2)}, u32[]{:S(2)}) collective-permute-start(bf16[128,2048]{1,0:T(8,128)(2,1)S(1)} %bitcast.167), channel_id=1, source_target_pairs={{0,16},{8,72},{16,32},{24,88},{32,48},{40,104},{48,0},{56,120},{64... | collective-permute-start | bytes 1572872 | tf_op jit(solution)/shard_map/ppermute | solution.py:122
  24.9 15.1 %collective-permute-start.7 = (bf16[128,2048]{1,0:T(8,128)(2,1)S(1)}, bf16[128,2048]{1,0:T(8,128)(2,1)S(1)}, u32[]{:S(2)}, u32[]{:S(2)}) collective-permute-start(bf16[128,2048]{1,0:T(8,128)(2,1)S(1)} %bitcast.168), channel_id=1, source_target_pairs={{0,48},{8,200},{16,0},{24,216},{32,16},{40,232},{48,32},{56,248},{... | collective-permute-start | bytes 1572872 | tf_op jit(solution)/shard_map/ppermute | solution.py:123
  27.6 9.6 %collective-permute-start.10 = (bf16[64,2048]{1,0:T(8,128)(2,1)S(1)}, bf16[64,2048]{1,0:T(8,128)(2,1)S(1)}, u32[]{:S(2)}, u32[]{:S(2)}) collective-permute-start(bf16[64,2048]{1,0:T(8,128)(2,1)S(1)} %bitcast.216), channel_id=1, source_target_pairs={{0,32},{8,136},{16,48},{24,152},{32,0},{40,168},{48,16},{56,184},{... | collective-permute-start | bytes 786440 | tf_op jit(solution)/shard_map/ppermute | solution.py:127
  37.2 5.9 %collective-permute-start.11 = (bf16[128,2048]{1,0:T(8,128)(2,1)S(1)}, bf16[128,2048]{1,0:T(8,128)(2,1)S(1)}, u32[]{:S(2)}, u32[]{:S(2)}) collective-permute-start(bf16[128,2048]{1,0:T(8,128)(2,1)S(1)} %constant_dynamic-update-slice_fusion.1), channel_id=1, source_target_pairs={{0,8},{8,0},{16,24},{24,16},{32,40},{40,32},{48,56},{56,48},{64,72... | collective-permute-start | bytes 1572872 | tf_op jit(solution)/shard_map/ppermute | solution.py:105
  54.2 7.1 %collective-permute-start.15 = (bf16[3,64,384]{2,1,0:T(8,128)(2,1)S(1)}, bf16[3,64,384]{2,1,0:T(8,128)(2,1)S(1)}, u32[]{:S(2)}, u32[]{:S(2)}) collective-permute-start(bf16[3,64,384]{2,1,0:T(8,128)(2,1)S(1)} %pad_maximum_fusion.3), channel_id=1, source_target_pairs={{0,7},{1,0},{2,1},{3,2},{4,3},{5,4},{6,5},{7,6},{8,15},{9,8},{10,9... | collective-permute-start | bytes 442376 | tf_op jit(solution)/shard_map/ppermute | solution.py:54
  58.2 6.4 %collective-permute-start.12 = (bf16[3,64,384]{2,1,0:T(8,128)(2,1)S(1)}, bf16[3,64,384]{2,1,0:T(8,128)(2,1)S(1)}, u32[]{:S(2)}, u32[]{:S(2)}) collective-permute-start(bf16[3,64,384]{2,1,0:T(8,128)(2,1)S(1)} %pad_maximum_fusion.2), channel_id=1, source_target_pairs={{0,1},{1,2},{2,3},{3,4},{4,5},{5,6},{6,7},{7,0},{8,9},{9,10},{10,1... | collective-permute-start | bytes 442376 | tf_op jit(solution)/shard_map/ppermute | solution.py:52
  58.3 6.5 %collective-permute-start.23 = (bf16[3,64,512]{2,1,0:T(8,128)(2,1)S(1)}, bf16[3,64,512]{2,1,0:T(8,128)(2,1)S(1)}, u32[]{:S(2)}, u32[]{:S(2)}) collective-permute-start(bf16[3,64,512]{2,1,0:T(8,128)(2,1)S(1)} %pad_maximum_fusion.1), channel_id=1, source_target_pairs={{0,7},{1,0},{2,1},{3,2},{4,3},{5,4},{6,5},{7,6},{8,15},{9,8},{10,9... | collective-permute-start | bytes 589832 | tf_op jit(solution)/shard_map/ppermute | solution.py:54
  61.1 7.5 %collective-permute-start.19 = (bf16[3,64,512]{2,1,0:T(8,128)(2,1)S(1)}, bf16[3,64,512]{2,1,0:T(8,128)(2,1)S(1)}, u32[]{:S(2)}, u32[]{:S(2)}) collective-permute-start(bf16[3,64,512]{2,1,0:T(8,128)(2,1)S(1)} %pad_maximum_fusion), channel_id=1, source_target_pairs={{0,1},{1,2},{2,3},{3,4},{4,5},{5,6},{6,7},{7,0},{8,9},{9,10},{10,1... | collective-permute-start | bytes 589832 | tf_op jit(solution)/shard_map/ppermute | solution.py:52
  61.3 7.4 %collective-permute-start.16 = (bf16[3,64,384]{2,1,0:T(8,128)(2,1)S(1)}, bf16[3,64,384]{2,1,0:T(8,128)(2,1)S(1)}, u32[]{:S(2)}, u32[]{:S(2)}) collective-permute-start(bf16[3,64,384]{2,1,0:T(8,128)(2,1)S(1)} %fusion.24), channel_id=1, source_target_pairs={{0,7},{1,0},{2,1},{3,2},{4,3},{5,4},{6,5},{7,6},{8,15},{9,8},{10,9... | collective-permute-start | bytes 442376 | tf_op jit(solution)/shard_map/ppermute | solution.py:54
  64.6 7.2 %collective-permute-start.13 = (bf16[3,64,384]{2,1,0:T(8,128)(2,1)S(1)}, bf16[3,64,384]{2,1,0:T(8,128)(2,1)S(1)}, u32[]{:S(2)}, u32[]{:S(2)}) collective-permute-start(bf16[3,64,384]{2,1,0:T(8,128)(2,1)S(1)} %fusion.22), channel_id=1, source_target_pairs={{0,1},{1,2},{2,3},{3,4},{4,5},{5,6},{6,7},{7,0},{8,9},{9,10},{10,1... | collective-permute-start | bytes 442376 | tf_op jit(solution)/shard_map/ppermute | solution.py:52
  64.9 7.0 %collective-permute-start.24 = (bf16[3,64,512]{2,1,0:T(8,128)(2,1)S(1)}, bf16[3,64,512]{2,1,0:T(8,128)(2,1)S(1)}, u32[]{:S(2)}, u32[]{:S(2)}) collective-permute-start(bf16[3,64,512]{2,1,0:T(8,128)(2,1)S(1)} %fusion.20), channel_id=1, source_target_pairs={{0,7},{1,0},{2,1},{3,2},{4,3},{5,4},{6,5},{7,6},{8,15},{9,8},{10,9... | collective-permute-start | bytes 589832 | tf_op jit(solution)/shard_map/ppermute | solution.py:54
  68.7 6.0 %collective-permute-start.20 = (bf16[3,64,512]{2,1,0:T(8,128)(2,1)S(1)}, bf16[3,64,512]{2,1,0:T(8,128)(2,1)S(1)}, u32[]{:S(2)}, u32[]{:S(2)}) collective-permute-start(bf16[3,64,512]{2,1,0:T(8,128)(2,1)S(1)} %fusion.17), channel_id=1, source_target_pairs={{0,1},{1,2},{2,3},{3,4},{4,5},{5,6},{6,7},{7,0},{8,9},{9,10},{10,1... | collective-permute-start | bytes 589832 | tf_op jit(solution)/shard_map/ppermute | solution.py:52
  68.8 6.6 %collective-permute-start.17 = (bf16[3,64,384]{2,1,0:T(8,128)(2,1)S(1)}, bf16[3,64,384]{2,1,0:T(8,128)(2,1)S(1)}, u32[]{:S(2)}, u32[]{:S(2)}) collective-permute-start(bf16[3,64,384]{2,1,0:T(8,128)(2,1)S(1)} %fusion.25), channel_id=1, source_target_pairs={{0,7},{1,0},{2,1},{3,2},{4,3},{5,4},{6,5},{7,6},{8,15},{9,8},{10,9... | collective-permute-start | bytes 442376 | tf_op jit(solution)/shard_map/ppermute | solution.py:54
  71.8 11.4 %collective-permute-start.14 = (bf16[3,64,384]{2,1,0:T(8,128)(2,1)S(1)}, bf16[3,64,384]{2,1,0:T(8,128)(2,1)S(1)}, u32[]{:S(2)}, u32[]{:S(2)}) collective-permute-start(bf16[3,64,384]{2,1,0:T(8,128)(2,1)S(1)} %fusion.23), channel_id=1, source_target_pairs={{0,1},{1,2},{2,3},{3,4},{4,5},{5,6},{6,7},{7,0},{8,9},{9,10},{10,1... | collective-permute-start | bytes 442376 | tf_op jit(solution)/shard_map/ppermute | solution.py:52
  72.0 11.3 %collective-permute-start.25 = (bf16[3,64,512]{2,1,0:T(8,128)(2,1)S(1)}, bf16[3,64,512]{2,1,0:T(8,128)(2,1)S(1)}, u32[]{:S(2)}, u32[]{:S(2)}) collective-permute-start(bf16[3,64,512]{2,1,0:T(8,128)(2,1)S(1)} %fusion.21), channel_id=1, source_target_pairs={{0,7},{1,0},{2,1},{3,2},{4,3},{5,4},{6,5},{7,6},{8,15},{9,8},{10,9... | collective-permute-start | bytes 589832 | tf_op jit(solution)/shard_map/ppermute | solution.py:54
  74.8 8.3 %collective-permute-start.21 = (bf16[3,64,512]{2,1,0:T(8,128)(2,1)S(1)}, bf16[3,64,512]{2,1,0:T(8,128)(2,1)S(1)}, u32[]{:S(2)}, u32[]{:S(2)}) collective-permute-start(bf16[3,64,512]{2,1,0:T(8,128)(2,1)S(1)} %fusion.18), channel_id=1, source_target_pairs={{0,1},{1,2},{2,3},{3,4},{4,5},{5,6},{6,7},{7,0},{8,9},{9,10},{10,1... | collective-permute-start | bytes 589832 | tf_op jit(solution)/shard_map/ppermute | solution.py:52
  75.5 7.8 %collective-permute-start.18 = (bf16[3,64,384]{2,1,0:T(8,128)(2,1)S(1)}, bf16[3,64,384]{2,1,0:T(8,128)(2,1)S(1)}, u32[]{:S(2)}, u32[]{:S(2)}) collective-permute-start(bf16[3,64,384]{2,1,0:T(8,128)(2,1)S(1)} %fusion.26), channel_id=1, source_target_pairs={{0,7},{1,0},{2,1},{3,2},{4,3},{5,4},{6,5},{7,6},{8,15},{9,8},{10,9... | collective-permute-start | bytes 442376 | tf_op jit(solution)/shard_map/ppermute | solution.py:54
  130.9 15.7 %all-to-all-start.1 = ((bf16[8,64,192]{2,1,0:T(8,128)(2,1)}), bf16[8,64,192]{2,1,0:T(8,128)(2,1)}, u32[]{:S(2)}, u32[]{:S(2)}) async-start(bf16[8,64,192]{2,1,0:T(8,128)(2,1)} %broadcast_in_dim.66), calls=%async_computation.1 | async-start | bytes 524288 | tf_op jit(solution)/shard_map/all_to_all | solution.py:263
  151.6 7.4 %collective-permute-start.26 = (bf16[256,2048]{1,0:T(8,128)(2,1)S(1)}, bf16[256,2048]{1,0:T(8,128)(2,1)S(1)}, u32[]{:S(2)}, u32[]{:S(2)}) collective-permute-start(bf16[256,2048]{1,0:T(8,128)(2,1)S(1)} %fusion.12), channel_id=1, source_target_pairs={{0,8},{8,0},{16,24},{24,16},{32,40},{40,32},{48,56},{56,48},{64,72... | collective-permute-start | bytes 3145736 | tf_op jit(solution)/shard_map/ppermute | solution.py:298
  161.3 22.4 %all-to-all-start.2 = ((bf16[16,16,2048]{2,1,0:T(8,128)(2,1)}), bf16[16,16,2048]{2,1,0:T(8,128)(2,1)}, u32[]{:S(2)}, u32[]{:S(2)}) async-start(bf16[16,16,2048]{2,1,0:T(8,128)(2,1)} %bitcast.170), calls=%async_computation.2 | async-start | bytes 2097152 | tf_op jit(solution)/shard_map/all_to_all | solution.py:300
  (22 other events, 162.9 us)
Sparse Core Ops, SparseCore 0:
  94.4 41.4 all-gather.1

commit v2 on v1

--- a/solution.py
+++ b/solution.py
@@ -243,27 +243,6 @@
     later_deltas = deltas_of(totals[:, :, :wide_size], low, later)
     earlier_deltas = deltas_of(second_totals, low, earlier)
 
-    own_factors = None
-    for (hidden, gate_delta, up_delta), columns in (
-        (later_deltas, later),
-        (earlier_deltas, earlier),
-    ):
-        term = jnp.concatenate(
-            [
-                matrix_multiply(hidden, down_adapter_first[columns]),
-                multiply_right_transposed(gate_delta, gate_adapter_second[:, columns]),
-                multiply_right_transposed(up_delta, up_adapter_second[:, columns]),
-            ],
-            axis=1,
-        )
-        own_factors = term if own_factors is None else own_factors + term
-
-    def to_all(value, axis):
-        count = lax.axis_size(axis)
-        return lax.all_to_all(
-            jnp.broadcast_to(value[None], (count,) + value.shape), axis, 0, 0, tiled=True
-        )
-
     packed = jnp.concatenate(
         [
             piece
@@ -273,11 +252,30 @@
         axis=1,
     )
     piece = lax.all_gather(packed, "col", axis=0, tiled=True)
-    factor_parts = to_all(own_factors.astype(jnp.bfloat16), "row")
+    packed_width = hidden_units + rank
+
+    def packed_part(which):
+        return packed[:, which * packed_width : which * packed_width + hidden_units]
+
+    own_factors = jnp.concatenate(
+        [
+            matrix_multiply(packed_part(2), down_adapter_first),
+            multiply_right_transposed(packed_part(0), gate_adapter_second),
+            multiply_right_transposed(packed_part(1), up_adapter_second),
+        ],
+        axis=1,
+    ).astype(jnp.bfloat16)
+
+    def to_all(value, axis, count, groups=None):
+        copies = jnp.broadcast_to(value[None], (count,) + value.shape)
+        return lax.all_to_all(copies, axis, 0, 0, axis_index_groups=groups, tiled=True)
+
+    other_factors = lax.ppermute(own_factors, "row", swap)
+    own_factors = own_factors.astype(jnp.float32) + other_factors.astype(jnp.float32)
+    factor_parts = to_all(own_factors.astype(jnp.bfloat16), "row", chips, same_core)
     own_factors = jnp.sum(factor_parts.astype(jnp.float32), axis=0).astype(jnp.bfloat16)
-    factors = to_all(own_factors, "col").reshape(tokens_all, 3 * rank)
+    factors = to_all(own_factors, "col", col_count).reshape(tokens_all, 3 * rank)
     piece, factors = lax.optimization_barrier((piece, factors))
-    packed_width = hidden_units + rank
     piece_gate, piece_up, piece_hidden = [
         piece[:, i * packed_width : i * packed_width + hidden_units] for i in range(3)
     ]
@@ -297,6 +295,7 @@
 
     other = lax.ppermute(input_part(1 - core).astype(jnp.bfloat16), "row", swap)
     share = (input_part(core) + other.astype(jnp.float32)).astype(jnp.bfloat16)
+    factors, share = lax.optimization_barrier((factors, share))
     shares = lax.all_to_all(share, "row", 0, 0, axis_index_groups=same_core, tiled=True)
     summed = jnp.sum(shares.reshape(chips, share_tokens, width).astype(jnp.float32), axis=0)
 

time: 194 us -> 195 us (level)
  waiting for transfers between devices: 52.4 us -> 43.9 us
  starting transfers between devices: 49.1 us -> 54.1 us
  blocking collectives: 28.3 us -> 32.6 us
    all_to_all x1 -> x0, waiting for transfers between devices: 10.6 us -> none  [to_all(): lax.all_to_all(jnp.broadcast_to(value[None], (count,) + value.shape), axi...]
    ppermute x0 -> x1, starting transfers between devices: none -> 5.67 us  [body(): other_factors = lax.ppermute(own_factors, 'row', swap)]
    all_to_all x1 -> x2, blocking collectives: 28.3 us -> 32.6 us  [to_all(): lax.all_to_all(copies, axis, 0, 0, axis_index_groups=groups, tiled=True)]
    all_to_all x1 -> x0, starting transfers between devices: 4.05 us -> none  [to_all(): lax.all_to_all(jnp.broadcast_to(value[None], (count,) + value.shape), axi...]
    all_gather x1, waiting for transfers between devices: 0.01 us -> 3.33 us  [body(): piece = lax.all_gather(packed, 'col', axis=0, tiled=True)]
    dot_general x5, matrix products: 6.91 us -> 9.13 us  [multiply_left_transposed(): lax.dot_general(left, right, (((0,), (0,)), ((), ())), preferred_element_...]
    all_to_all x1, waiting for transfers between devices: 13.9 us -> 11.8 us  [body(): lax.all_to_all(share, 'row', 0, 0, axis_index_groups=same_core, tiled=True)]
    dot_general x6 -> x5, matrix products: 4.19 us -> 3.33 us  [matrix_multiply(): return jnp.dot(left, right, preferred_element_type=jnp.float32)]
  transfers between devices with their start and end apart: 30 -> 30, of which waited for: 14 -> 15; matrix products, arithmetic and copies ran while one was open for 11% -> 10% of each run, Pallas kernels for 0% -> 0%
where the time goes in v2:
time: 195 us; the launch traced here: 194 us
  starting transfers between devices  54.1 us (28%)
  waiting for transfers between devices  43.9 us (23%)
  blocking collectives  32.6 us (17%)
  matrix products  32.5 us (17%)
  between operations  14.8 us (8%)
  local copies, waits for them, and re-layouts  12.7 us (7%)
  other arithmetic  3.86 us (2%)
    all_to_all x2, blocking collectives, to_all(): lax.all_to_all(copies, axis, 0, 0, axis_index_groups=groups, tiled=True)  32.6 us
    ppermute x7, starting transfers between devices, two_way_rings(): down = lax.ppermute(down, axis, shifted(size, -1))  22.8 us
    dot_general x13, matrix products, multiply_right_transposed(): lax.dot_general(left, right, (((1,), (1,)), ((), ())), preferred_element_...  20 us
    all_to_all x1, waiting for transfers between devices, body(): lax.all_to_all(share, 'row', 0, 0, axis_index_groups=same_core, tiled=True)  11.8 us
    ppermute x7, waiting for transfers between devices, two_way_rings(): up = lax.ppermute(up, axis, shifted(size, 1))  9.78 us
    dot_general x5, matrix products, multiply_left_transposed(): lax.dot_general(left, right, (((0,), (0,)), ((), ())), preferred_element_...  9.13 us
    ppermute x5, starting transfers between devices, to_other_core(): return lax.ppermute(value, 'row', swap)  8.88 us
    ppermute x1, waiting for transfers between devices, gather_tokens(): lax.ppermute(slab[half:], 'row', moves(0, -2))  8.45 us
  transfers between devices with their start and end apart: 30, of which 15 were waited for; matrix products, arithmetic and copies ran while one was open for 10% of the time, Pallas kernels for 0%

profile of v2, /device:TPU:1, one launch (start us, length us, event | category | flops | bytes accessed | tf_op | source)
XLA Modules:
  0.0 194.4 jit_solution(6903980422298519917)
XLA Ops:
  8.1 3.3 %collective-permute-start = (bf16[16,2048]{1,0:T(8,128)(2,1)S(1)}, bf16[16,2048]{1,0:T(8,128)(2,1)S(1)}, u32[]{:S(2)}, u32[]{:S(2)}) collective-permute-start(bf16[16,2048]{1,0:T(8,128)(2,1)S(1)} %broadcast_select_fusion.2), channel_id=1, source_target_pairs={{0,8},{8,0},{16,24},{24,16},{32,40},{40,32},{48,56},{56,48},{64,72... | collective-permute-start | bytes 196616 | tf_op jit(solution)/shard_map/ppermute | solution.py:105
  13.3 2.7 %collective-permute-start.2 = (bf16[32,2048]{1,0:T(8,128)(2,1)S(1)}, bf16[32,2048]{1,0:T(8,128)(2,1)S(1)}, u32[]{:S(2)}, u32[]{:S(2)}) collective-permute-start(bf16[32,2048]{1,0:T(8,128)(2,1)S(1)} %pad_maximum_fusion.4), channel_id=1, source_target_pairs={{0,192},{8,56},{16,208},{24,8},{32,224},{40,24},{48,240},{56,40},{... | collective-permute-start | bytes 393224 | tf_op jit(solution)/shard_map/ppermute | solution.py:115
  16.0 2.6 %collective-permute-done.1 = bf16[32,2048]{1,0:T(8,128)(2,1)S(1)} collective-permute-done((bf16[32,2048]{1,0:T(8,128)(2,1)S(1)}, bf16[32,2048]{1,0:T(8,128)(2,1)S(1)}, u32[]{:S(2)}, u32[]{:S(2)}) %collective-permute-start.1) | collective-permute-done | bytes 131104 | tf_op jit(solution)/shard_map/ppermute | solution.py:115
  24.9 2.7 %collective-permute-start.7 = (bf16[128,2048]{1,0:T(8,128)(2,1)S(1)}, bf16[128,2048]{1,0:T(8,128)(2,1)S(1)}, u32[]{:S(2)}, u32[]{:S(2)}) collective-permute-start(bf16[128,2048]{1,0:T(8,128)(2,1)S(1)} %bitcast.165), channel_id=1, source_target_pairs={{0,48},{8,200},{16,0},{24,216},{32,16},{40,232},{48,32},{56,248},{... | collective-permute-start | bytes 1572872 | tf_op jit(solution)/shard_map/ppermute | solution.py:123
  28.8 8.5 %collective-permute-done.10 = bf16[64,2048]{1,0:T(8,128)(2,1)S(1)} collective-permute-done((bf16[64,2048]{1,0:T(8,128)(2,1)S(1)}, bf16[64,2048]{1,0:T(8,128)(2,1)S(1)}, u32[]{:S(2)}, u32[]{:S(2)}) %collective-permute-start.10) | collective-permute-done | bytes 262176 | tf_op jit(solution)/shard_map/ppermute | solution.py:127
  37.2 2.7 %collective-permute-start.11 = (bf16[128,2048]{1,0:T(8,128)(2,1)S(1)}, bf16[128,2048]{1,0:T(8,128)(2,1)S(1)}, u32[]{:S(2)}, u32[]{:S(2)}) collective-permute-start(bf16[128,2048]{1,0:T(8,128)(2,1)S(1)} %constant_dynamic-update-slice_fusion.1), channel_id=1, source_target_pairs={{0,8},{8,0},{16,24},{24,16},{32,40},{40,32},{48,56},{56,48},{64,72... | collective-permute-start | bytes 1572872 | tf_op jit(solution)/shard_map/ppermute | solution.py:105
  54.2 4.0 %collective-permute-start.15 = (bf16[3,64,384]{2,1,0:T(8,128)(2,1)S(1)}, bf16[3,64,384]{2,1,0:T(8,128)(2,1)S(1)}, u32[]{:S(2)}, u32[]{:S(2)}) collective-permute-start(bf16[3,64,384]{2,1,0:T(8,128)(2,1)S(1)} %pad_maximum_fusion.3), channel_id=1, source_target_pairs={{0,7},{1,0},{2,1},{3,2},{4,3},{5,4},{6,5},{7,6},{8,15},{9,8},{10,9... | collective-permute-start | bytes 442376 | tf_op jit(solution)/shard_map/ppermute | solution.py:54
  58.3 2.7 %collective-permute-start.23 = (bf16[3,64,512]{2,1,0:T(8,128)(2,1)S(1)}, bf16[3,64,512]{2,1,0:T(8,128)(2,1)S(1)}, u32[]{:S(2)}, u32[]{:S(2)}) collective-permute-start(bf16[3,64,512]{2,1,0:T(8,128)(2,1)S(1)} %pad_maximum_fusion.1), channel_id=1, source_target_pairs={{0,7},{1,0},{2,1},{3,2},{4,3},{5,4},{6,5},{7,6},{8,15},{9,8},{10,9... | collective-permute-start | bytes 589832 | tf_op jit(solution)/shard_map/ppermute | solution.py:54
  61.3 3.2 %collective-permute-start.16 = (bf16[3,64,384]{2,1,0:T(8,128)(2,1)S(1)}, bf16[3,64,384]{2,1,0:T(8,128)(2,1)S(1)}, u32[]{:S(2)}, u32[]{:S(2)}) collective-permute-start(bf16[3,64,384]{2,1,0:T(8,128)(2,1)S(1)} %fusion.24), channel_id=1, source_target_pairs={{0,7},{1,0},{2,1},{3,2},{4,3},{5,4},{6,5},{7,6},{8,15},{9,8},{10,9... | collective-permute-start | bytes 442376 | tf_op jit(solution)/shard_map/ppermute | solution.py:54
  64.9 3.7 %collective-permute-start.24 = (bf16[3,64,512]{2,1,0:T(8,128)(2,1)S(1)}, bf16[3,64,512]{2,1,0:T(8,128)(2,1)S(1)}, u32[]{:S(2)}, u32[]{:S(2)}) collective-permute-start(bf16[3,64,512]{2,1,0:T(8,128)(2,1)S(1)} %fusion.20), channel_id=1, source_target_pairs={{0,7},{1,0},{2,1},{3,2},{4,3},{5,4},{6,5},{7,6},{8,15},{9,8},{10,9... | collective-permute-start | bytes 589832 | tf_op jit(solution)/shard_map/ppermute | solution.py:54
  68.8 3.0 %collective-permute-start.17 = (bf16[3,64,384]{2,1,0:T(8,128)(2,1)S(1)}, bf16[3,64,384]{2,1,0:T(8,128)(2,1)S(1)}, u32[]{:S(2)}, u32[]{:S(2)}) collective-permute-start(bf16[3,64,384]{2,1,0:T(8,128)(2,1)S(1)} %fusion.25), channel_id=1, source_target_pairs={{0,7},{1,0},{2,1},{3,2},{4,3},{5,4},{6,5},{7,6},{8,15},{9,8},{10,9... | collective-permute-start | bytes 442376 | tf_op jit(solution)/shard_map/ppermute | solution.py:54
  72.0 2.7 %collective-permute-start.25 = (bf16[3,64,512]{2,1,0:T(8,128)(2,1)S(1)}, bf16[3,64,512]{2,1,0:T(8,128)(2,1)S(1)}, u32[]{:S(2)}, u32[]{:S(2)}) collective-permute-start(bf16[3,64,512]{2,1,0:T(8,128)(2,1)S(1)} %fusion.21), channel_id=1, source_target_pairs={{0,7},{1,0},{2,1},{3,2},{4,3},{5,4},{6,5},{7,6},{8,15},{9,8},{10,9... | collective-permute-start | bytes 589832 | tf_op jit(solution)/shard_map/ppermute | solution.py:54
  75.5 3.5 %collective-permute-start.18 = (bf16[3,64,384]{2,1,0:T(8,128)(2,1)S(1)}, bf16[3,64,384]{2,1,0:T(8,128)(2,1)S(1)}, u32[]{:S(2)}, u32[]{:S(2)}) collective-permute-start(bf16[3,64,384]{2,1,0:T(8,128)(2,1)S(1)} %fusion.26), channel_id=1, source_target_pairs={{0,7},{1,0},{2,1},{3,2},{4,3},{5,4},{6,5},{7,6},{8,15},{9,8},{10,9... | collective-permute-start | bytes 442376 | tf_op jit(solution)/shard_map/ppermute | solution.py:54
  79.0 4.1 %collective-permute-done.21 = bf16[3,64,512]{2,1,0:T(8,128)(2,1)S(1)} collective-permute-done((bf16[3,64,512]{2,1,0:T(8,128)(2,1)S(1)}, bf16[3,64,512]{2,1,0:T(8,128)(2,1)S(1)}, u32[]{:S(2)}, u32[]{:S(2)}) %collective-permute-start.21) | collective-permute-done | bytes 196640 | tf_op jit(solution)/shard_map/ppermute | solution.py:52
  83.3 5.6 %collective-permute-done.22 = bf16[3,64,512]{2,1,0:T(8,128)(2,1)S(1)} collective-permute-done((bf16[3,64,512]{2,1,0:T(8,128)(2,1)S(1)}, bf16[3,64,512]{2,1,0:T(8,128)(2,1)S(1)}, u32[]{:S(2)}, u32[]{:S(2)}) %collective-permute-start.22) | collective-permute-done | bytes 196640 | tf_op jit(solution)/shard_map/ppermute | solution.py:52
  97.6 5.7 %collective-permute-start.26 = (bf16[64,192]{1,0:T(8,128)(2,1)S(1)}, bf16[64,192]{1,0:T(8,128)(2,1)S(1)}, u32[]{:S(2)}, u32[]{:S(2)}) collective-permute-start(bf16[64,192]{1,0:T(8,128)(2,1)S(1)} %pad_maximum_fusion.5), channel_id=1, source_target_pairs={{0,8},{8,0},{16,24},{24,16},{32,40},{40,32},{48,56},{56,48},{64,72... | collective-permute-start | bytes 73736 | tf_op jit(solution)/shard_map/ppermute | solution.py:273
  104.3 15.8 %all_to_all.19 = bf16[16,64,192]{2,1,0:T(8,128)(2,1)} all-to-all(bf16[16,64,192]{2,1,0:T(8,128)(2,1)S(1)} %broadcast_in_dim.65), channel_id=1, replica_groups={{0,16,32,48,64,80,96,112,128,144,160,176,192,208,224,240},{8,24,40,56,7..., dimensions={0} | all-to-all | bytes 786432 | tf_op jit(solution)/shard_map/all_to_all | solution.py:271
  121.3 16.8 %all_to_all.20 = bf16[8,64,192]{2,1,0:T(8,128)(2,1)} all-to-all(bf16[8,64,192]{2,1,0:T(8,128)(2,1)S(1)} %broadcast_in_dim.66), channel_id=1, replica_groups=mesh['row'=32,'col'=8] {'col'}, dimensions={0} | all-to-all | bytes 393216 | tf_op jit(solution)/shard_map/all_to_all | solution.py:271
  138.1 3.3 %all-gather.2.cloned.1.call-done = bf16[512,2688]{1,0:T(8,128)(2,1)} async-done(((bf16[64,2688]{1,0:T(8,128)(2,1)}), bf16[512,2688]{1,0:T(8,128)(2,1)}) %all-gather.2.cloned.1.call-update) | async-done | bytes 2752528 | tf_op jit(solution)/shard_map/all_gather | solution.py:254
  148.3 3.1 %collective-permute-start.27 = (bf16[256,2048]{1,0:T(8,128)(2,1)}, bf16[256,2048]{1,0:T(8,128)(2,1)}, u32[]{:S(2)}, u32[]{:S(2)}) collective-permute-start(bf16[256,2048]{1,0:T(8,128)(2,1)} %fusion.12), channel_id=1, source_target_pairs={{0,8},{8,0},{16,24},{24,16},{32,40},{40,32},{48,56},{56,48},{64,72... | collective-permute-start | bytes 3145736 | tf_op jit(solution)/shard_map/ppermute | solution.py:296
  154.9 2.5 %convolution_multiply_fusion.1 = f32[64,832]{1,0:T(8,128)} fusion(bf16[512,2688]{1,0:T(8,128)(2,1)} %all-gather.2.cloned.1.call-done), kind=kOutput, calls=%fused_computation.22 | convolution fusion | flops 54579200 | bytes 1261568 | tf_op jit(solution)/shard_map/dot_general | solution.py:22
  159.6 3.6 %add_convert_fusion = bf16[256,2048]{1,0:T(8,128)(2,1)} fusion(bf16[256,2048]{1,0:T(8,128)(2,1)} %collective-permute-done.27, f32[256,2048]{1,0:T(8,128)S(1)} %fusion.85, bf16[256,832]{1,0:T(8,128)(2,1)S(1)} %bitcast.176, bf16[2048,832]{0,1:T(8,128)(2,1)S(1)} %copy-done.3), kind=kOutput, calls=%fused_computation.20 | convolution fusion | flops 874512384 | bytes 8028160 | tf_op jit(solution)/shard_map/dot_general | solution.py:16
  163.2 6.3 %all-to-all-start.2 = ((bf16[16,16,2048]{2,1,0:T(8,128)(2,1)}), bf16[16,16,2048]{2,1,0:T(8,128)(2,1)S(1)}, u32[]{:S(2)}, u32[]{:S(2)}) async-start(bf16[16,16,2048]{2,1,0:T(8,128)(2,1)} %bitcast.83), calls=%async_computation.2 | async-start | bytes 2097152 | tf_op jit(solution)/shard_map/all_to_all | solution.py:299
  174.8 11.8 %all-to-all-done.2 = bf16[16,16,2048]{2,1,0:T(8,128)(2,1)S(1)} async-done(((bf16[16,16,2048]{2,1,0:T(8,128)(2,1)}), bf16[16,16,2048]{2,1,0:T(8,128)(2,1)S(1)}, u32[]{:S(2)}, u32[]{:S(2)}) %all-to-all-start.2) | async-done | bytes 1048608 | tf_op jit(solution)/shard_map/all_to_all | solution.py:299
  (158 shorter events, 55.8 us)
Async XLA Ops:
  7.2 134.2 %all-gather.2.cloned.1.call-start = ((), (), s32[]{:S(2)}) async-start(), calls=%async_computation.3 | async-start | bytes 3096576 | tf_op jit(solution)/shard_map/all_gather | solution.py:254
  13.3 6.0 %collective-permute-start.2 = (bf16[32,2048]{1,0:T(8,128)(2,1)S(1)}, bf16[32,2048]{1,0:T(8,128)(2,1)S(1)}, u32[]{:S(2)}, u32[]{:S(2)}) collective-permute-start(bf16[32,2048]{1,0:T(8,128)(2,1)S(1)} %pad_maximum_fusion.4), channel_id=1, source_target_pairs={{0,192},{8,56},{16,208},{24,8},{32,224},{40,24},{48,240},{56,40},{... | collective-permute-start | bytes 393224 | tf_op jit(solution)/shard_map/ppermute | solution.py:115
  21.6 7.1 %collective-permute-start.9 = (bf16[64,2048]{1,0:T(8,128)(2,1)S(1)}, bf16[64,2048]{1,0:T(8,128)(2,1)S(1)}, u32[]{:S(2)}, u32[]{:S(2)}) collective-permute-start(bf16[64,2048]{1,0:T(8,128)(2,1)S(1)} %bitcast.217), channel_id=1, source_target_pairs={{0,32},{8,136},{16,48},{24,152},{32,0},{40,168},{48,16},{56,184},{... | collective-permute-start | bytes 786440 | tf_op jit(solution)/shard_map/ppermute | solution.py:126
  22.6 17.9 %collective-permute-start.4 = (bf16[128,2048]{1,0:T(8,128)(2,1)S(1)}, bf16[128,2048]{1,0:T(8,128)(2,1)S(1)}, u32[]{:S(2)}, u32[]{:S(2)}) collective-permute-start(bf16[128,2048]{1,0:T(8,128)(2,1)S(1)} %bitcast.163), channel_id=1, source_target_pairs={{0,8},{8,0},{16,24},{24,16},{32,40},{40,32},{48,56},{56,48},{64,72... | collective-permute-start | bytes 1572872 | tf_op jit(solution)/shard_map/ppermute | solution.py:105
  24.9 15.0 %collective-permute-start.5 = (bf16[128,2048]{1,0:T(8,128)(2,1)S(1)}, bf16[128,2048]{1,0:T(8,128)(2,1)S(1)}, u32[]{:S(2)}, u32[]{:S(2)}) collective-permute-start(bf16[128,2048]{1,0:T(8,128)(2,1)S(1)} %bitcast.164), channel_id=1, source_target_pairs={{0,16},{8,72},{16,32},{24,88},{32,48},{40,104},{48,0},{56,120},{64... | collective-permute-start | bytes 1572872 | tf_op jit(solution)/shard_map/ppermute | solution.py:122
  24.9 15.1 %collective-permute-start.7 = (bf16[128,2048]{1,0:T(8,128)(2,1)S(1)}, bf16[128,2048]{1,0:T(8,128)(2,1)S(1)}, u32[]{:S(2)}, u32[]{:S(2)}) collective-permute-start(bf16[128,2048]{1,0:T(8,128)(2,1)S(1)} %bitcast.165), channel_id=1, source_target_pairs={{0,48},{8,200},{16,0},{24,216},{32,16},{40,232},{48,32},{56,248},{... | collective-permute-start | bytes 1572872 | tf_op jit(solution)/shard_map/ppermute | solution.py:123
  27.6 9.6 %collective-permute-start.10 = (bf16[64,2048]{1,0:T(8,128)(2,1)S(1)}, bf16[64,2048]{1,0:T(8,128)(2,1)S(1)}, u32[]{:S(2)}, u32[]{:S(2)}) collective-permute-start(bf16[64,2048]{1,0:T(8,128)(2,1)S(1)} %bitcast.216), channel_id=1, source_target_pairs={{0,32},{8,136},{16,48},{24,152},{32,0},{40,168},{48,16},{56,184},{... | collective-permute-start | bytes 786440 | tf_op jit(solution)/shard_map/ppermute | solution.py:127
  37.2 5.9 %collective-permute-start.11 = (bf16[128,2048]{1,0:T(8,128)(2,1)S(1)}, bf16[128,2048]{1,0:T(8,128)(2,1)S(1)}, u32[]{:S(2)}, u32[]{:S(2)}) collective-permute-start(bf16[128,2048]{1,0:T(8,128)(2,1)S(1)} %constant_dynamic-update-slice_fusion.1), channel_id=1, source_target_pairs={{0,8},{8,0},{16,24},{24,16},{32,40},{40,32},{48,56},{56,48},{64,72... | collective-permute-start | bytes 1572872 | tf_op jit(solution)/shard_map/ppermute | solution.py:105
  54.2 7.1 %collective-permute-start.15 = (bf16[3,64,384]{2,1,0:T(8,128)(2,1)S(1)}, bf16[3,64,384]{2,1,0:T(8,128)(2,1)S(1)}, u32[]{:S(2)}, u32[]{:S(2)}) collective-permute-start(bf16[3,64,384]{2,1,0:T(8,128)(2,1)S(1)} %pad_maximum_fusion.3), channel_id=1, source_target_pairs={{0,7},{1,0},{2,1},{3,2},{4,3},{5,4},{6,5},{7,6},{8,15},{9,8},{10,9... | collective-permute-start | bytes 442376 | tf_op jit(solution)/shard_map/ppermute | solution.py:54
  58.2 6.4 %collective-permute-start.12 = (bf16[3,64,384]{2,1,0:T(8,128)(2,1)S(1)}, bf16[3,64,384]{2,1,0:T(8,128)(2,1)S(1)}, u32[]{:S(2)}, u32[]{:S(2)}) collective-permute-start(bf16[3,64,384]{2,1,0:T(8,128)(2,1)S(1)} %pad_maximum_fusion.2), channel_id=1, source_target_pairs={{0,1},{1,2},{2,3},{3,4},{4,5},{5,6},{6,7},{7,0},{8,9},{9,10},{10,1... | collective-permute-start | bytes 442376 | tf_op jit(solution)/shard_map/ppermute | solution.py:52
  58.3 6.5 %collective-permute-start.23 = (bf16[3,64,512]{2,1,0:T(8,128)(2,1)S(1)}, bf16[3,64,512]{2,1,0:T(8,128)(2,1)S(1)}, u32[]{:S(2)}, u32[]{:S(2)}) collective-permute-start(bf16[3,64,512]{2,1,0:T(8,128)(2,1)S(1)} %pad_maximum_fusion.1), channel_id=1, source_target_pairs={{0,7},{1,0},{2,1},{3,2},{4,3},{5,4},{6,5},{7,6},{8,15},{9,8},{10,9... | collective-permute-start | bytes 589832 | tf_op jit(solution)/shard_map/ppermute | solution.py:54
  61.1 7.5 %collective-permute-start.19 = (bf16[3,64,512]{2,1,0:T(8,128)(2,1)S(1)}, bf16[3,64,512]{2,1,0:T(8,128)(2,1)S(1)}, u32[]{:S(2)}, u32[]{:S(2)}) collective-permute-start(bf16[3,64,512]{2,1,0:T(8,128)(2,1)S(1)} %pad_maximum_fusion), channel_id=1, source_target_pairs={{0,1},{1,2},{2,3},{3,4},{4,5},{5,6},{6,7},{7,0},{8,9},{9,10},{10,1... | collective-permute-start | bytes 589832 | tf_op jit(solution)/shard_map/ppermute | solution.py:52
  61.3 7.4 %collective-permute-start.16 = (bf16[3,64,384]{2,1,0:T(8,128)(2,1)S(1)}, bf16[3,64,384]{2,1,0:T(8,128)(2,1)S(1)}, u32[]{:S(2)}, u32[]{:S(2)}) collective-permute-start(bf16[3,64,384]{2,1,0:T(8,128)(2,1)S(1)} %fusion.24), channel_id=1, source_target_pairs={{0,7},{1,0},{2,1},{3,2},{4,3},{5,4},{6,5},{7,6},{8,15},{9,8},{10,9... | collective-permute-start | bytes 442376 | tf_op jit(solution)/shard_map/ppermute | solution.py:54
  64.6 7.2 %collective-permute-start.13 = (bf16[3,64,384]{2,1,0:T(8,128)(2,1)S(1)}, bf16[3,64,384]{2,1,0:T(8,128)(2,1)S(1)}, u32[]{:S(2)}, u32[]{:S(2)}) collective-permute-start(bf16[3,64,384]{2,1,0:T(8,128)(2,1)S(1)} %fusion.22), channel_id=1, source_target_pairs={{0,1},{1,2},{2,3},{3,4},{4,5},{5,6},{6,7},{7,0},{8,9},{9,10},{10,1... | collective-permute-start | bytes 442376 | tf_op jit(solution)/shard_map/ppermute | solution.py:52
  64.9 7.0 %collective-permute-start.24 = (bf16[3,64,512]{2,1,0:T(8,128)(2,1)S(1)}, bf16[3,64,512]{2,1,0:T(8,128)(2,1)S(1)}, u32[]{:S(2)}, u32[]{:S(2)}) collective-permute-start(bf16[3,64,512]{2,1,0:T(8,128)(2,1)S(1)} %fusion.20), channel_id=1, source_target_pairs={{0,7},{1,0},{2,1},{3,2},{4,3},{5,4},{6,5},{7,6},{8,15},{9,8},{10,9... | collective-permute-start | bytes 589832 | tf_op jit(solution)/shard_map/ppermute | solution.py:54
  68.7 6.0 %collective-permute-start.20 = (bf16[3,64,512]{2,1,0:T(8,128)(2,1)S(1)}, bf16[3,64,512]{2,1,0:T(8,128)(2,1)S(1)}, u32[]{:S(2)}, u32[]{:S(2)}) collective-permute-start(bf16[3,64,512]{2,1,0:T(8,128)(2,1)S(1)} %fusion.17), channel_id=1, source_target_pairs={{0,1},{1,2},{2,3},{3,4},{4,5},{5,6},{6,7},{7,0},{8,9},{9,10},{10,1... | collective-permute-start | bytes 589832 | tf_op jit(solution)/shard_map/ppermute | solution.py:52
  68.8 6.6 %collective-permute-start.17 = (bf16[3,64,384]{2,1,0:T(8,128)(2,1)S(1)}, bf16[3,64,384]{2,1,0:T(8,128)(2,1)S(1)}, u32[]{:S(2)}, u32[]{:S(2)}) collective-permute-start(bf16[3,64,384]{2,1,0:T(8,128)(2,1)S(1)} %fusion.25), channel_id=1, source_target_pairs={{0,7},{1,0},{2,1},{3,2},{4,3},{5,4},{6,5},{7,6},{8,15},{9,8},{10,9... | collective-permute-start | bytes 442376 | tf_op jit(solution)/shard_map/ppermute | solution.py:54
  71.8 11.4 %collective-permute-start.14 = (bf16[3,64,384]{2,1,0:T(8,128)(2,1)S(1)}, bf16[3,64,384]{2,1,0:T(8,128)(2,1)S(1)}, u32[]{:S(2)}, u32[]{:S(2)}) collective-permute-start(bf16[3,64,384]{2,1,0:T(8,128)(2,1)S(1)} %fusion.23), channel_id=1, source_target_pairs={{0,1},{1,2},{2,3},{3,4},{4,5},{5,6},{6,7},{7,0},{8,9},{9,10},{10,1... | collective-permute-start | bytes 442376 | tf_op jit(solution)/shard_map/ppermute | solution.py:52
  72.0 11.3 %collective-permute-start.25 = (bf16[3,64,512]{2,1,0:T(8,128)(2,1)S(1)}, bf16[3,64,512]{2,1,0:T(8,128)(2,1)S(1)}, u32[]{:S(2)}, u32[]{:S(2)}) collective-permute-start(bf16[3,64,512]{2,1,0:T(8,128)(2,1)S(1)} %fusion.21), channel_id=1, source_target_pairs={{0,7},{1,0},{2,1},{3,2},{4,3},{5,4},{6,5},{7,6},{8,15},{9,8},{10,9... | collective-permute-start | bytes 589832 | tf_op jit(solution)/shard_map/ppermute | solution.py:54
  74.8 8.3 %collective-permute-start.21 = (bf16[3,64,512]{2,1,0:T(8,128)(2,1)S(1)}, bf16[3,64,512]{2,1,0:T(8,128)(2,1)S(1)}, u32[]{:S(2)}, u32[]{:S(2)}) collective-permute-start(bf16[3,64,512]{2,1,0:T(8,128)(2,1)S(1)} %fusion.18), channel_id=1, source_target_pairs={{0,1},{1,2},{2,3},{3,4},{4,5},{5,6},{6,7},{7,0},{8,9},{9,10},{10,1... | collective-permute-start | bytes 589832 | tf_op jit(solution)/shard_map/ppermute | solution.py:52
  75.5 7.8 %collective-permute-start.18 = (bf16[3,64,384]{2,1,0:T(8,128)(2,1)S(1)}, bf16[3,64,384]{2,1,0:T(8,128)(2,1)S(1)}, u32[]{:S(2)}, u32[]{:S(2)}) collective-permute-start(bf16[3,64,384]{2,1,0:T(8,128)(2,1)S(1)} %fusion.26), channel_id=1, source_target_pairs={{0,7},{1,0},{2,1},{3,2},{4,3},{5,4},{6,5},{7,6},{8,15},{9,8},{10,9... | collective-permute-start | bytes 442376 | tf_op jit(solution)/shard_map/ppermute | solution.py:54
  97.6 6.5 %collective-permute-start.26 = (bf16[64,192]{1,0:T(8,128)(2,1)S(1)}, bf16[64,192]{1,0:T(8,128)(2,1)S(1)}, u32[]{:S(2)}, u32[]{:S(2)}) collective-permute-start(bf16[64,192]{1,0:T(8,128)(2,1)S(1)} %pad_maximum_fusion.5), channel_id=1, source_target_pairs={{0,8},{8,0},{16,24},{24,16},{32,40},{40,32},{48,56},{56,48},{64,72... | collective-permute-start | bytes 73736 | tf_op jit(solution)/shard_map/ppermute | solution.py:273
  148.3 11.3 %collective-permute-start.27 = (bf16[256,2048]{1,0:T(8,128)(2,1)}, bf16[256,2048]{1,0:T(8,128)(2,1)}, u32[]{:S(2)}, u32[]{:S(2)}) collective-permute-start(bf16[256,2048]{1,0:T(8,128)(2,1)} %fusion.12), channel_id=1, source_target_pairs={{0,8},{8,0},{16,24},{24,16},{32,40},{40,32},{48,56},{56,48},{64,72... | collective-permute-start | bytes 3145736 | tf_op jit(solution)/shard_map/ppermute | solution.py:296
  163.2 23.3 %all-to-all-start.2 = ((bf16[16,16,2048]{2,1,0:T(8,128)(2,1)}), bf16[16,16,2048]{2,1,0:T(8,128)(2,1)S(1)}, u32[]{:S(2)}, u32[]{:S(2)}) async-start(bf16[16,16,2048]{2,1,0:T(8,128)(2,1)} %bitcast.83), calls=%async_computation.2 | async-start | bytes 2097152 | tf_op jit(solution)/shard_map/all_to_all | solution.py:299
  (23 other events, 171.4 us)
Sparse Core Ops, SparseCore 0:
  94.4 46.9 all-gather.1

commit v3 on v2

--- a/solution.py
+++ b/solution.py
@@ -42,40 +42,32 @@
     return [(i, (i + step) % size) for i in range(size)]
 
 
-def two_way_rings(axis, operands, up_steps, arrive):
-    size = lax.axis_size(axis)
-    state = list(operands)
-    for step in range(1, size // 2 + 1):
-        for stream, steps in enumerate(up_steps):
-            up, down = state[stream]
-            if step <= steps:
-                up = lax.ppermute(up, axis, shifted(size, 1))
-            if step <= size - 1 - steps:
-                down = lax.ppermute(down, axis, shifted(size, -1))
-            state[stream] = arrive(stream, step, up, down)
-    return state
-
-
-def ring_sums(block_ofs, axis, up_steps, operands):
+def ring_sums(block_ofs, axis, ways):
     size = lax.axis_size(axis)
     here = lax.axis_index(axis)
+    far = size // 2
 
     def block(stream, offset):
-        return block_ofs[stream](lax.rem(here + offset + size, size))
-
-    def arrive(stream, step, up, down):
-        ups = up_steps[stream]
-        downs = size - 1 - ups
-        if step < ups:
-            up = (up.astype(jnp.float32) + block(stream, ups - step)).astype(jnp.bfloat16)
-        if step < downs:
-            down = (down.astype(jnp.float32) + block(stream, step - downs)).astype(jnp.bfloat16)
-        return up, down
-
-    return [
-        up.astype(jnp.float32) + down.astype(jnp.float32) + block(stream, 0)
-        for stream, (up, down) in enumerate(two_way_rings(axis, operands, up_steps, arrive))
-    ]
+        return block_ofs[stream](lax.rem(here + offset * ways[stream] + size, size))
+
+    def send(stream, value, step):
+        return lax.ppermute(
+            value.astype(jnp.bfloat16), axis, shifted(size, step * ways[stream])
+        ).astype(jnp.float32)
+
+    streams = range(len(ways))
+    ahead = []
+    behind = []
+    for stream in streams:
+        ahead.append(
+            send(stream, block(stream, far), 2) + send(stream, block(stream, far - 1), 1)
+        )
+        behind.append(send(stream, block(stream, 1 - far), -1))
+    for offset in range(far - 2, 0, -1):
+        for stream in streams:
+            ahead[stream] = send(stream, ahead[stream] + block(stream, offset), 1)
+            behind[stream] = send(stream, behind[stream] + block(stream, -offset), -1)
+    return [ahead[stream] + behind[stream] + block(stream, 0) for stream in streams]
 
 
 def gather_tokens(activations, output_gradient):
@@ -197,13 +189,6 @@
 
         return block_of
 
-    def first_operands(block_of, ups):
-        here = lax.axis_index("col")
-        return tuple(
-            block_of(lax.rem(here + offset + col_count, col_count)).astype(jnp.bfloat16)
-            for offset in (ups, ups + 1 - col_count)
-        )
-
     def deltas_of(totals, low, columns):
         gate_activation = totals[0] + adapter_scale * matrix_multiply(
             low[0], gate_adapter_second[:, columns]
@@ -231,13 +216,8 @@
     )
     later = slice(cut, hidden_units)
     earlier = slice(0, cut)
-    up_steps = (col_count // 2, col_count - 1 - col_count // 2)
-    block_ofs = (blocks_of(cut, wide_size + rank), blocks_of(0, cut))
     totals, second_totals = ring_sums(
-        block_ofs,
-        "col",
-        up_steps,
-        [first_operands(block_of, ups) for block_of, ups in zip(block_ofs, up_steps)],
+        (blocks_of(cut, wide_size + rank), blocks_of(0, cut)), "col", (1, -1)
     )
     low = totals[:, :, wide_size:].astype(jnp.bfloat16)
     later_deltas = deltas_of(totals[:, :, :wide_size], low, later)
@@ -295,7 +275,6 @@
 
     other = lax.ppermute(input_part(1 - core).astype(jnp.bfloat16), "row", swap)
     share = (input_part(core) + other.astype(jnp.float32)).astype(jnp.bfloat16)
-    factors, share = lax.optimization_barrier((factors, share))
     shares = lax.all_to_all(share, "row", 0, 0, axis_index_groups=same_core, tiled=True)
     summed = jnp.sum(shares.reshape(chips, share_tokens, width).astype(jnp.float32), axis=0)
 

time: 195 us -> 193 us (0.990)
  waiting for transfers between devices: 43.9 us -> 64 us
  blocking collectives: 32.6 us -> 15.8 us
  matrix products: 32.5 us -> 28.4 us
  starting transfers between devices: 54.1 us -> 51.5 us
    all_to_all x2 -> x1, blocking collectives: 32.6 us -> 15.8 us  [to_all(): lax.all_to_all(copies, axis, 0, 0, axis_index_groups=groups, tiled=True)]
    all_to_all x0 -> x1, waiting for transfers between devices: none -> 12.5 us  [to_all(): lax.all_to_all(copies, axis, 0, 0, axis_index_groups=groups, tiled=True)]
    ppermute x14, waiting for transfers between devices: 10.5 us -> 18.1 us  [send(): lax.ppermute(value.astype(jnp.bfloat16), axis, shifted(size, step * ways[...]
    ppermute x14, starting transfers between devices: 23.4 us -> 17.8 us  [send(): lax.ppermute(value.astype(jnp.bfloat16), axis, shifted(size, step * ways[...]
    all_to_all x0 -> x1, starting transfers between devices: none -> 4.04 us  [to_all(): lax.all_to_all(copies, axis, 0, 0, axis_index_groups=groups, tiled=True)]
    dot_general x5, matrix products: 9.13 us -> 6.91 us  [multiply_left_transposed(): lax.dot_general(left, right, (((0,), (0,)), ((), ())), preferred_element_...]
  transfers between devices with their start and end apart: 30 -> 31, of which waited for: 15 -> 19; matrix products, arithmetic and copies ran while one was open for 10% -> 9% of each run, Pallas kernels for 0% -> 0%
where the time goes in v3:
time: 193 us; the launch traced here: 192 us
  waiting for transfers between devices  64 us (33%)
  starting transfers between devices  51.5 us (27%)
  matrix products  28.4 us (15%)
  blocking collectives  15.8 us (8%)
  between operations  14.8 us (8%)
  local copies, waits for them, and re-layouts  12.4 us (6%)
  other arithmetic  5.08 us (3%)
    dot_general x13, matrix products, multiply_right_transposed(): lax.dot_general(left, right, (((1,), (1,)), ((), ())), preferred_element_...  18.1 us
    ppermute x14, waiting for transfers between devices, send(): lax.ppermute(value.astype(jnp.bfloat16), axis, shifted(size, step * ways[...  18.1 us
    ppermute x14, starting transfers between devices, send(): lax.ppermute(value.astype(jnp.bfloat16), axis, shifted(size, step * ways[...  17.8 us
    all_to_all x1, blocking collectives, to_all(): lax.all_to_all(copies, axis, 0, 0, axis_index_groups=groups, tiled=True)  15.8 us
    all_to_all x1, waiting for transfers between devices, body(): lax.all_to_all(share, 'row', 0, 0, axis_index_groups=same_core, tiled=True)  13 us
    all_to_all x1, waiting for transfers between devices, to_all(): lax.all_to_all(copies, axis, 0, 0, axis_index_groups=groups, tiled=True)  12.5 us
    ppermute x5, starting transfers between devices, to_other_core(): return lax.ppermute(value, 'row', swap)  8.88 us
    ppermute x1, waiting for transfers between devices, gather_tokens(): lax.ppermute(slab[half:], 'row', moves(0, -2))  8.45 us
  transfers between devices with their start and end apart: 31, of which 19 were waited for; matrix products, arithmetic and copies ran while one was open for 9% of the time, Pallas kernels for 0%

profile of v3, /device:TPU:1, one launch (start us, length us, event | category | flops | bytes accessed | tf_op | source)
XLA Modules:
  0.0 191.8 jit_solution(4124301267350464849)
XLA Ops:
  8.1 3.3 %collective-permute-start = (bf16[16,2048]{1,0:T(8,128)(2,1)S(1)}, bf16[16,2048]{1,0:T(8,128)(2,1)S(1)}, u32[]{:S(2)}, u32[]{:S(2)}) collective-permute-start(bf16[16,2048]{1,0:T(8,128)(2,1)S(1)} %broadcast_select_fusion.2), channel_id=1, source_target_pairs={{0,8},{8,0},{16,24},{24,16},{32,40},{40,32},{48,56},{56,48},{64,72... | collective-permute-start | bytes 196616 | tf_op jit(solution)/shard_map/ppermute | solution.py:97
  13.3 2.7 %collective-permute-start.2 = (bf16[32,2048]{1,0:T(8,128)(2,1)S(1)}, bf16[32,2048]{1,0:T(8,128)(2,1)S(1)}, u32[]{:S(2)}, u32[]{:S(2)}) collective-permute-start(bf16[32,2048]{1,0:T(8,128)(2,1)S(1)} %pad_maximum_fusion.6), channel_id=1, source_target_pairs={{0,192},{8,56},{16,208},{24,8},{32,224},{40,24},{48,240},{56,40},{... | collective-permute-start | bytes 393224 | tf_op jit(solution)/shard_map/ppermute | solution.py:107
  16.0 2.6 %collective-permute-done.1 = bf16[32,2048]{1,0:T(8,128)(2,1)S(1)} collective-permute-done((bf16[32,2048]{1,0:T(8,128)(2,1)S(1)}, bf16[32,2048]{1,0:T(8,128)(2,1)S(1)}, u32[]{:S(2)}, u32[]{:S(2)}) %collective-permute-start.1) | collective-permute-done | bytes 131104 | tf_op jit(solution)/shard_map/ppermute | solution.py:107
  22.6 2.4 %collective-permute-start.4 = (bf16[128,2048]{1,0:T(8,128)(2,1)S(1)}, bf16[128,2048]{1,0:T(8,128)(2,1)S(1)}, u32[]{:S(2)}, u32[]{:S(2)}) collective-permute-start(bf16[128,2048]{1,0:T(8,128)(2,1)S(1)} %bitcast.163), channel_id=1, source_target_pairs={{0,8},{8,0},{16,24},{24,16},{32,40},{40,32},{48,56},{56,48},{64,72... | collective-permute-start | bytes 1572872 | tf_op jit(solution)/shard_map/ppermute | solution.py:97
  24.9 2.7 %collective-permute-start.7 = (bf16[128,2048]{1,0:T(8,128)(2,1)S(1)}, bf16[128,2048]{1,0:T(8,128)(2,1)S(1)}, u32[]{:S(2)}, u32[]{:S(2)}) collective-permute-start(bf16[128,2048]{1,0:T(8,128)(2,1)S(1)} %bitcast.165), channel_id=1, source_target_pairs={{0,48},{8,200},{16,0},{24,216},{32,16},{40,232},{48,32},{56,248},{... | collective-permute-start | bytes 1572872 | tf_op jit(solution)/shard_map/ppermute | solution.py:115
  28.8 8.5 %collective-permute-done.10 = bf16[64,2048]{1,0:T(8,128)(2,1)S(1)} collective-permute-done((bf16[64,2048]{1,0:T(8,128)(2,1)S(1)}, bf16[64,2048]{1,0:T(8,128)(2,1)S(1)}, u32[]{:S(2)}, u32[]{:S(2)}) %collective-permute-start.10) | collective-permute-done | bytes 262176 | tf_op jit(solution)/shard_map/ppermute | solution.py:119
  37.2 2.7 %collective-permute-start.11 = (bf16[128,2048]{1,0:T(8,128)(2,1)S(1)}, bf16[128,2048]{1,0:T(8,128)(2,1)S(1)}, u32[]{:S(2)}, u32[]{:S(2)}) collective-permute-start(bf16[128,2048]{1,0:T(8,128)(2,1)S(1)} %constant_dynamic-update-slice_fusion.1), channel_id=1, source_target_pairs={{0,8},{8,0},{16,24},{24,16},{32,40},{40,32},{48,56},{56,48},{64,72... | collective-permute-start | bytes 1572872 | tf_op jit(solution)/shard_map/ppermute | solution.py:97
  46.3 2.4 %fusion = f32[512,896]{1,0:T(8,128)S(1)} fusion(bf16[512,2048]{1,0:T(8,128)(2,1)S(1)} %bitcast.172, bf16[2048,64]{0,1:T(8,128)(2,1)S(1)} %copy-done.9, bf16[2048,832]{0,1:T(8,128)(2,1)S(1)} %copy-done), kind=kOutput, calls=%fused_computation | convolution fusion | flops 1886388224 | bytes 7602176 | tf_op jit(solution)/shard_map/dot_general | solution.py:16
  48.7 2.4 %fusion.4 = f32[512,896]{1,0:T(8,128)S(1)} fusion(bf16[512,2048]{1,0:T(8,128)(2,1)S(1)} %bitcast.173, bf16[2048,64]{0,1:T(8,128)(2,1)S(1)} %copy-done.7, bf16[2048,832]{0,1:T(8,128)(2,1)S(1)} %copy-done.1), kind=kOutput, calls=%fused_computation.4 | convolution fusion | flops 1886388224 | bytes 7602176 | tf_op jit(solution)/shard_map/dot_general | solution.py:16
  51.1 2.4 %fusion.8 = f32[512,896]{1,0:T(8,128)S(1)} fusion(bf16[512,2048]{1,0:T(8,128)(2,1)S(1)} %bitcast.170, bf16[64,2048]{1,0:T(8,128)(2,1)S(1)} %copy-done.14, bf16[832,2048]{1,0:T(8,128)(2,1)S(1)} %copy-done.13), kind=kOutput, calls=%fused_computation.8 | convolution fusion | flops 1886388224 | bytes 7602176 | tf_op jit(solution)/shard_map/dot_general | solution.py:16
  54.3 4.0 %collective-permute-start.13 = (bf16[3,64,384]{2,1,0:T(8,128)(2,1)S(1)}, bf16[3,64,384]{2,1,0:T(8,128)(2,1)S(1)}, u32[]{:S(2)}, u32[]{:S(2)}) collective-permute-start(bf16[3,64,384]{2,1,0:T(8,128)(2,1)S(1)} %pad_maximum_fusion.4), channel_id=1, source_target_pairs={{0,7},{1,0},{2,1},{3,2},{4,3},{5,4},{6,5},{7,6},{8,15},{9,8},{10,9... | collective-permute-start | bytes 442376 | tf_op jit(solution)/shard_map/ppermute | solution.py:54
  63.8 3.5 %collective-permute-done.12 = bf16[3,64,384]{2,1,0:T(8,128)(2,1)S(1)} collective-permute-done((bf16[3,64,384]{2,1,0:T(8,128)(2,1)S(1)}, bf16[3,64,384]{2,1,0:T(8,128)(2,1)S(1)}, u32[]{:S(2)}, u32[]{:S(2)}) %collective-permute-start.12) | collective-permute-done | bytes 147488 | tf_op jit(solution)/shard_map/ppermute | solution.py:54
  67.3 2.7 %collective-permute-start.14 = (bf16[3,64,384]{2,1,0:T(8,128)(2,1)S(1)}, bf16[3,64,384]{2,1,0:T(8,128)(2,1)S(1)}, u32[]{:S(2)}, u32[]{:S(2)}) collective-permute-start(bf16[3,64,384]{2,1,0:T(8,128)(2,1)S(1)} %fusion.21), channel_id=1, source_target_pairs={{0,7},{1,0},{2,1},{3,2},{4,3},{5,4},{6,5},{7,6},{8,15},{9,8},{10,9... | collective-permute-start | bytes 442376 | tf_op jit(solution)/shard_map/ppermute | solution.py:54
  72.4 2.7 %collective-permute-start.24 = (bf16[3,64,512]{2,1,0:T(8,128)(2,1)S(1)}, bf16[3,64,512]{2,1,0:T(8,128)(2,1)S(1)}, u32[]{:S(2)}, u32[]{:S(2)}) collective-permute-start(bf16[3,64,512]{2,1,0:T(8,128)(2,1)S(1)} %fusion.19), channel_id=1, source_target_pairs={{0,7},{1,0},{2,1},{3,2},{4,3},{5,4},{6,5},{7,6},{8,15},{9,8},{10,9... | collective-permute-start | bytes 589832 | tf_op jit(solution)/shard_map/ppermute | solution.py:54
  75.4 2.9 %collective-permute-done.17 = bf16[3,64,384]{2,1,0:T(8,128)(2,1)S(1)} collective-permute-done((bf16[3,64,384]{2,1,0:T(8,128)(2,1)S(1)}, bf16[3,64,384]{2,1,0:T(8,128)(2,1)S(1)}, u32[]{:S(2)}, u32[]{:S(2)}) %collective-permute-start.17) | collective-permute-done | bytes 147488 | tf_op jit(solution)/shard_map/ppermute | solution.py:54
  78.4 2.7 %collective-permute-start.15 = (bf16[3,64,384]{2,1,0:T(8,128)(2,1)S(1)}, bf16[3,64,384]{2,1,0:T(8,128)(2,1)S(1)}, u32[]{:S(2)}, u32[]{:S(2)}) collective-permute-start(bf16[3,64,384]{2,1,0:T(8,128)(2,1)S(1)} %fusion.22), channel_id=1, source_target_pairs={{0,7},{1,0},{2,1},{3,2},{4,3},{5,4},{6,5},{7,6},{8,15},{9,8},{10,9... | collective-permute-start | bytes 442376 | tf_op jit(solution)/shard_map/ppermute | solution.py:54
  86.1 4.8 %collective-permute-done.22 = bf16[3,64,512]{2,1,0:T(8,128)(2,1)S(1)} collective-permute-done((bf16[3,64,512]{2,1,0:T(8,128)(2,1)S(1)}, bf16[3,64,512]{2,1,0:T(8,128)(2,1)S(1)}, u32[]{:S(2)}, u32[]{:S(2)}) %collective-permute-start.22) | collective-permute-done | bytes 196640 | tf_op jit(solution)/shard_map/ppermute | solution.py:54
  99.5 4.3 %collective-permute-start.26 = (bf16[64,192]{1,0:T(8,128)(2,1)S(1)}, bf16[64,192]{1,0:T(8,128)(2,1)S(1)}, u32[]{:S(2)}, u32[]{:S(2)}) collective-permute-start(bf16[64,192]{1,0:T(8,128)(2,1)S(1)} %pad_maximum_fusion.7), channel_id=1, source_target_pairs={{0,8},{8,0},{16,24},{24,16},{32,40},{40,32},{48,56},{56,48},{64,72... | collective-permute-start | bytes 73736 | tf_op jit(solution)/shard_map/ppermute | solution.py:253
  104.8 15.8 %all_to_all.19 = bf16[16,64,192]{2,1,0:T(8,128)(2,1)} all-to-all(bf16[16,64,192]{2,1,0:T(8,128)(2,1)S(1)} %broadcast_in_dim.65), channel_id=1, replica_groups={{0,16,32,48,64,80,96,112,128,144,160,176,192,208,224,240},{8,24,40,56,7..., dimensions={0} | all-to-all | bytes 786432 | tf_op jit(solution)/shard_map/all_to_all | solution.py:251
  122.5 4.0 %all-to-all-start.1 = ((bf16[8,64,192]{2,1,0:T(8,128)(2,1)}), bf16[8,64,192]{2,1,0:T(8,128)(2,1)}, u32[]{:S(2)}, u32[]{:S(2)}) async-start(bf16[8,64,192]{2,1,0:T(8,128)(2,1)} %broadcast_in_dim.66), calls=%async_computation.1 | async-start | bytes 524288 | tf_op jit(solution)/shard_map/all_to_all | solution.py:251
  127.6 12.5 %all-to-all-done.1 = bf16[8,64,192]{2,1,0:T(8,128)(2,1)} async-done(((bf16[8,64,192]{2,1,0:T(8,128)(2,1)}), bf16[8,64,192]{2,1,0:T(8,128)(2,1)}, u32[]{:S(2)}, u32[]{:S(2)}) %all-to-all-start.1) | async-done | bytes 196640 | tf_op jit(solution)/shard_map/all_to_all | solution.py:251
  147.3 2.6 %collective-permute-start.27 = (bf16[256,2048]{1,0:T(8,128)(2,1)S(1)}, bf16[256,2048]{1,0:T(8,128)(2,1)S(1)}, u32[]{:S(2)}, u32[]{:S(2)}) collective-permute-start(bf16[256,2048]{1,0:T(8,128)(2,1)S(1)} %fusion.12), channel_id=1, source_target_pairs={{0,8},{8,0},{16,24},{24,16},{32,40},{40,32},{48,56},{56,48},{64,72... | collective-permute-start | bytes 3145736 | tf_op jit(solution)/shard_map/ppermute | solution.py:276
  158.1 7.1 %all-to-all-start.2 = ((bf16[16,16,2048]{2,1,0:T(8,128)(2,1)}), bf16[16,16,2048]{2,1,0:T(8,128)(2,1)}, u32[]{:S(2)}, u32[]{:S(2)}) async-start(bf16[16,16,2048]{2,1,0:T(8,128)(2,1)} %bitcast.167), calls=%async_computation.2 | async-start | bytes 2097152 | tf_op jit(solution)/shard_map/all_to_all | solution.py:278
  169.1 13.0 %all-to-all-done.2 = bf16[16,16,2048]{2,1,0:T(8,128)(2,1)} async-done(((bf16[16,16,2048]{2,1,0:T(8,128)(2,1)}), bf16[16,16,2048]{2,1,0:T(8,128)(2,1)}, u32[]{:S(2)}, u32[]{:S(2)}) %all-to-all-start.2) | async-done | bytes 1048608 | tf_op jit(solution)/shard_map/all_to_all | solution.py:278
  (157 shorter events, 62.6 us)
Async XLA Ops:
  7.2 135.1 %all-gather.2.cloned.1.call-start = ((), (), s32[]{:S(2)}) async-start(), calls=%async_computation.3 | async-start | bytes 3096576 | tf_op jit(solution)/shard_map/all_gather | solution.py:234
  13.3 6.0 %collective-permute-start.2 = (bf16[32,2048]{1,0:T(8,128)(2,1)S(1)}, bf16[32,2048]{1,0:T(8,128)(2,1)S(1)}, u32[]{:S(2)}, u32[]{:S(2)}) collective-permute-start(bf16[32,2048]{1,0:T(8,128)(2,1)S(1)} %pad_maximum_fusion.6), channel_id=1, source_target_pairs={{0,192},{8,56},{16,208},{24,8},{32,224},{40,24},{48,240},{56,40},{... | collective-permute-start | bytes 393224 | tf_op jit(solution)/shard_map/ppermute | solution.py:107
  21.6 7.1 %collective-permute-start.9 = (bf16[64,2048]{1,0:T(8,128)(2,1)S(1)}, bf16[64,2048]{1,0:T(8,128)(2,1)S(1)}, u32[]{:S(2)}, u32[]{:S(2)}) collective-permute-start(bf16[64,2048]{1,0:T(8,128)(2,1)S(1)} %bitcast.210), channel_id=1, source_target_pairs={{0,32},{8,136},{16,48},{24,152},{32,0},{40,168},{48,16},{56,184},{... | collective-permute-start | bytes 786440 | tf_op jit(solution)/shard_map/ppermute | solution.py:118
  22.6 17.9 %collective-permute-start.4 = (bf16[128,2048]{1,0:T(8,128)(2,1)S(1)}, bf16[128,2048]{1,0:T(8,128)(2,1)S(1)}, u32[]{:S(2)}, u32[]{:S(2)}) collective-permute-start(bf16[128,2048]{1,0:T(8,128)(2,1)S(1)} %bitcast.163), channel_id=1, source_target_pairs={{0,8},{8,0},{16,24},{24,16},{32,40},{40,32},{48,56},{56,48},{64,72... | collective-permute-start | bytes 1572872 | tf_op jit(solution)/shard_map/ppermute | solution.py:97
  24.9 15.0 %collective-permute-start.5 = (bf16[128,2048]{1,0:T(8,128)(2,1)S(1)}, bf16[128,2048]{1,0:T(8,128)(2,1)S(1)}, u32[]{:S(2)}, u32[]{:S(2)}) collective-permute-start(bf16[128,2048]{1,0:T(8,128)(2,1)S(1)} %bitcast.164), channel_id=1, source_target_pairs={{0,16},{8,72},{16,32},{24,88},{32,48},{40,104},{48,0},{56,120},{64... | collective-permute-start | bytes 1572872 | tf_op jit(solution)/shard_map/ppermute | solution.py:114
  24.9 15.1 %collective-permute-start.7 = (bf16[128,2048]{1,0:T(8,128)(2,1)S(1)}, bf16[128,2048]{1,0:T(8,128)(2,1)S(1)}, u32[]{:S(2)}, u32[]{:S(2)}) collective-permute-start(bf16[128,2048]{1,0:T(8,128)(2,1)S(1)} %bitcast.165), channel_id=1, source_target_pairs={{0,48},{8,200},{16,0},{24,216},{32,16},{40,232},{48,32},{56,248},{... | collective-permute-start | bytes 1572872 | tf_op jit(solution)/shard_map/ppermute | solution.py:115
  27.6 9.6 %collective-permute-start.10 = (bf16[64,2048]{1,0:T(8,128)(2,1)S(1)}, bf16[64,2048]{1,0:T(8,128)(2,1)S(1)}, u32[]{:S(2)}, u32[]{:S(2)}) collective-permute-start(bf16[64,2048]{1,0:T(8,128)(2,1)S(1)} %bitcast.209), channel_id=1, source_target_pairs={{0,32},{8,136},{16,48},{24,152},{32,0},{40,168},{48,16},{56,184},{... | collective-permute-start | bytes 786440 | tf_op jit(solution)/shard_map/ppermute | solution.py:119
  37.2 5.9 %collective-permute-start.11 = (bf16[128,2048]{1,0:T(8,128)(2,1)S(1)}, bf16[128,2048]{1,0:T(8,128)(2,1)S(1)}, u32[]{:S(2)}, u32[]{:S(2)}) collective-permute-start(bf16[128,2048]{1,0:T(8,128)(2,1)S(1)} %constant_dynamic-update-slice_fusion.1), channel_id=1, source_target_pairs={{0,8},{8,0},{16,24},{24,16},{32,40},{40,32},{48,56},{56,48},{64,72... | collective-permute-start | bytes 1572872 | tf_op jit(solution)/shard_map/ppermute | solution.py:97
  54.1 7.9 %collective-permute-start.16 = (bf16[3,64,384]{2,1,0:T(8,128)(2,1)S(1)}, bf16[3,64,384]{2,1,0:T(8,128)(2,1)S(1)}, u32[]{:S(2)}, u32[]{:S(2)}) collective-permute-start(bf16[3,64,384]{2,1,0:T(8,128)(2,1)S(1)} %pad_maximum_fusion.5), channel_id=1, source_target_pairs={{0,1},{1,2},{2,3},{3,4},{4,5},{5,6},{6,7},{7,0},{8,9},{9,10},{10,1... | collective-permute-start | bytes 442376 | tf_op jit(solution)/shard_map/ppermute | solution.py:54
  54.3 8.4 %collective-permute-start.13 = (bf16[3,64,384]{2,1,0:T(8,128)(2,1)S(1)}, bf16[3,64,384]{2,1,0:T(8,128)(2,1)S(1)}, u32[]{:S(2)}, u32[]{:S(2)}) collective-permute-start(bf16[3,64,384]{2,1,0:T(8,128)(2,1)S(1)} %pad_maximum_fusion.4), channel_id=1, source_target_pairs={{0,7},{1,0},{2,1},{3,2},{4,3},{5,4},{6,5},{7,6},{8,15},{9,8},{10,9... | collective-permute-start | bytes 442376 | tf_op jit(solution)/shard_map/ppermute | solution.py:54
  58.3 9.0 %collective-permute-start.12 = (bf16[3,64,384]{2,1,0:T(8,128)(2,1)S(1)}, bf16[3,64,384]{2,1,0:T(8,128)(2,1)S(1)}, u32[]{:S(2)}, u32[]{:S(2)}) collective-permute-start(bf16[3,64,384]{2,1,0:T(8,128)(2,1)S(1)} %pad_maximum_fusion.3), channel_id=1, source_target_pairs={{0,6},{1,7},{2,0},{3,1},{4,2},{5,3},{6,4},{7,5},{8,14},{9,15},{10,... | collective-permute-start | bytes 442376 | tf_op jit(solution)/shard_map/ppermute | solution.py:54
  60.3 12.1 %collective-permute-start.23 = (bf16[3,64,512]{2,1,0:T(8,128)(2,1)S(1)}, bf16[3,64,512]{2,1,0:T(8,128)(2,1)S(1)}, u32[]{:S(2)}, u32[]{:S(2)}) collective-permute-start(bf16[3,64,512]{2,1,0:T(8,128)(2,1)S(1)} %pad_maximum_fusion.2), channel_id=1, source_target_pairs={{0,7},{1,0},{2,1},{3,2},{4,3},{5,4},{6,5},{7,6},{8,15},{9,8},{10,9... | collective-permute-start | bytes 589832 | tf_op jit(solution)/shard_map/ppermute | solution.py:54
  61.1 14.0 %collective-permute-start.20 = (bf16[3,64,512]{2,1,0:T(8,128)(2,1)S(1)}, bf16[3,64,512]{2,1,0:T(8,128)(2,1)S(1)}, u32[]{:S(2)}, u32[]{:S(2)}) collective-permute-start(bf16[3,64,512]{2,1,0:T(8,128)(2,1)S(1)} %pad_maximum_fusion.1), channel_id=1, source_target_pairs={{0,1},{1,2},{2,3},{3,4},{4,5},{5,6},{6,7},{7,0},{8,9},{9,10},{10,1... | collective-permute-start | bytes 589832 | tf_op jit(solution)/shard_map/ppermute | solution.py:54
  62.1 13.1 %collective-permute-start.19 = (bf16[3,64,512]{2,1,0:T(8,128)(2,1)S(1)}, bf16[3,64,512]{2,1,0:T(8,128)(2,1)S(1)}, u32[]{:S(2)}, u32[]{:S(2)}) collective-permute-start(bf16[3,64,512]{2,1,0:T(8,128)(2,1)S(1)} %pad_maximum_fusion), channel_id=1, source_target_pairs={{0,2},{1,3},{2,4},{3,5},{4,6},{5,7},{6,0},{7,1},{8,10},{9,11},{10,... | collective-permute-start | bytes 589832 | tf_op jit(solution)/shard_map/ppermute | solution.py:54
  62.7 15.5 %collective-permute-start.17 = (bf16[3,64,384]{2,1,0:T(8,128)(2,1)S(1)}, bf16[3,64,384]{2,1,0:T(8,128)(2,1)S(1)}, u32[]{:S(2)}, u32[]{:S(2)}) collective-permute-start(bf16[3,64,384]{2,1,0:T(8,128)(2,1)S(1)} %fusion.23), channel_id=1, source_target_pairs={{0,1},{1,2},{2,3},{3,4},{4,5},{5,6},{6,7},{7,0},{8,9},{9,10},{10,1... | collective-permute-start | bytes 442376 | tf_op jit(solution)/shard_map/ppermute | solution.py:54
  67.3 11.0 %collective-permute-start.14 = (bf16[3,64,384]{2,1,0:T(8,128)(2,1)S(1)}, bf16[3,64,384]{2,1,0:T(8,128)(2,1)S(1)}, u32[]{:S(2)}, u32[]{:S(2)}) collective-permute-start(bf16[3,64,384]{2,1,0:T(8,128)(2,1)S(1)} %fusion.21), channel_id=1, source_target_pairs={{0,7},{1,0},{2,1},{3,2},{4,3},{5,4},{6,5},{7,6},{8,15},{9,8},{10,9... | collective-permute-start | bytes 442376 | tf_op jit(solution)/shard_map/ppermute | solution.py:54
  72.4 8.7 %collective-permute-start.24 = (bf16[3,64,512]{2,1,0:T(8,128)(2,1)S(1)}, bf16[3,64,512]{2,1,0:T(8,128)(2,1)S(1)}, u32[]{:S(2)}, u32[]{:S(2)}) collective-permute-start(bf16[3,64,512]{2,1,0:T(8,128)(2,1)S(1)} %fusion.19), channel_id=1, source_target_pairs={{0,7},{1,0},{2,1},{3,2},{4,3},{5,4},{6,5},{7,6},{8,15},{9,8},{10,9... | collective-permute-start | bytes 589832 | tf_op jit(solution)/shard_map/ppermute | solution.py:54
  75.3 7.5 %collective-permute-start.21 = (bf16[3,64,512]{2,1,0:T(8,128)(2,1)S(1)}, bf16[3,64,512]{2,1,0:T(8,128)(2,1)S(1)}, u32[]{:S(2)}, u32[]{:S(2)}) collective-permute-start(bf16[3,64,512]{2,1,0:T(8,128)(2,1)S(1)} %fusion.17), channel_id=1, source_target_pairs={{0,1},{1,2},{2,3},{3,4},{4,5},{5,6},{6,7},{7,0},{8,9},{9,10},{10,1... | collective-permute-start | bytes 589832 | tf_op jit(solution)/shard_map/ppermute | solution.py:54
  78.3 6.1 %collective-permute-start.18 = (bf16[3,64,384]{2,1,0:T(8,128)(2,1)S(1)}, bf16[3,64,384]{2,1,0:T(8,128)(2,1)S(1)}, u32[]{:S(2)}, u32[]{:S(2)}) collective-permute-start(bf16[3,64,384]{2,1,0:T(8,128)(2,1)S(1)} %fusion.24), channel_id=1, source_target_pairs={{0,1},{1,2},{2,3},{3,4},{4,5},{5,6},{6,7},{7,0},{8,9},{9,10},{10,1... | collective-permute-start | bytes 442376 | tf_op jit(solution)/shard_map/ppermute | solution.py:54
  78.4 5.9 %collective-permute-start.15 = (bf16[3,64,384]{2,1,0:T(8,128)(2,1)S(1)}, bf16[3,64,384]{2,1,0:T(8,128)(2,1)S(1)}, u32[]{:S(2)}, u32[]{:S(2)}) collective-permute-start(bf16[3,64,384]{2,1,0:T(8,128)(2,1)S(1)} %fusion.22), channel_id=1, source_target_pairs={{0,7},{1,0},{2,1},{3,2},{4,3},{5,4},{6,5},{7,6},{8,15},{9,8},{10,9... | collective-permute-start | bytes 442376 | tf_op jit(solution)/shard_map/ppermute | solution.py:54
  82.8 8.1 %collective-permute-start.22 = (bf16[3,64,512]{2,1,0:T(8,128)(2,1)S(1)}, bf16[3,64,512]{2,1,0:T(8,128)(2,1)S(1)}, u32[]{:S(2)}, u32[]{:S(2)}) collective-permute-start(bf16[3,64,512]{2,1,0:T(8,128)(2,1)S(1)} %fusion.18), channel_id=1, source_target_pairs={{0,1},{1,2},{2,3},{3,4},{4,5},{5,6},{6,7},{7,0},{8,9},{9,10},{10,1... | collective-permute-start | bytes 589832 | tf_op jit(solution)/shard_map/ppermute | solution.py:54
  122.5 17.6 %all-to-all-start.1 = ((bf16[8,64,192]{2,1,0:T(8,128)(2,1)}), bf16[8,64,192]{2,1,0:T(8,128)(2,1)}, u32[]{:S(2)}, u32[]{:S(2)}) async-start(bf16[8,64,192]{2,1,0:T(8,128)(2,1)} %broadcast_in_dim.66), calls=%async_computation.1 | async-start | bytes 524288 | tf_op jit(solution)/shard_map/all_to_all | solution.py:251
  147.3 8.5 %collective-permute-start.27 = (bf16[256,2048]{1,0:T(8,128)(2,1)S(1)}, bf16[256,2048]{1,0:T(8,128)(2,1)S(1)}, u32[]{:S(2)}, u32[]{:S(2)}) collective-permute-start(bf16[256,2048]{1,0:T(8,128)(2,1)S(1)} %fusion.12), channel_id=1, source_target_pairs={{0,8},{8,0},{16,24},{24,16},{32,40},{40,32},{48,56},{56,48},{64,72... | collective-permute-start | bytes 3145736 | tf_op jit(solution)/shard_map/ppermute | solution.py:276
  158.1 24.0 %all-to-all-start.2 = ((bf16[16,16,2048]{2,1,0:T(8,128)(2,1)}), bf16[16,16,2048]{2,1,0:T(8,128)(2,1)}, u32[]{:S(2)}, u32[]{:S(2)}) async-start(bf16[16,16,2048]{2,1,0:T(8,128)(2,1)} %bitcast.167), calls=%async_computation.2 | async-start | bytes 2097152 | tf_op jit(solution)/shard_map/all_to_all | solution.py:278
  (23 other events, 169.9 us)
Sparse Core Ops, SparseCore 0:
  96.3 45.9 all-gather.1

commit v4 on v3

--- a/solution.py
+++ b/solution.py
@@ -256,11 +256,8 @@
     own_factors = jnp.sum(factor_parts.astype(jnp.float32), axis=0).astype(jnp.bfloat16)
     factors = to_all(own_factors, "col", col_count).reshape(tokens_all, 3 * rank)
     piece, factors = lax.optimization_barrier((piece, factors))
-    piece_gate, piece_up, piece_hidden = [
-        piece[:, i * packed_width : i * packed_width + hidden_units] for i in range(3)
-    ]
-    gate_low, up_low, down_low = [
-        piece[:, i * packed_width + hidden_units : (i + 1) * packed_width] for i in range(3)
+    piece_gate, piece_up = [
+        piece[:, i * packed_width : i * packed_width + hidden_units] for i in range(2)
     ]
 
     def input_part(which):
@@ -275,6 +272,7 @@
 
     other = lax.ppermute(input_part(1 - core).astype(jnp.bfloat16), "row", swap)
     share = (input_part(core) + other.astype(jnp.float32)).astype(jnp.bfloat16)
+    factors, piece, share = lax.optimization_barrier((factors, piece, share))
     shares = lax.all_to_all(share, "row", 0, 0, axis_index_groups=same_core, tiled=True)
     summed = jnp.sum(shares.reshape(chips, share_tokens, width).astype(jnp.float32), axis=0)
 
@@ -304,6 +302,12 @@
         factors[:, :rank], output_columns
     )
 
+    piece_gate, piece_up, piece_hidden = [
+        piece[:, i * packed_width : i * packed_width + hidden_units] for i in range(3)
+    ]
+    gate_low, up_low, down_low = [
+        piece[:, i * packed_width + hidden_units : (i + 1) * packed_width] for i in range(3)
+    ]
     gate_adapter_second_gradient = adapter_scale * multiply_left_transposed(gate_low, piece_gate)
     up_adapter_second_gradient = adapter_scale * multiply_left_transposed(up_low, piece_up)
     down_adapter_first_gradient = adapter_scale * multiply_left_transposed(piece_hidden, down_low)

time: 193 us -> 193 us (level)
  blocking collectives: 15.8 us -> 32.6 us
  waiting for transfers between devices: 64 us -> 49.5 us
  starting transfers between devices: 51.5 us -> 47.4 us
  matrix products: 28.4 us -> 30.6 us
    all_to_all x1 -> x2, blocking collectives: 15.8 us -> 32.6 us  [to_all(): lax.all_to_all(copies, axis, 0, 0, axis_index_groups=groups, tiled=True)]
    all_to_all x1 -> x0, waiting for transfers between devices: 12.5 us -> none  [to_all(): lax.all_to_all(copies, axis, 0, 0, axis_index_groups=groups, tiled=True)]
    all_to_all x1 -> x0, starting transfers between devices: 4.04 us -> none  [to_all(): lax.all_to_all(copies, axis, 0, 0, axis_index_groups=groups, tiled=True)]
    dot_general x13, matrix products: 18.1 us -> 22 us  [multiply_right_transposed(): lax.dot_general(left, right, (((1,), (1,)), ((), ())), preferred_element_...]
    all_to_all x1, waiting for transfers between devices: 13 us -> 9.88 us  [body(): lax.all_to_all(share, 'row', 0, 0, axis_index_groups=same_core, tiled=True)]
  transfers between devices with their start and end apart: 31 -> 30, of which waited for: 19 -> 18; matrix products, arithmetic and copies ran while one was open for 9% -> 9% of each run, Pallas kernels for 0% -> 0%
where the time goes in v4:
time: 193 us
  waiting for transfers between devices  49.5 us (26%)
  starting transfers between devices  47.4 us (25%)
  blocking collectives  32.6 us (17%)
  matrix products  30.6 us (16%)
  between operations  14.7 us (8%)
  local copies, waits for them, and re-layouts  12.8 us (7%)
  other arithmetic  5.08 us (3%)
    all_to_all x2, blocking collectives, to_all(): lax.all_to_all(copies, axis, 0, 0, axis_index_groups=groups, tiled=True)  32.6 us
    dot_general x13, matrix products, multiply_right_transposed(): lax.dot_general(left, right, (((1,), (1,)), ((), ())), preferred_element_...  22 us
    ppermute x14, waiting for transfers between devices, send(): lax.ppermute(value.astype(jnp.bfloat16), axis, shifted(size, step * ways[...  18.1 us
    ppermute x14, starting transfers between devices, send(): lax.ppermute(value.astype(jnp.bfloat16), axis, shifted(size, step * ways[...  17.8 us
    all_to_all x1, waiting for transfers between devices, body(): lax.all_to_all(share, 'row', 0, 0, axis_index_groups=same_core, tiled=True)  9.88 us
    ppermute x5, starting transfers between devices, to_other_core(): return lax.ppermute(value, 'row', swap)  8.88 us
    ppermute x1, waiting for transfers between devices, gather_tokens(): lax.ppermute(slab[half:], 'row', moves(0, -2))  8.45 us
    all_to_all x1, starting transfers between devices, body(): lax.all_to_all(share, 'row', 0, 0, axis_index_groups=same_core, tiled=True)  6.48 us
  transfers between devices with their start and end apart: 30, of which 18 were waited for; matrix products, arithmetic and copies ran while one was open for 9% of the time, Pallas kernels for 0%

profile of v4, /device:TPU:1, one launch (start us, length us, event | category | flops | bytes accessed | tf_op | source)
XLA Modules:
  0.0 192.7 jit_solution(17527534479626878278)
XLA Ops:
  8.1 3.3 %collective-permute-start = (bf16[16,2048]{1,0:T(8,128)(2,1)S(1)}, bf16[16,2048]{1,0:T(8,128)(2,1)S(1)}, u32[]{:S(2)}, u32[]{:S(2)}) collective-permute-start(bf16[16,2048]{1,0:T(8,128)(2,1)S(1)} %broadcast_select_fusion.2), channel_id=1, source_target_pairs={{0,8},{8,0},{16,24},{24,16},{32,40},{40,32},{48,56},{56,48},{64,72... | collective-permute-start | bytes 196616 | tf_op jit(solution)/shard_map/ppermute | solution.py:97
  13.3 2.7 %collective-permute-start.2 = (bf16[32,2048]{1,0:T(8,128)(2,1)S(1)}, bf16[32,2048]{1,0:T(8,128)(2,1)S(1)}, u32[]{:S(2)}, u32[]{:S(2)}) collective-permute-start(bf16[32,2048]{1,0:T(8,128)(2,1)S(1)} %pad_maximum_fusion.6), channel_id=1, source_target_pairs={{0,192},{8,56},{16,208},{24,8},{32,224},{40,24},{48,240},{56,40},{... | collective-permute-start | bytes 393224 | tf_op jit(solution)/shard_map/ppermute | solution.py:107
  16.0 2.6 %collective-permute-done.1 = bf16[32,2048]{1,0:T(8,128)(2,1)S(1)} collective-permute-done((bf16[32,2048]{1,0:T(8,128)(2,1)S(1)}, bf16[32,2048]{1,0:T(8,128)(2,1)S(1)}, u32[]{:S(2)}, u32[]{:S(2)}) %collective-permute-start.1) | collective-permute-done | bytes 131104 | tf_op jit(solution)/shard_map/ppermute | solution.py:107
  22.6 2.4 %collective-permute-start.4 = (bf16[128,2048]{1,0:T(8,128)(2,1)S(1)}, bf16[128,2048]{1,0:T(8,128)(2,1)S(1)}, u32[]{:S(2)}, u32[]{:S(2)}) collective-permute-start(bf16[128,2048]{1,0:T(8,128)(2,1)S(1)} %bitcast.163), channel_id=1, source_target_pairs={{0,8},{8,0},{16,24},{24,16},{32,40},{40,32},{48,56},{56,48},{64,72... | collective-permute-start | bytes 1572872 | tf_op jit(solution)/shard_map/ppermute | solution.py:97
  24.9 2.7 %collective-permute-start.7 = (bf16[128,2048]{1,0:T(8,128)(2,1)S(1)}, bf16[128,2048]{1,0:T(8,128)(2,1)S(1)}, u32[]{:S(2)}, u32[]{:S(2)}) collective-permute-start(bf16[128,2048]{1,0:T(8,128)(2,1)S(1)} %bitcast.165), channel_id=1, source_target_pairs={{0,48},{8,200},{16,0},{24,216},{32,16},{40,232},{48,32},{56,248},{... | collective-permute-start | bytes 1572872 | tf_op jit(solution)/shard_map/ppermute | solution.py:115
  28.8 8.5 %collective-permute-done.10 = bf16[64,2048]{1,0:T(8,128)(2,1)S(1)} collective-permute-done((bf16[64,2048]{1,0:T(8,128)(2,1)S(1)}, bf16[64,2048]{1,0:T(8,128)(2,1)S(1)}, u32[]{:S(2)}, u32[]{:S(2)}) %collective-permute-start.10) | collective-permute-done | bytes 262176 | tf_op jit(solution)/shard_map/ppermute | solution.py:119
  37.2 2.7 %collective-permute-start.11 = (bf16[128,2048]{1,0:T(8,128)(2,1)S(1)}, bf16[128,2048]{1,0:T(8,128)(2,1)S(1)}, u32[]{:S(2)}, u32[]{:S(2)}) collective-permute-start(bf16[128,2048]{1,0:T(8,128)(2,1)S(1)} %constant_dynamic-update-slice_fusion.1), channel_id=1, source_target_pairs={{0,8},{8,0},{16,24},{24,16},{32,40},{40,32},{48,56},{56,48},{64,72... | collective-permute-start | bytes 1572872 | tf_op jit(solution)/shard_map/ppermute | solution.py:97
  48.7 2.4 %fusion.4 = f32[512,896]{1,0:T(8,128)S(1)} fusion(bf16[512,2048]{1,0:T(8,128)(2,1)S(1)} %bitcast.173, bf16[2048,64]{0,1:T(8,128)(2,1)S(1)} %copy-done.9, bf16[2048,832]{0,1:T(8,128)(2,1)S(1)} %copy-done.1), kind=kOutput, calls=%fused_computation.4 | convolution fusion | flops 1886388224 | bytes 7602176 | tf_op jit(solution)/shard_map/dot_general | solution.py:16
  51.1 2.4 %fusion.8 = f32[512,896]{1,0:T(8,128)S(1)} fusion(bf16[512,2048]{1,0:T(8,128)(2,1)S(1)} %bitcast.170, bf16[64,2048]{1,0:T(8,128)(2,1)S(1)} %copy-done.14, bf16[832,2048]{1,0:T(8,128)(2,1)S(1)} %copy-done.13), kind=kOutput, calls=%fused_computation.8 | convolution fusion | flops 1886388224 | bytes 7602176 | tf_op jit(solution)/shard_map/dot_general | solution.py:16
  54.3 4.0 %collective-permute-start.13 = (bf16[3,64,384]{2,1,0:T(8,128)(2,1)S(1)}, bf16[3,64,384]{2,1,0:T(8,128)(2,1)S(1)}, u32[]{:S(2)}, u32[]{:S(2)}) collective-permute-start(bf16[3,64,384]{2,1,0:T(8,128)(2,1)S(1)} %pad_maximum_fusion.4), channel_id=1, source_target_pairs={{0,7},{1,0},{2,1},{3,2},{4,3},{5,4},{6,5},{7,6},{8,15},{9,8},{10,9... | collective-permute-start | bytes 442376 | tf_op jit(solution)/shard_map/ppermute | solution.py:54
  63.8 3.5 %collective-permute-done.12 = bf16[3,64,384]{2,1,0:T(8,128)(2,1)S(1)} collective-permute-done((bf16[3,64,384]{2,1,0:T(8,128)(2,1)S(1)}, bf16[3,64,384]{2,1,0:T(8,128)(2,1)S(1)}, u32[]{:S(2)}, u32[]{:S(2)}) %collective-permute-start.12) | collective-permute-done | bytes 147488 | tf_op jit(solution)/shard_map/ppermute | solution.py:54
  67.3 2.7 %collective-permute-start.14 = (bf16[3,64,384]{2,1,0:T(8,128)(2,1)S(1)}, bf16[3,64,384]{2,1,0:T(8,128)(2,1)S(1)}, u32[]{:S(2)}, u32[]{:S(2)}) collective-permute-start(bf16[3,64,384]{2,1,0:T(8,128)(2,1)S(1)} %fusion.23), channel_id=1, source_target_pairs={{0,7},{1,0},{2,1},{3,2},{4,3},{5,4},{6,5},{7,6},{8,15},{9,8},{10,9... | collective-permute-start | bytes 442376 | tf_op jit(solution)/shard_map/ppermute | solution.py:54
  72.4 2.7 %collective-permute-start.24 = (bf16[3,64,512]{2,1,0:T(8,128)(2,1)S(1)}, bf16[3,64,512]{2,1,0:T(8,128)(2,1)S(1)}, u32[]{:S(2)}, u32[]{:S(2)}) collective-permute-start(bf16[3,64,512]{2,1,0:T(8,128)(2,1)S(1)} %fusion.21), channel_id=1, source_target_pairs={{0,7},{1,0},{2,1},{3,2},{4,3},{5,4},{6,5},{7,6},{8,15},{9,8},{10,9... | collective-permute-start | bytes 589832 | tf_op jit(solution)/shard_map/ppermute | solution.py:54
  75.4 2.9 %collective-permute-done.17 = bf16[3,64,384]{2,1,0:T(8,128)(2,1)S(1)} collective-permute-done((bf16[3,64,384]{2,1,0:T(8,128)(2,1)S(1)}, bf16[3,64,384]{2,1,0:T(8,128)(2,1)S(1)}, u32[]{:S(2)}, u32[]{:S(2)}) %collective-permute-start.17) | collective-permute-done | bytes 147488 | tf_op jit(solution)/shard_map/ppermute | solution.py:54
  78.4 2.7 %collective-permute-start.15 = (bf16[3,64,384]{2,1,0:T(8,128)(2,1)S(1)}, bf16[3,64,384]{2,1,0:T(8,128)(2,1)S(1)}, u32[]{:S(2)}, u32[]{:S(2)}) collective-permute-start(bf16[3,64,384]{2,1,0:T(8,128)(2,1)S(1)} %fusion.24), channel_id=1, source_target_pairs={{0,7},{1,0},{2,1},{3,2},{4,3},{5,4},{6,5},{7,6},{8,15},{9,8},{10,9... | collective-permute-start | bytes 442376 | tf_op jit(solution)/shard_map/ppermute | solution.py:54
  86.1 4.8 %collective-permute-done.22 = bf16[3,64,512]{2,1,0:T(8,128)(2,1)S(1)} collective-permute-done((bf16[3,64,512]{2,1,0:T(8,128)(2,1)S(1)}, bf16[3,64,512]{2,1,0:T(8,128)(2,1)S(1)}, u32[]{:S(2)}, u32[]{:S(2)}) %collective-permute-start.22) | collective-permute-done | bytes 196640 | tf_op jit(solution)/shard_map/ppermute | solution.py:54
  99.6 4.3 %collective-permute-start.26 = (bf16[64,192]{1,0:T(8,128)(2,1)S(1)}, bf16[64,192]{1,0:T(8,128)(2,1)S(1)}, u32[]{:S(2)}, u32[]{:S(2)}) collective-permute-start(bf16[64,192]{1,0:T(8,128)(2,1)S(1)} %pad_maximum_fusion.7), channel_id=1, source_target_pairs={{0,8},{8,0},{16,24},{24,16},{32,40},{40,32},{48,56},{56,48},{64,72... | collective-permute-start | bytes 73736 | tf_op jit(solution)/shard_map/ppermute | solution.py:253
  104.9 15.8 %all_to_all.19 = bf16[16,64,192]{2,1,0:T(8,128)(2,1)} all-to-all(bf16[16,64,192]{2,1,0:T(8,128)(2,1)S(1)} %broadcast_in_dim.65), channel_id=1, replica_groups={{0,16,32,48,64,80,96,112,128,144,160,176,192,208,224,240},{8,24,40,56,7..., dimensions={0} | all-to-all | bytes 786432 | tf_op jit(solution)/shard_map/all_to_all | solution.py:251
  121.8 16.8 %all_to_all.20 = bf16[8,64,192]{2,1,0:T(8,128)(2,1)} all-to-all(bf16[8,64,192]{2,1,0:T(8,128)(2,1)S(1)} %broadcast_in_dim.66), channel_id=1, replica_groups=mesh['row'=32,'col'=8] {'col'}, dimensions={0} | all-to-all | bytes 393216 | tf_op jit(solution)/shard_map/all_to_all | solution.py:251
  138.6 3.3 %all-gather.2.cloned.1.call-done = bf16[512,2688]{1,0:T(8,128)(2,1)} async-done(((bf16[64,2688]{1,0:T(8,128)(2,1)}), bf16[512,2688]{1,0:T(8,128)(2,1)}) %all-gather.2.cloned.1.call-update) | async-done | bytes 2752528 | tf_op jit(solution)/shard_map/all_gather | solution.py:234
  148.9 3.2 %collective-permute-start.27 = (bf16[256,2048]{1,0:T(8,128)(2,1)}, bf16[256,2048]{1,0:T(8,128)(2,1)}, u32[]{:S(2)}, u32[]{:S(2)}) collective-permute-start(bf16[256,2048]{1,0:T(8,128)(2,1)} %fusion.12), channel_id=1, source_target_pairs={{0,8},{8,0},{16,24},{24,16},{32,40},{40,32},{48,56},{56,48},{64,72... | collective-permute-start | bytes 3145736 | tf_op jit(solution)/shard_map/ppermute | solution.py:273
  155.6 3.6 %add_convert_fusion = bf16[256,2048]{1,0:T(8,128)(2,1)} fusion(bf16[256,2048]{1,0:T(8,128)(2,1)} %collective-permute-done.27, f32[256,2048]{1,0:T(8,128)S(1)} %fusion.85, bf16[256,832]{1,0:T(8,128)(2,1)S(1)} %bitcast.177, bf16[2048,832]{0,1:T(8,128)(2,1)S(1)} %copy-done.3), kind=kOutput, calls=%fused_computation.20 | convolution fusion | flops 874512384 | bytes 8028160 | tf_op jit(solution)/shard_map/dot_general | solution.py:16
  159.2 6.5 %all-to-all-start.2 = ((bf16[16,16,2048]{2,1,0:T(8,128)(2,1)}), bf16[16,16,2048]{2,1,0:T(8,128)(2,1)}, u32[]{:S(2)}, u32[]{:S(2)}) async-start(bf16[16,16,2048]{2,1,0:T(8,128)(2,1)} %bitcast.167), calls=%async_computation.2 | async-start | bytes 2097152 | tf_op jit(solution)/shard_map/all_to_all | solution.py:276
  172.9 9.9 %all-to-all-done.2 = bf16[16,16,2048]{2,1,0:T(8,128)(2,1)} async-done(((bf16[16,16,2048]{2,1,0:T(8,128)(2,1)}), bf16[16,16,2048]{2,1,0:T(8,128)(2,1)}, u32[]{:S(2)}, u32[]{:S(2)}) %all-to-all-start.2) | async-done | bytes 1048608 | tf_op jit(solution)/shard_map/all_to_all | solution.py:276
  (156 shorter events, 61.8 us)
Async XLA Ops:
  7.2 134.8 %all-gather.2.cloned.1.call-start = ((), (), s32[]{:S(2)}) async-start(), calls=%async_computation.3 | async-start | bytes 3096576 | tf_op jit(solution)/shard_map/all_gather | solution.py:234
  13.3 6.0 %collective-permute-start.2 = (bf16[32,2048]{1,0:T(8,128)(2,1)S(1)}, bf16[32,2048]{1,0:T(8,128)(2,1)S(1)}, u32[]{:S(2)}, u32[]{:S(2)}) collective-permute-start(bf16[32,2048]{1,0:T(8,128)(2,1)S(1)} %pad_maximum_fusion.6), channel_id=1, source_target_pairs={{0,192},{8,56},{16,208},{24,8},{32,224},{40,24},{48,240},{56,40},{... | collective-permute-start | bytes 393224 | tf_op jit(solution)/shard_map/ppermute | solution.py:107
  15.9 5.6 %collective-permute-start.3 = (bf16[32,2048]{1,0:T(8,128)(2,1)S(1)}, bf16[32,2048]{1,0:T(8,128)(2,1)S(1)}, u32[]{:S(2)}, u32[]{:S(2)}) collective-permute-start(bf16[32,2048]{1,0:T(8,128)(2,1)S(1)} %pad_maximum_fusion.6), channel_id=1, source_target_pairs={{0,128},{8,40},{16,144},{24,56},{32,160},{40,8},{48,176},{56,24},{... | collective-permute-start | bytes 393224 | tf_op jit(solution)/shard_map/ppermute | solution.py:107
  21.6 7.1 %collective-permute-start.9 = (bf16[64,2048]{1,0:T(8,128)(2,1)S(1)}, bf16[64,2048]{1,0:T(8,128)(2,1)S(1)}, u32[]{:S(2)}, u32[]{:S(2)}) collective-permute-start(bf16[64,2048]{1,0:T(8,128)(2,1)S(1)} %bitcast.214), channel_id=1, source_target_pairs={{0,32},{8,136},{16,48},{24,152},{32,0},{40,168},{48,16},{56,184},{... | collective-permute-start | bytes 786440 | tf_op jit(solution)/shard_map/ppermute | solution.py:118
  22.6 17.9 %collective-permute-start.4 = (bf16[128,2048]{1,0:T(8,128)(2,1)S(1)}, bf16[128,2048]{1,0:T(8,128)(2,1)S(1)}, u32[]{:S(2)}, u32[]{:S(2)}) collective-permute-start(bf16[128,2048]{1,0:T(8,128)(2,1)S(1)} %bitcast.163), channel_id=1, source_target_pairs={{0,8},{8,0},{16,24},{24,16},{32,40},{40,32},{48,56},{56,48},{64,72... | collective-permute-start | bytes 1572872 | tf_op jit(solution)/shard_map/ppermute | solution.py:97
  24.9 15.0 %collective-permute-start.5 = (bf16[128,2048]{1,0:T(8,128)(2,1)S(1)}, bf16[128,2048]{1,0:T(8,128)(2,1)S(1)}, u32[]{:S(2)}, u32[]{:S(2)}) collective-permute-start(bf16[128,2048]{1,0:T(8,128)(2,1)S(1)} %bitcast.164), channel_id=1, source_target_pairs={{0,16},{8,72},{16,32},{24,88},{32,48},{40,104},{48,0},{56,120},{64... | collective-permute-start | bytes 1572872 | tf_op jit(solution)/shard_map/ppermute | solution.py:114
  24.9 15.1 %collective-permute-start.7 = (bf16[128,2048]{1,0:T(8,128)(2,1)S(1)}, bf16[128,2048]{1,0:T(8,128)(2,1)S(1)}, u32[]{:S(2)}, u32[]{:S(2)}) collective-permute-start(bf16[128,2048]{1,0:T(8,128)(2,1)S(1)} %bitcast.165), channel_id=1, source_target_pairs={{0,48},{8,200},{16,0},{24,216},{32,16},{40,232},{48,32},{56,248},{... | collective-permute-start | bytes 1572872 | tf_op jit(solution)/shard_map/ppermute | solution.py:115
  27.6 9.6 %collective-permute-start.10 = (bf16[64,2048]{1,0:T(8,128)(2,1)S(1)}, bf16[64,2048]{1,0:T(8,128)(2,1)S(1)}, u32[]{:S(2)}, u32[]{:S(2)}) collective-permute-start(bf16[64,2048]{1,0:T(8,128)(2,1)S(1)} %bitcast.213), channel_id=1, source_target_pairs={{0,32},{8,136},{16,48},{24,152},{32,0},{40,168},{48,16},{56,184},{... | collective-permute-start | bytes 786440 | tf_op jit(solution)/shard_map/ppermute | solution.py:119
  37.2 5.9 %collective-permute-start.11 = (bf16[128,2048]{1,0:T(8,128)(2,1)S(1)}, bf16[128,2048]{1,0:T(8,128)(2,1)S(1)}, u32[]{:S(2)}, u32[]{:S(2)}) collective-permute-start(bf16[128,2048]{1,0:T(8,128)(2,1)S(1)} %constant_dynamic-update-slice_fusion.1), channel_id=1, source_target_pairs={{0,8},{8,0},{16,24},{24,16},{32,40},{40,32},{48,56},{56,48},{64,72... | collective-permute-start | bytes 1572872 | tf_op jit(solution)/shard_map/ppermute | solution.py:97
  54.1 7.9 %collective-permute-start.16 = (bf16[3,64,384]{2,1,0:T(8,128)(2,1)S(1)}, bf16[3,64,384]{2,1,0:T(8,128)(2,1)S(1)}, u32[]{:S(2)}, u32[]{:S(2)}) collective-permute-start(bf16[3,64,384]{2,1,0:T(8,128)(2,1)S(1)} %pad_maximum_fusion.5), channel_id=1, source_target_pairs={{0,1},{1,2},{2,3},{3,4},{4,5},{5,6},{6,7},{7,0},{8,9},{9,10},{10,1... | collective-permute-start | bytes 442376 | tf_op jit(solution)/shard_map/ppermute | solution.py:54
  54.3 8.4 %collective-permute-start.13 = (bf16[3,64,384]{2,1,0:T(8,128)(2,1)S(1)}, bf16[3,64,384]{2,1,0:T(8,128)(2,1)S(1)}, u32[]{:S(2)}, u32[]{:S(2)}) collective-permute-start(bf16[3,64,384]{2,1,0:T(8,128)(2,1)S(1)} %pad_maximum_fusion.4), channel_id=1, source_target_pairs={{0,7},{1,0},{2,1},{3,2},{4,3},{5,4},{6,5},{7,6},{8,15},{9,8},{10,9... | collective-permute-start | bytes 442376 | tf_op jit(solution)/shard_map/ppermute | solution.py:54
  58.3 9.0 %collective-permute-start.12 = (bf16[3,64,384]{2,1,0:T(8,128)(2,1)S(1)}, bf16[3,64,384]{2,1,0:T(8,128)(2,1)S(1)}, u32[]{:S(2)}, u32[]{:S(2)}) collective-permute-start(bf16[3,64,384]{2,1,0:T(8,128)(2,1)S(1)} %pad_maximum_fusion.3), channel_id=1, source_target_pairs={{0,6},{1,7},{2,0},{3,1},{4,2},{5,3},{6,4},{7,5},{8,14},{9,15},{10,... | collective-permute-start | bytes 442376 | tf_op jit(solution)/shard_map/ppermute | solution.py:54
  60.3 12.1 %collective-permute-start.23 = (bf16[3,64,512]{2,1,0:T(8,128)(2,1)S(1)}, bf16[3,64,512]{2,1,0:T(8,128)(2,1)S(1)}, u32[]{:S(2)}, u32[]{:S(2)}) collective-permute-start(bf16[3,64,512]{2,1,0:T(8,128)(2,1)S(1)} %pad_maximum_fusion.2), channel_id=1, source_target_pairs={{0,7},{1,0},{2,1},{3,2},{4,3},{5,4},{6,5},{7,6},{8,15},{9,8},{10,9... | collective-permute-start | bytes 589832 | tf_op jit(solution)/shard_map/ppermute | solution.py:54
  61.1 14.0 %collective-permute-start.20 = (bf16[3,64,512]{2,1,0:T(8,128)(2,1)S(1)}, bf16[3,64,512]{2,1,0:T(8,128)(2,1)S(1)}, u32[]{:S(2)}, u32[]{:S(2)}) collective-permute-start(bf16[3,64,512]{2,1,0:T(8,128)(2,1)S(1)} %pad_maximum_fusion.1), channel_id=1, source_target_pairs={{0,1},{1,2},{2,3},{3,4},{4,5},{5,6},{6,7},{7,0},{8,9},{9,10},{10,1... | collective-permute-start | bytes 589832 | tf_op jit(solution)/shard_map/ppermute | solution.py:54
  62.1 13.1 %collective-permute-start.19 = (bf16[3,64,512]{2,1,0:T(8,128)(2,1)S(1)}, bf16[3,64,512]{2,1,0:T(8,128)(2,1)S(1)}, u32[]{:S(2)}, u32[]{:S(2)}) collective-permute-start(bf16[3,64,512]{2,1,0:T(8,128)(2,1)S(1)} %pad_maximum_fusion), channel_id=1, source_target_pairs={{0,2},{1,3},{2,4},{3,5},{4,6},{5,7},{6,0},{7,1},{8,10},{9,11},{10,... | collective-permute-start | bytes 589832 | tf_op jit(solution)/shard_map/ppermute | solution.py:54
  62.7 15.5 %collective-permute-start.17 = (bf16[3,64,384]{2,1,0:T(8,128)(2,1)S(1)}, bf16[3,64,384]{2,1,0:T(8,128)(2,1)S(1)}, u32[]{:S(2)}, u32[]{:S(2)}) collective-permute-start(bf16[3,64,384]{2,1,0:T(8,128)(2,1)S(1)} %fusion.25), channel_id=1, source_target_pairs={{0,1},{1,2},{2,3},{3,4},{4,5},{5,6},{6,7},{7,0},{8,9},{9,10},{10,1... | collective-permute-start | bytes 442376 | tf_op jit(solution)/shard_map/ppermute | solution.py:54
  67.3 11.0 %collective-permute-start.14 = (bf16[3,64,384]{2,1,0:T(8,128)(2,1)S(1)}, bf16[3,64,384]{2,1,0:T(8,128)(2,1)S(1)}, u32[]{:S(2)}, u32[]{:S(2)}) collective-permute-start(bf16[3,64,384]{2,1,0:T(8,128)(2,1)S(1)} %fusion.23), channel_id=1, source_target_pairs={{0,7},{1,0},{2,1},{3,2},{4,3},{5,4},{6,5},{7,6},{8,15},{9,8},{10,9... | collective-permute-start | bytes 442376 | tf_op jit(solution)/shard_map/ppermute | solution.py:54
  72.4 8.7 %collective-permute-start.24 = (bf16[3,64,512]{2,1,0:T(8,128)(2,1)S(1)}, bf16[3,64,512]{2,1,0:T(8,128)(2,1)S(1)}, u32[]{:S(2)}, u32[]{:S(2)}) collective-permute-start(bf16[3,64,512]{2,1,0:T(8,128)(2,1)S(1)} %fusion.21), channel_id=1, source_target_pairs={{0,7},{1,0},{2,1},{3,2},{4,3},{5,4},{6,5},{7,6},{8,15},{9,8},{10,9... | collective-permute-start | bytes 589832 | tf_op jit(solution)/shard_map/ppermute | solution.py:54
  75.3 7.5 %collective-permute-start.21 = (bf16[3,64,512]{2,1,0:T(8,128)(2,1)S(1)}, bf16[3,64,512]{2,1,0:T(8,128)(2,1)S(1)}, u32[]{:S(2)}, u32[]{:S(2)}) collective-permute-start(bf16[3,64,512]{2,1,0:T(8,128)(2,1)S(1)} %fusion.19), channel_id=1, source_target_pairs={{0,1},{1,2},{2,3},{3,4},{4,5},{5,6},{6,7},{7,0},{8,9},{9,10},{10,1... | collective-permute-start | bytes 589832 | tf_op jit(solution)/shard_map/ppermute | solution.py:54
  78.3 6.1 %collective-permute-start.18 = (bf16[3,64,384]{2,1,0:T(8,128)(2,1)S(1)}, bf16[3,64,384]{2,1,0:T(8,128)(2,1)S(1)}, u32[]{:S(2)}, u32[]{:S(2)}) collective-permute-start(bf16[3,64,384]{2,1,0:T(8,128)(2,1)S(1)} %fusion.26), channel_id=1, source_target_pairs={{0,1},{1,2},{2,3},{3,4},{4,5},{5,6},{6,7},{7,0},{8,9},{9,10},{10,1... | collective-permute-start | bytes 442376 | tf_op jit(solution)/shard_map/ppermute | solution.py:54
  78.4 5.9 %collective-permute-start.15 = (bf16[3,64,384]{2,1,0:T(8,128)(2,1)S(1)}, bf16[3,64,384]{2,1,0:T(8,128)(2,1)S(1)}, u32[]{:S(2)}, u32[]{:S(2)}) collective-permute-start(bf16[3,64,384]{2,1,0:T(8,128)(2,1)S(1)} %fusion.24), channel_id=1, source_target_pairs={{0,7},{1,0},{2,1},{3,2},{4,3},{5,4},{6,5},{7,6},{8,15},{9,8},{10,9... | collective-permute-start | bytes 442376 | tf_op jit(solution)/shard_map/ppermute | solution.py:54
  82.8 8.1 %collective-permute-start.22 = (bf16[3,64,512]{2,1,0:T(8,128)(2,1)S(1)}, bf16[3,64,512]{2,1,0:T(8,128)(2,1)S(1)}, u32[]{:S(2)}, u32[]{:S(2)}) collective-permute-start(bf16[3,64,512]{2,1,0:T(8,128)(2,1)S(1)} %fusion.20), channel_id=1, source_target_pairs={{0,1},{1,2},{2,3},{3,4},{4,5},{5,6},{6,7},{7,0},{8,9},{9,10},{10,1... | collective-permute-start | bytes 589832 | tf_op jit(solution)/shard_map/ppermute | solution.py:54
  148.9 6.7 %collective-permute-start.27 = (bf16[256,2048]{1,0:T(8,128)(2,1)}, bf16[256,2048]{1,0:T(8,128)(2,1)}, u32[]{:S(2)}, u32[]{:S(2)}) collective-permute-start(bf16[256,2048]{1,0:T(8,128)(2,1)} %fusion.12), channel_id=1, source_target_pairs={{0,8},{8,0},{16,24},{24,16},{32,40},{40,32},{48,56},{56,48},{64,72... | collective-permute-start | bytes 3145736 | tf_op jit(solution)/shard_map/ppermute | solution.py:273
  159.2 23.6 %all-to-all-start.2 = ((bf16[16,16,2048]{2,1,0:T(8,128)(2,1)}), bf16[16,16,2048]{2,1,0:T(8,128)(2,1)}, u32[]{:S(2)}, u32[]{:S(2)}) async-start(bf16[16,16,2048]{2,1,0:T(8,128)(2,1)} %bitcast.167), calls=%async_computation.2 | async-start | bytes 2097152 | tf_op jit(solution)/shard_map/all_to_all | solution.py:276
  (22 other events, 139.4 us)
Sparse Core Ops, SparseCore 0:
  96.3 45.6 all-gather.1

commit v5 on v3

--- a/solution.py
+++ b/solution.py
@@ -252,9 +252,24 @@
 
     other_factors = lax.ppermute(own_factors, "row", swap)
     own_factors = own_factors.astype(jnp.float32) + other_factors.astype(jnp.float32)
+    half_tokens = col_tokens // 2
+    own_factors = jnp.concatenate(
+        [
+            own_factors[:, : 2 * rank],
+            jnp.concatenate(
+                [own_factors[:half_tokens, 2 * rank :], own_factors[half_tokens:, 2 * rank :]],
+                axis=1,
+            ),
+        ],
+        axis=0,
+    )
     factor_parts = to_all(own_factors.astype(jnp.bfloat16), "row", chips, same_core)
     own_factors = jnp.sum(factor_parts.astype(jnp.float32), axis=0).astype(jnp.bfloat16)
-    factors = to_all(own_factors, "col", col_count).reshape(tokens_all, 3 * rank)
+    factors = to_all(own_factors, "col", col_count)
+    last = factors[:, col_tokens:]
+    last = jnp.concatenate([last[:, :, :rank], last[:, :, rank:]], axis=1)
+    factors = jnp.concatenate([factors[:, :col_tokens], last], axis=2)
+    factors = factors.reshape(tokens_all, 3 * rank)
     piece, factors = lax.optimization_barrier((piece, factors))
     piece_gate, piece_up, piece_hidden = [
         piece[:, i * packed_width : i * packed_width + hidden_units] for i in range(3)

time: 193 us -> 189 us (0.979)
  waiting for transfers between devices: 64 us -> 60.3 us
  transfers between devices with their start and end apart: 31 -> 31, of which waited for: 19 -> 19; matrix products, arithmetic and copies ran while one was open for 9% -> 10% of each run, Pallas kernels for 0% -> 0%
where the time goes in v5:
time: 189 us
  waiting for transfers between devices  60.3 us (32%)
  starting transfers between devices  52.1 us (28%)
  matrix products  26.7 us (14%)
  between operations  14.8 us (8%)
  blocking collectives  14.6 us (8%)
  local copies, waits for them, and re-layouts  14.3 us (8%)
  other arithmetic  5.84 us (3%)
    ppermute x14, waiting for transfers between devices, send(): lax.ppermute(value.astype(jnp.bfloat16), axis, shifted(size, step * ways[...  18.1 us
    ppermute x14, starting transfers between devices, send(): lax.ppermute(value.astype(jnp.bfloat16), axis, shifted(size, step * ways[...  17.8 us
    dot_general x13, matrix products, multiply_right_transposed(): lax.dot_general(left, right, (((1,), (1,)), ((), ())), preferred_element_...  17.5 us
    all_to_all x1, blocking collectives, to_all(): lax.all_to_all(copies, axis, 0, 0, axis_index_groups=groups, tiled=True)  14.6 us
    all_to_all x1, waiting for transfers between devices, body(): lax.all_to_all(share, 'row', 0, 0, axis_index_groups=same_core, tiled=True)  12.9 us
    all_to_all x1, waiting for transfers between devices, to_all(): lax.all_to_all(copies, axis, 0, 0, axis_index_groups=groups, tiled=True)  10.8 us
    ppermute x5, starting transfers between devices, to_other_core(): return lax.ppermute(value, 'row', swap)  8.88 us
    ppermute x1, waiting for transfers between devices, gather_tokens(): lax.ppermute(slab[half:], 'row', moves(0, -2))  8.45 us
  transfers between devices with their start and end apart: 31, of which 19 were waited for; matrix products, arithmetic and copies ran while one was open for 10% of the time, Pallas kernels for 0%

profile of v5, /device:TPU:1, one launch (start us, length us, event | category | flops | bytes accessed | tf_op | source)
XLA Modules:
  0.0 188.6 jit_solution(13256183689227010651)
XLA Ops:
  8.1 3.3 %collective-permute-start = (bf16[16,2048]{1,0:T(8,128)(2,1)S(1)}, bf16[16,2048]{1,0:T(8,128)(2,1)S(1)}, u32[]{:S(2)}, u32[]{:S(2)}) collective-permute-start(bf16[16,2048]{1,0:T(8,128)(2,1)S(1)} %broadcast_select_fusion.2), channel_id=1, source_target_pairs={{0,8},{8,0},{16,24},{24,16},{32,40},{40,32},{48,56},{56,48},{64,72... | collective-permute-start | bytes 196616 | tf_op jit(solution)/shard_map/ppermute | solution.py:97
  13.3 2.7 %collective-permute-start.2 = (bf16[32,2048]{1,0:T(8,128)(2,1)S(1)}, bf16[32,2048]{1,0:T(8,128)(2,1)S(1)}, u32[]{:S(2)}, u32[]{:S(2)}) collective-permute-start(bf16[32,2048]{1,0:T(8,128)(2,1)S(1)} %pad_maximum_fusion.6), channel_id=1, source_target_pairs={{0,192},{8,56},{16,208},{24,8},{32,224},{40,24},{48,240},{56,40},{... | collective-permute-start | bytes 393224 | tf_op jit(solution)/shard_map/ppermute | solution.py:107
  16.0 2.6 %collective-permute-done.1 = bf16[32,2048]{1,0:T(8,128)(2,1)S(1)} collective-permute-done((bf16[32,2048]{1,0:T(8,128)(2,1)S(1)}, bf16[32,2048]{1,0:T(8,128)(2,1)S(1)}, u32[]{:S(2)}, u32[]{:S(2)}) %collective-permute-start.1) | collective-permute-done | bytes 131104 | tf_op jit(solution)/shard_map/ppermute | solution.py:107
  22.6 2.4 %collective-permute-start.4 = (bf16[128,2048]{1,0:T(8,128)(2,1)S(1)}, bf16[128,2048]{1,0:T(8,128)(2,1)S(1)}, u32[]{:S(2)}, u32[]{:S(2)}) collective-permute-start(bf16[128,2048]{1,0:T(8,128)(2,1)S(1)} %bitcast.163), channel_id=1, source_target_pairs={{0,8},{8,0},{16,24},{24,16},{32,40},{40,32},{48,56},{56,48},{64,72... | collective-permute-start | bytes 1572872 | tf_op jit(solution)/shard_map/ppermute | solution.py:97
  24.9 2.7 %collective-permute-start.7 = (bf16[128,2048]{1,0:T(8,128)(2,1)S(1)}, bf16[128,2048]{1,0:T(8,128)(2,1)S(1)}, u32[]{:S(2)}, u32[]{:S(2)}) collective-permute-start(bf16[128,2048]{1,0:T(8,128)(2,1)S(1)} %bitcast.165), channel_id=1, source_target_pairs={{0,48},{8,200},{16,0},{24,216},{32,16},{40,232},{48,32},{56,248},{... | collective-permute-start | bytes 1572872 | tf_op jit(solution)/shard_map/ppermute | solution.py:115
  28.8 8.5 %collective-permute-done.10 = bf16[64,2048]{1,0:T(8,128)(2,1)S(1)} collective-permute-done((bf16[64,2048]{1,0:T(8,128)(2,1)S(1)}, bf16[64,2048]{1,0:T(8,128)(2,1)S(1)}, u32[]{:S(2)}, u32[]{:S(2)}) %collective-permute-start.10) | collective-permute-done | bytes 262176 | tf_op jit(solution)/shard_map/ppermute | solution.py:119
  37.2 2.7 %collective-permute-start.11 = (bf16[128,2048]{1,0:T(8,128)(2,1)S(1)}, bf16[128,2048]{1,0:T(8,128)(2,1)S(1)}, u32[]{:S(2)}, u32[]{:S(2)}) collective-permute-start(bf16[128,2048]{1,0:T(8,128)(2,1)S(1)} %constant_dynamic-update-slice_fusion.1), channel_id=1, source_target_pairs={{0,8},{8,0},{16,24},{24,16},{32,40},{40,32},{48,56},{56,48},{64,72... | collective-permute-start | bytes 1572872 | tf_op jit(solution)/shard_map/ppermute | solution.py:97
  46.3 2.4 %fusion = f32[512,896]{1,0:T(8,128)S(1)} fusion(bf16[512,2048]{1,0:T(8,128)(2,1)S(1)} %bitcast.172, bf16[2048,64]{0,1:T(8,128)(2,1)S(1)} %copy-done.10, bf16[2048,832]{0,1:T(8,128)(2,1)S(1)} %copy-done), kind=kOutput, calls=%fused_computation | convolution fusion | flops 1886388224 | bytes 7602176 | tf_op jit(solution)/shard_map/dot_general | solution.py:16
  48.7 2.4 %fusion.4 = f32[512,896]{1,0:T(8,128)S(1)} fusion(bf16[512,2048]{1,0:T(8,128)(2,1)S(1)} %bitcast.173, bf16[2048,64]{0,1:T(8,128)(2,1)S(1)} %copy-done.8, bf16[2048,832]{0,1:T(8,128)(2,1)S(1)} %copy-done.1), kind=kOutput, calls=%fused_computation.4 | convolution fusion | flops 1886388224 | bytes 7602176 | tf_op jit(solution)/shard_map/dot_general | solution.py:16
  51.1 2.4 %fusion.8 = f32[512,896]{1,0:T(8,128)S(1)} fusion(bf16[512,2048]{1,0:T(8,128)(2,1)S(1)} %bitcast.170, bf16[64,2048]{1,0:T(8,128)(2,1)S(1)} %copy-done.15, bf16[832,2048]{1,0:T(8,128)(2,1)S(1)} %copy-done.14), kind=kOutput, calls=%fused_computation.8 | convolution fusion | flops 1886388224 | bytes 7602176 | tf_op jit(solution)/shard_map/dot_general | solution.py:16
  54.3 4.0 %collective-permute-start.13 = (bf16[3,64,384]{2,1,0:T(8,128)(2,1)S(1)}, bf16[3,64,384]{2,1,0:T(8,128)(2,1)S(1)}, u32[]{:S(2)}, u32[]{:S(2)}) collective-permute-start(bf16[3,64,384]{2,1,0:T(8,128)(2,1)S(1)} %pad_maximum_fusion.4), channel_id=1, source_target_pairs={{0,7},{1,0},{2,1},{3,2},{4,3},{5,4},{6,5},{7,6},{8,15},{9,8},{10,9... | collective-permute-start | bytes 442376 | tf_op jit(solution)/shard_map/ppermute | solution.py:54
  63.8 3.5 %collective-permute-done.12 = bf16[3,64,384]{2,1,0:T(8,128)(2,1)S(1)} collective-permute-done((bf16[3,64,384]{2,1,0:T(8,128)(2,1)S(1)}, bf16[3,64,384]{2,1,0:T(8,128)(2,1)S(1)}, u32[]{:S(2)}, u32[]{:S(2)}) %collective-permute-start.12) | collective-permute-done | bytes 147488 | tf_op jit(solution)/shard_map/ppermute | solution.py:54
  67.3 2.7 %collective-permute-start.14 = (bf16[3,64,384]{2,1,0:T(8,128)(2,1)S(1)}, bf16[3,64,384]{2,1,0:T(8,128)(2,1)S(1)}, u32[]{:S(2)}, u32[]{:S(2)}) collective-permute-start(bf16[3,64,384]{2,1,0:T(8,128)(2,1)S(1)} %fusion.21), channel_id=1, source_target_pairs={{0,7},{1,0},{2,1},{3,2},{4,3},{5,4},{6,5},{7,6},{8,15},{9,8},{10,9... | collective-permute-start | bytes 442376 | tf_op jit(solution)/shard_map/ppermute | solution.py:54
  72.4 2.7 %collective-permute-start.24 = (bf16[3,64,512]{2,1,0:T(8,128)(2,1)S(1)}, bf16[3,64,512]{2,1,0:T(8,128)(2,1)S(1)}, u32[]{:S(2)}, u32[]{:S(2)}) collective-permute-start(bf16[3,64,512]{2,1,0:T(8,128)(2,1)S(1)} %fusion.19), channel_id=1, source_target_pairs={{0,7},{1,0},{2,1},{3,2},{4,3},{5,4},{6,5},{7,6},{8,15},{9,8},{10,9... | collective-permute-start | bytes 589832 | tf_op jit(solution)/shard_map/ppermute | solution.py:54
  75.4 2.9 %collective-permute-done.17 = bf16[3,64,384]{2,1,0:T(8,128)(2,1)S(1)} collective-permute-done((bf16[3,64,384]{2,1,0:T(8,128)(2,1)S(1)}, bf16[3,64,384]{2,1,0:T(8,128)(2,1)S(1)}, u32[]{:S(2)}, u32[]{:S(2)}) %collective-permute-start.17) | collective-permute-done | bytes 147488 | tf_op jit(solution)/shard_map/ppermute | solution.py:54
  78.4 2.7 %collective-permute-start.15 = (bf16[3,64,384]{2,1,0:T(8,128)(2,1)S(1)}, bf16[3,64,384]{2,1,0:T(8,128)(2,1)S(1)}, u32[]{:S(2)}, u32[]{:S(2)}) collective-permute-start(bf16[3,64,384]{2,1,0:T(8,128)(2,1)S(1)} %fusion.22), channel_id=1, source_target_pairs={{0,7},{1,0},{2,1},{3,2},{4,3},{5,4},{6,5},{7,6},{8,15},{9,8},{10,9... | collective-permute-start | bytes 442376 | tf_op jit(solution)/shard_map/ppermute | solution.py:54
  86.1 4.8 %collective-permute-done.22 = bf16[3,64,512]{2,1,0:T(8,128)(2,1)S(1)} collective-permute-done((bf16[3,64,512]{2,1,0:T(8,128)(2,1)S(1)}, bf16[3,64,512]{2,1,0:T(8,128)(2,1)S(1)}, u32[]{:S(2)}, u32[]{:S(2)}) %collective-permute-start.22) | collective-permute-done | bytes 196640 | tf_op jit(solution)/shard_map/ppermute | solution.py:54
  99.6 4.3 %collective-permute-start.26 = (bf16[64,192]{1,0:T(8,128)(2,1)S(1)}, bf16[64,192]{1,0:T(8,128)(2,1)S(1)}, u32[]{:S(2)}, u32[]{:S(2)}) collective-permute-start(bf16[64,192]{1,0:T(8,128)(2,1)S(1)} %pad_maximum_fusion.7), channel_id=1, source_target_pairs={{0,8},{8,0},{16,24},{24,16},{32,40},{40,32},{48,56},{56,48},{64,72... | collective-permute-start | bytes 73736 | tf_op jit(solution)/shard_map/ppermute | solution.py:253
  105.0 14.6 %all_to_all.19 = bf16[16,96,128]{2,1,0:T(8,128)(2,1)} all-to-all(bf16[16,96,128]{2,1,0:T(8,128)(2,1)S(1)} %broadcast_in_dim.65), channel_id=1, replica_groups={{0,16,32,48,64,80,96,112,128,144,160,176,192,208,224,240},{8,24,40,56,7..., dimensions={0} | all-to-all | bytes 786432 | tf_op jit(solution)/shard_map/all_to_all | solution.py:251
  121.4 4.0 %all-to-all-start.1 = ((bf16[8,96,128]{2,1,0:T(8,128)(2,1)}), bf16[8,96,128]{2,1,0:T(8,128)(2,1)}, u32[]{:S(2)}, u32[]{:S(2)}) async-start(bf16[8,96,128]{2,1,0:T(8,128)(2,1)} %broadcast_in_dim.66), calls=%async_computation.1 | async-start | bytes 393216 | tf_op jit(solution)/shard_map/all_to_all | solution.py:251
  126.5 10.8 %all-to-all-done.1 = bf16[8,96,128]{2,1,0:T(8,128)(2,1)} async-done(((bf16[8,96,128]{2,1,0:T(8,128)(2,1)}), bf16[8,96,128]{2,1,0:T(8,128)(2,1)}, u32[]{:S(2)}, u32[]{:S(2)}) %all-to-all-start.1) | async-done | bytes 196640 | tf_op jit(solution)/shard_map/all_to_all | solution.py:251
  145.2 3.5 %collective-permute-start.27 = (bf16[256,2048]{1,0:T(8,128)(2,1)S(1)}, bf16[256,2048]{1,0:T(8,128)(2,1)S(1)}, u32[]{:S(2)}, u32[]{:S(2)}) collective-permute-start(bf16[256,2048]{1,0:T(8,128)(2,1)S(1)} %fusion.12), channel_id=1, source_target_pairs={{0,8},{8,0},{16,24},{24,16},{32,40},{40,32},{48,56},{56,48},{64,72... | collective-permute-start | bytes 3145736 | tf_op jit(solution)/shard_map/ppermute | solution.py:291
  155.3 6.7 %all-to-all-start.2 = ((bf16[16,16,2048]{2,1,0:T(8,128)(2,1)}), bf16[16,16,2048]{2,1,0:T(8,128)(2,1)}, u32[]{:S(2)}, u32[]{:S(2)}) async-start(bf16[16,16,2048]{2,1,0:T(8,128)(2,1)} %bitcast.167), calls=%async_computation.2 | async-start | bytes 2097152 | tf_op jit(solution)/shard_map/all_to_all | solution.py:293
  166.0 12.9 %all-to-all-done.2 = bf16[16,16,2048]{2,1,0:T(8,128)(2,1)} async-done(((bf16[16,16,2048]{2,1,0:T(8,128)(2,1)}), bf16[16,16,2048]{2,1,0:T(8,128)(2,1)}, u32[]{:S(2)}, u32[]{:S(2)}) %all-to-all-start.2) | async-done | bytes 1048608 | tf_op jit(solution)/shard_map/all_to_all | solution.py:293
  (165 shorter events, 61.7 us)
Async XLA Ops:
  7.2 133.1 %all-gather.2.cloned.1.call-start = ((), (), s32[]{:S(2)}) async-start(), calls=%async_computation.3 | async-start | bytes 3096576 | tf_op jit(solution)/shard_map/all_gather | solution.py:234
  13.3 6.0 %collective-permute-start.2 = (bf16[32,2048]{1,0:T(8,128)(2,1)S(1)}, bf16[32,2048]{1,0:T(8,128)(2,1)S(1)}, u32[]{:S(2)}, u32[]{:S(2)}) collective-permute-start(bf16[32,2048]{1,0:T(8,128)(2,1)S(1)} %pad_maximum_fusion.6), channel_id=1, source_target_pairs={{0,192},{8,56},{16,208},{24,8},{32,224},{40,24},{48,240},{56,40},{... | collective-permute-start | bytes 393224 | tf_op jit(solution)/shard_map/ppermute | solution.py:107
  21.6 7.1 %collective-permute-start.9 = (bf16[64,2048]{1,0:T(8,128)(2,1)S(1)}, bf16[64,2048]{1,0:T(8,128)(2,1)S(1)}, u32[]{:S(2)}, u32[]{:S(2)}) collective-permute-start(bf16[64,2048]{1,0:T(8,128)(2,1)S(1)} %bitcast.214), channel_id=1, source_target_pairs={{0,32},{8,136},{16,48},{24,152},{32,0},{40,168},{48,16},{56,184},{... | collective-permute-start | bytes 786440 | tf_op jit(solution)/shard_map/ppermute | solution.py:118
  22.6 17.9 %collective-permute-start.4 = (bf16[128,2048]{1,0:T(8,128)(2,1)S(1)}, bf16[128,2048]{1,0:T(8,128)(2,1)S(1)}, u32[]{:S(2)}, u32[]{:S(2)}) collective-permute-start(bf16[128,2048]{1,0:T(8,128)(2,1)S(1)} %bitcast.163), channel_id=1, source_target_pairs={{0,8},{8,0},{16,24},{24,16},{32,40},{40,32},{48,56},{56,48},{64,72... | collective-permute-start | bytes 1572872 | tf_op jit(solution)/shard_map/ppermute | solution.py:97
  24.9 15.0 %collective-permute-start.5 = (bf16[128,2048]{1,0:T(8,128)(2,1)S(1)}, bf16[128,2048]{1,0:T(8,128)(2,1)S(1)}, u32[]{:S(2)}, u32[]{:S(2)}) collective-permute-start(bf16[128,2048]{1,0:T(8,128)(2,1)S(1)} %bitcast.164), channel_id=1, source_target_pairs={{0,16},{8,72},{16,32},{24,88},{32,48},{40,104},{48,0},{56,120},{64... | collective-permute-start | bytes 1572872 | tf_op jit(solution)/shard_map/ppermute | solution.py:114
  24.9 15.1 %collective-permute-start.7 = (bf16[128,2048]{1,0:T(8,128)(2,1)S(1)}, bf16[128,2048]{1,0:T(8,128)(2,1)S(1)}, u32[]{:S(2)}, u32[]{:S(2)}) collective-permute-start(bf16[128,2048]{1,0:T(8,128)(2,1)S(1)} %bitcast.165), channel_id=1, source_target_pairs={{0,48},{8,200},{16,0},{24,216},{32,16},{40,232},{48,32},{56,248},{... | collective-permute-start | bytes 1572872 | tf_op jit(solution)/shard_map/ppermute | solution.py:115
  27.6 9.6 %collective-permute-start.10 = (bf16[64,2048]{1,0:T(8,128)(2,1)S(1)}, bf16[64,2048]{1,0:T(8,128)(2,1)S(1)}, u32[]{:S(2)}, u32[]{:S(2)}) collective-permute-start(bf16[64,2048]{1,0:T(8,128)(2,1)S(1)} %bitcast.213), channel_id=1, source_target_pairs={{0,32},{8,136},{16,48},{24,152},{32,0},{40,168},{48,16},{56,184},{... | collective-permute-start | bytes 786440 | tf_op jit(solution)/shard_map/ppermute | solution.py:119
  37.2 5.9 %collective-permute-start.11 = (bf16[128,2048]{1,0:T(8,128)(2,1)S(1)}, bf16[128,2048]{1,0:T(8,128)(2,1)S(1)}, u32[]{:S(2)}, u32[]{:S(2)}) collective-permute-start(bf16[128,2048]{1,0:T(8,128)(2,1)S(1)} %constant_dynamic-update-slice_fusion.1), channel_id=1, source_target_pairs={{0,8},{8,0},{16,24},{24,16},{32,40},{40,32},{48,56},{56,48},{64,72... | collective-permute-start | bytes 1572872 | tf_op jit(solution)/shard_map/ppermute | solution.py:97
  54.1 7.9 %collective-permute-start.16 = (bf16[3,64,384]{2,1,0:T(8,128)(2,1)S(1)}, bf16[3,64,384]{2,1,0:T(8,128)(2,1)S(1)}, u32[]{:S(2)}, u32[]{:S(2)}) collective-permute-start(bf16[3,64,384]{2,1,0:T(8,128)(2,1)S(1)} %pad_maximum_fusion.5), channel_id=1, source_target_pairs={{0,1},{1,2},{2,3},{3,4},{4,5},{5,6},{6,7},{7,0},{8,9},{9,10},{10,1... | collective-permute-start | bytes 442376 | tf_op jit(solution)/shard_map/ppermute | solution.py:54
  54.3 8.4 %collective-permute-start.13 = (bf16[3,64,384]{2,1,0:T(8,128)(2,1)S(1)}, bf16[3,64,384]{2,1,0:T(8,128)(2,1)S(1)}, u32[]{:S(2)}, u32[]{:S(2)}) collective-permute-start(bf16[3,64,384]{2,1,0:T(8,128)(2,1)S(1)} %pad_maximum_fusion.4), channel_id=1, source_target_pairs={{0,7},{1,0},{2,1},{3,2},{4,3},{5,4},{6,5},{7,6},{8,15},{9,8},{10,9... | collective-permute-start | bytes 442376 | tf_op jit(solution)/shard_map/ppermute | solution.py:54
  58.3 9.0 %collective-permute-start.12 = (bf16[3,64,384]{2,1,0:T(8,128)(2,1)S(1)}, bf16[3,64,384]{2,1,0:T(8,128)(2,1)S(1)}, u32[]{:S(2)}, u32[]{:S(2)}) collective-permute-start(bf16[3,64,384]{2,1,0:T(8,128)(2,1)S(1)} %pad_maximum_fusion.3), channel_id=1, source_target_pairs={{0,6},{1,7},{2,0},{3,1},{4,2},{5,3},{6,4},{7,5},{8,14},{9,15},{10,... | collective-permute-start | bytes 442376 | tf_op jit(solution)/shard_map/ppermute | solution.py:54
  60.3 12.1 %collective-permute-start.23 = (bf16[3,64,512]{2,1,0:T(8,128)(2,1)S(1)}, bf16[3,64,512]{2,1,0:T(8,128)(2,1)S(1)}, u32[]{:S(2)}, u32[]{:S(2)}) collective-permute-start(bf16[3,64,512]{2,1,0:T(8,128)(2,1)S(1)} %pad_maximum_fusion.2), channel_id=1, source_target_pairs={{0,7},{1,0},{2,1},{3,2},{4,3},{5,4},{6,5},{7,6},{8,15},{9,8},{10,9... | collective-permute-start | bytes 589832 | tf_op jit(solution)/shard_map/ppermute | solution.py:54
  61.1 14.0 %collective-permute-start.20 = (bf16[3,64,512]{2,1,0:T(8,128)(2,1)S(1)}, bf16[3,64,512]{2,1,0:T(8,128)(2,1)S(1)}, u32[]{:S(2)}, u32[]{:S(2)}) collective-permute-start(bf16[3,64,512]{2,1,0:T(8,128)(2,1)S(1)} %pad_maximum_fusion.1), channel_id=1, source_target_pairs={{0,1},{1,2},{2,3},{3,4},{4,5},{5,6},{6,7},{7,0},{8,9},{9,10},{10,1... | collective-permute-start | bytes 589832 | tf_op jit(solution)/shard_map/ppermute | solution.py:54
  62.1 13.1 %collective-permute-start.19 = (bf16[3,64,512]{2,1,0:T(8,128)(2,1)S(1)}, bf16[3,64,512]{2,1,0:T(8,128)(2,1)S(1)}, u32[]{:S(2)}, u32[]{:S(2)}) collective-permute-start(bf16[3,64,512]{2,1,0:T(8,128)(2,1)S(1)} %pad_maximum_fusion), channel_id=1, source_target_pairs={{0,2},{1,3},{2,4},{3,5},{4,6},{5,7},{6,0},{7,1},{8,10},{9,11},{10,... | collective-permute-start | bytes 589832 | tf_op jit(solution)/shard_map/ppermute | solution.py:54
  62.7 15.5 %collective-permute-start.17 = (bf16[3,64,384]{2,1,0:T(8,128)(2,1)S(1)}, bf16[3,64,384]{2,1,0:T(8,128)(2,1)S(1)}, u32[]{:S(2)}, u32[]{:S(2)}) collective-permute-start(bf16[3,64,384]{2,1,0:T(8,128)(2,1)S(1)} %fusion.23), channel_id=1, source_target_pairs={{0,1},{1,2},{2,3},{3,4},{4,5},{5,6},{6,7},{7,0},{8,9},{9,10},{10,1... | collective-permute-start | bytes 442376 | tf_op jit(solution)/shard_map/ppermute | solution.py:54
  67.3 11.0 %collective-permute-start.14 = (bf16[3,64,384]{2,1,0:T(8,128)(2,1)S(1)}, bf16[3,64,384]{2,1,0:T(8,128)(2,1)S(1)}, u32[]{:S(2)}, u32[]{:S(2)}) collective-permute-start(bf16[3,64,384]{2,1,0:T(8,128)(2,1)S(1)} %fusion.21), channel_id=1, source_target_pairs={{0,7},{1,0},{2,1},{3,2},{4,3},{5,4},{6,5},{7,6},{8,15},{9,8},{10,9... | collective-permute-start | bytes 442376 | tf_op jit(solution)/shard_map/ppermute | solution.py:54
  72.4 8.7 %collective-permute-start.24 = (bf16[3,64,512]{2,1,0:T(8,128)(2,1)S(1)}, bf16[3,64,512]{2,1,0:T(8,128)(2,1)S(1)}, u32[]{:S(2)}, u32[]{:S(2)}) collective-permute-start(bf16[3,64,512]{2,1,0:T(8,128)(2,1)S(1)} %fusion.19), channel_id=1, source_target_pairs={{0,7},{1,0},{2,1},{3,2},{4,3},{5,4},{6,5},{7,6},{8,15},{9,8},{10,9... | collective-permute-start | bytes 589832 | tf_op jit(solution)/shard_map/ppermute | solution.py:54
  75.3 7.5 %collective-permute-start.21 = (bf16[3,64,512]{2,1,0:T(8,128)(2,1)S(1)}, bf16[3,64,512]{2,1,0:T(8,128)(2,1)S(1)}, u32[]{:S(2)}, u32[]{:S(2)}) collective-permute-start(bf16[3,64,512]{2,1,0:T(8,128)(2,1)S(1)} %fusion.17), channel_id=1, source_target_pairs={{0,1},{1,2},{2,3},{3,4},{4,5},{5,6},{6,7},{7,0},{8,9},{9,10},{10,1... | collective-permute-start | bytes 589832 | tf_op jit(solution)/shard_map/ppermute | solution.py:54
  78.3 6.1 %collective-permute-start.18 = (bf16[3,64,384]{2,1,0:T(8,128)(2,1)S(1)}, bf16[3,64,384]{2,1,0:T(8,128)(2,1)S(1)}, u32[]{:S(2)}, u32[]{:S(2)}) collective-permute-start(bf16[3,64,384]{2,1,0:T(8,128)(2,1)S(1)} %fusion.24), channel_id=1, source_target_pairs={{0,1},{1,2},{2,3},{3,4},{4,5},{5,6},{6,7},{7,0},{8,9},{9,10},{10,1... | collective-permute-start | bytes 442376 | tf_op jit(solution)/shard_map/ppermute | solution.py:54
  78.4 5.9 %collective-permute-start.15 = (bf16[3,64,384]{2,1,0:T(8,128)(2,1)S(1)}, bf16[3,64,384]{2,1,0:T(8,128)(2,1)S(1)}, u32[]{:S(2)}, u32[]{:S(2)}) collective-permute-start(bf16[3,64,384]{2,1,0:T(8,128)(2,1)S(1)} %fusion.22), channel_id=1, source_target_pairs={{0,7},{1,0},{2,1},{3,2},{4,3},{5,4},{6,5},{7,6},{8,15},{9,8},{10,9... | collective-permute-start | bytes 442376 | tf_op jit(solution)/shard_map/ppermute | solution.py:54
  82.8 8.1 %collective-permute-start.22 = (bf16[3,64,512]{2,1,0:T(8,128)(2,1)S(1)}, bf16[3,64,512]{2,1,0:T(8,128)(2,1)S(1)}, u32[]{:S(2)}, u32[]{:S(2)}) collective-permute-start(bf16[3,64,512]{2,1,0:T(8,128)(2,1)S(1)} %fusion.18), channel_id=1, source_target_pairs={{0,1},{1,2},{2,3},{3,4},{4,5},{5,6},{6,7},{7,0},{8,9},{9,10},{10,1... | collective-permute-start | bytes 589832 | tf_op jit(solution)/shard_map/ppermute | solution.py:54
  121.4 15.9 %all-to-all-start.1 = ((bf16[8,96,128]{2,1,0:T(8,128)(2,1)}), bf16[8,96,128]{2,1,0:T(8,128)(2,1)}, u32[]{:S(2)}, u32[]{:S(2)}) async-start(bf16[8,96,128]{2,1,0:T(8,128)(2,1)} %broadcast_in_dim.66), calls=%async_computation.1 | async-start | bytes 393216 | tf_op jit(solution)/shard_map/all_to_all | solution.py:251
  145.2 7.7 %collective-permute-start.27 = (bf16[256,2048]{1,0:T(8,128)(2,1)S(1)}, bf16[256,2048]{1,0:T(8,128)(2,1)S(1)}, u32[]{:S(2)}, u32[]{:S(2)}) collective-permute-start(bf16[256,2048]{1,0:T(8,128)(2,1)S(1)} %fusion.12), channel_id=1, source_target_pairs={{0,8},{8,0},{16,24},{24,16},{32,40},{40,32},{48,56},{56,48},{64,72... | collective-permute-start | bytes 3145736 | tf_op jit(solution)/shard_map/ppermute | solution.py:291
  155.3 23.6 %all-to-all-start.2 = ((bf16[16,16,2048]{2,1,0:T(8,128)(2,1)}), bf16[16,16,2048]{2,1,0:T(8,128)(2,1)}, u32[]{:S(2)}, u32[]{:S(2)}) async-start(bf16[16,16,2048]{2,1,0:T(8,128)(2,1)} %bitcast.167), calls=%async_computation.2 | async-start | bytes 2097152 | tf_op jit(solution)/shard_map/all_to_all | solution.py:293
  (24 other events, 173.6 us)
Sparse Core Ops, SparseCore 0:
  96.3 43.8 all-gather.1
